TPU v7x, 128 devices: a whole 4x4x4 slice. The times are simulated.
128 devices in a mesh: row: 8 (over z, core), col: 16 (over y, x).
Axes of the slice: x: 4, y: 4, z: 4, core: 2. Of those that a mesh axis runs over, the one named last changes fastest.
Arguments:
- noise: bfloat16 [8192, 4096], P('row', 'col'), may hold values from -6 to 6
- data: bfloat16 [8192, 4096], P('col', 'row'), may hold values from -6 to 6
Outputs:
- targets: bfloat16 [8192, 4096], P('row', 'col')
- noise_potential: float32 [8192], P('row')
- data_potential: float32 [8192], P('col')
All inputs are finite; a program needn't handle non-finite values.
Results may differ from a plain program's by a relative error of at most 0.0043.
Values may be sent and summed in bfloat16 or wider, within the bound.
No kernel may reach another device: no remote copies, remote signals or barrier semaphores. Data moves between devices by JAX's collectives and lax.ppermute only.
A program may use at most 128 MiB of HBM per device.

v0:
```python
import jax
import jax.numpy as jnp
from jax import lax
from jax.sharding import PartitionSpec as P

D = 4096
ITERS = 4


EPS = 0.02


def row_logsum(scores):
    peak = lax.pmax(jnp.max(scores, axis=1), "col")
    total = lax.psum(jnp.sum(jnp.exp(scores - peak[:, None]), axis=1), "col")
    return peak + jnp.log(total)


def col_logsum(scores):
    peak = lax.pmax(jnp.max(scores, axis=0), "row")
    total = lax.psum(jnp.sum(jnp.exp(scores - peak[None, :]), axis=0), "row")
    return peak + jnp.log(total)


def local(noise, data):
    data_whole = lax.all_gather(data, "row", axis=1, tiled=True)
    data_sq = jnp.sum(data_whole.astype(jnp.float32) ** 2, axis=1)
    rows_here = noise.shape[0]
    noise_whole = lax.all_gather(noise, "col", axis=1, tiled=True)
    gram = lax.dot_general(
        noise_whole, data_whole, (((1,), (1,)), ((), ())), preferred_element_type=jnp.float32
    )
    noise_sq = jnp.sum(noise_whole.astype(jnp.float32) ** 2, axis=1)
    cost = (noise_sq[:, None] + data_sq[None, :] - 2.0 * gram) / D
    noise_count = float(rows_here * lax.axis_size("row"))
    data_count = float(data_whole.shape[0] * lax.axis_size("col"))
    noise_potential = jnp.zeros((rows_here,), jnp.float32)
    data_potential = jnp.zeros((data_whole.shape[0],), jnp.float32)
    for step in range(ITERS):
        noise_potential = -EPS * jnp.log(noise_count) - EPS * row_logsum(
            (data_potential[None, :] - cost) / EPS
        )
        data_potential = -EPS * jnp.log(data_count) - EPS * col_logsum(
            (noise_potential[:, None] - cost) / EPS
        )
    scores = (data_potential[None, :] - cost) / EPS
    row_lse = row_logsum(scores)
    weights = jnp.exp(scores - row_lse[:, None]).astype(jnp.bfloat16)
    partial_targets = jnp.dot(weights, data_whole, preferred_element_type=jnp.float32)
    targets = lax.psum_scatter(partial_targets, "col", scatter_dimension=1, tiled=True).astype(
        jnp.bfloat16
    )
    return (targets, noise_potential, data_potential)


def solution(mesh):
    placed = (P("row", "col"), P("col", "row"))
    return jax.shard_map(
        local,
        mesh=mesh,
        in_specs=placed,
        out_specs=(P("row", "col"), P("row"), P("col")),
        check_vma=False,
    )
```

profile of v0, /device:TPU:0, one launch (start us, length us, event | category | flops | bytes accessed | tf_op | source)
XLA Modules:
  0.0 734.6 jit_solution(5781939437795706487)
XLA Ops:
  7.2 0.7 all-gather.5.cloned.1.call-update
  7.9 0.7 all-gather.3.cloned.1.call-update
  8.7 35.8 %all-gather.5.cloned.1.call-done = bf16[512,4096]{1,0:T(8,128)(2,1)} async-done(((bf16[512,512]{1,0:T(8,128)(2,1)}), bf16[512,4096]{1,0:T(8,128)(2,1)}) %all-gather.5.cloned.1.call-update) | async-done | bytes 4194320 | tf_op jit(solution)/shard_map/all_gather | solution.py:26
  44.5 3.1 multiply_reduce_fusion.1
  47.6 77.1 %all-gather.3.cloned.1.call-done = bf16[1024,4096]{1,0:T(8,128)(2,1)} async-done(((bf16[1024,256]{1,0:T(8,128)(2,1)}), bf16[1024,4096]{1,0:T(8,128)(2,1)}) %all-gather.3.cloned.1.call-update) | async-done | bytes 8388624 | tf_op jit(solution)/shard_map/all_gather | solution.py:29
  124.7 5.2 multiply_reduce_fusion
  130.5 7.2 fusion
  137.6 38.1 %pmax.63 = f32[1024]{0:T(1024)S(1)} all-reduce(f32[1024]{0:T(1024)S(1)} %get-tuple-element.3), channel_id=1, replica_groups=mesh['row'=8,'col'=16] {'col'}, use_global_device_ids=true, to_apply=%region_3.0 | all-reduce | flops 1024 | bytes 8192 | tf_op jit(solution)/shard_map/pmax | solution.py:14
  176.2 35.5 %psum.63 = f32[1024]{0:T(1024)S(1)} all-reduce(f32[1024]{0:T(1024)S(1)} %exponential_reduce_fusion.8), channel_id=1, replica_groups=mesh['row'=8,'col'=16] {'col'}, use_global_device_ids=true, to_apply=%region_5.0 | all-reduce | flops 1024 | bytes 8192 | tf_op jit(solution)/shard_map/psum | solution.py:15
  212.0 12.4 %pmax.64 = f32[512]{0:T(512)S(1)} all-reduce(f32[512]{0:T(512)S(1)} %fusion.1), channel_id=1, replica_groups=mesh['row'=8,'col'=16] {'row'}, use_global_device_ids=true, to_apply=%region_7.0 | all-reduce | flops 512 | bytes 4096 | tf_op jit(solution)/shard_map/pmax | solution.py:20
  224.4 0.6 exponential_reduce_fusion.7
  224.9 12.4 %psum.64 = f32[512]{0:T(512)S(1)} all-reduce(f32[512]{0:T(512)S(1)} %exponential_reduce_fusion.7), channel_id=1, replica_groups=mesh['row'=8,'col'=16] {'row'}, use_global_device_ids=true, to_apply=%region_9.0 | all-reduce | flops 512 | bytes 4096 | tf_op jit(solution)/shard_map/psum | solution.py:21
  237.7 37.5 %pmax.65 = f32[1024]{0:T(1024)S(1)} all-reduce(f32[1024]{0:T(1024)S(1)} %fusion.2), channel_id=1, replica_groups=mesh['row'=8,'col'=16] {'col'}, use_global_device_ids=true, to_apply=%region_11.0 | all-reduce | flops 1024 | bytes 8192 | tf_op jit(solution)/shard_map/pmax | solution.py:14
  275.6 35.5 %psum.65 = f32[1024]{0:T(1024)S(1)} all-reduce(f32[1024]{0:T(1024)S(1)} %exponential_reduce_fusion.6), channel_id=1, replica_groups=mesh['row'=8,'col'=16] {'col'}, use_global_device_ids=true, to_apply=%region_13.0 | all-reduce | flops 1024 | bytes 8192 | tf_op jit(solution)/shard_map/psum | solution.py:15
  311.4 12.4 %pmax.66 = f32[512]{0:T(512)S(1)} all-reduce(f32[512]{0:T(512)S(1)} %fusion.3), channel_id=1, replica_groups=mesh['row'=8,'col'=16] {'row'}, use_global_device_ids=true, to_apply=%region_15.0 | all-reduce | flops 512 | bytes 4096 | tf_op jit(solution)/shard_map/pmax | solution.py:20
  323.8 0.6 exponential_reduce_fusion.5
  324.4 12.4 %psum.66 = f32[512]{0:T(512)S(1)} all-reduce(f32[512]{0:T(512)S(1)} %exponential_reduce_fusion.5), channel_id=1, replica_groups=mesh['row'=8,'col'=16] {'row'}, use_global_device_ids=true, to_apply=%region_17.0 | all-reduce | flops 512 | bytes 4096 | tf_op jit(solution)/shard_map/psum | solution.py:21
  337.1 37.5 %pmax.67 = f32[1024]{0:T(1024)S(1)} all-reduce(f32[1024]{0:T(1024)S(1)} %fusion.4), channel_id=1, replica_groups=mesh['row'=8,'col'=16] {'col'}, use_global_device_ids=true, to_apply=%region_19.0 | all-reduce | flops 1024 | bytes 8192 | tf_op jit(solution)/shard_map/pmax | solution.py:14
  375.1 35.5 %psum.67 = f32[1024]{0:T(1024)S(1)} all-reduce(f32[1024]{0:T(1024)S(1)} %exponential_reduce_fusion.4), channel_id=1, replica_groups=mesh['row'=8,'col'=16] {'col'}, use_global_device_ids=true, to_apply=%region_21.0 | all-reduce | flops 1024 | bytes 8192 | tf_op jit(solution)/shard_map/psum | solution.py:15
  410.8 12.4 %pmax.68 = f32[512]{0:T(512)S(1)} all-reduce(f32[512]{0:T(512)S(1)} %fusion.5), channel_id=1, replica_groups=mesh['row'=8,'col'=16] {'row'}, use_global_device_ids=true, to_apply=%region_23.0 | all-reduce | flops 512 | bytes 4096 | tf_op jit(solution)/shard_map/pmax | solution.py:20
  423.3 0.6 exponential_reduce_fusion.3
  423.8 12.4 %psum.68 = f32[512]{0:T(512)S(1)} all-reduce(f32[512]{0:T(512)S(1)} %exponential_reduce_fusion.3), channel_id=1, replica_groups=mesh['row'=8,'col'=16] {'row'}, use_global_device_ids=true, to_apply=%region_25.0 | all-reduce | flops 512 | bytes 4096 | tf_op jit(solution)/shard_map/psum | solution.py:21
  436.6 37.5 %pmax.69 = f32[1024]{0:T(1024)S(1)} all-reduce(f32[1024]{0:T(1024)S(1)} %fusion.6), channel_id=1, replica_groups=mesh['row'=8,'col'=16] {'col'}, use_global_device_ids=true, to_apply=%region_27.0 | all-reduce | flops 1024 | bytes 8192 | tf_op jit(solution)/shard_map/pmax | solution.py:14
  474.5 35.6 %psum.69 = f32[1024]{0:T(1024)S(1)} all-reduce(f32[1024]{0:T(1024)S(1)} %exponential_reduce_fusion.2), channel_id=1, replica_groups=mesh['row'=8,'col'=16] {'col'}, use_global_device_ids=true, to_apply=%region_29.0 | all-reduce | flops 1024 | bytes 8192 | tf_op jit(solution)/shard_map/psum | solution.py:15
  510.5 12.4 %pmax.70 = f32[512]{0:T(512)S(1)} all-reduce(f32[512]{0:T(512)S(1)} %fusion.7), channel_id=1, replica_groups=mesh['row'=8,'col'=16] {'row'}, use_global_device_ids=true, to_apply=%region_31.0 | all-reduce | flops 512 | bytes 4096 | tf_op jit(solution)/shard_map/pmax | solution.py:20
  522.9 0.6 exponential_reduce_fusion.1
  523.5 12.4 %psum.70 = f32[512]{0:T(512)S(1)} all-reduce(f32[512]{0:T(512)S(1)} %exponential_reduce_fusion.1), channel_id=1, replica_groups=mesh['row'=8,'col'=16] {'row'}, use_global_device_ids=true, to_apply=%region_33.0 | all-reduce | flops 512 | bytes 4096 | tf_op jit(solution)/shard_map/psum | solution.py:21
  536.2 37.5 %pmax.71 = f32[1024]{0:T(1024)S(1)} all-reduce(f32[1024]{0:T(1024)S(1)} %fusion.8), channel_id=1, replica_groups=mesh['row'=8,'col'=16] {'col'}, use_global_device_ids=true, to_apply=%region_35.0 | all-reduce | flops 1024 | bytes 8192 | tf_op jit(solution)/shard_map/pmax | solution.py:14
  574.2 35.5 %psum.71 = f32[1024]{0:T(1024)S(1)} all-reduce(f32[1024]{0:T(1024)S(1)} %exponential_reduce_fusion), channel_id=1, replica_groups=mesh['row'=8,'col'=16] {'col'}, use_global_device_ids=true, to_apply=%region_37.0 | all-reduce | flops 1024 | bytes 8192 | tf_op jit(solution)/shard_map/psum | solution.py:15
  609.6 10.4 %fusion.9 = f32[1024,4096]{1,0:T(8,128)} fusion(bf16[512,4096]{1,0:T(8,128)(2,1)} %all-gather.5.cloned.1.call-done, f32[1024,512]{0,1:T(8,128)S(1)} %get-tuple-element.4, f32[1024]{0:T(1024)S(1)} %log_add_fusion, f32[512]{0:T(512)S(1)} %multiply_subtract_fusion.4), kind=kOutput, calls=%fused_computation.31 | convolution fusion | flops 4297064448 | bytes 23074816 | tf_op jit(solution)/shard_map/dot_general | solution.py:49
  620.1 105.9 %reduce-scatter.2.cloned.1.call-done = f32[1024,256]{1,0:T(8,128)} async-done(((f32[1024,4096]{1,0:T(8,128)}), f32[1024,256]{1,0:T(8,128)}) %reduce-scatter.2.cloned.1.call-update) | async-done | bytes 1048592 | tf_op jit(solution)/shard_map/reduce_scatter | solution.py:50
  726.0 2.1 convert_element_type.15
  (32 shorter events, 5.5 us)
Async XLA Ops:
  7.2 37.4 %all-gather.5.cloned.1.call-start = ((), (), s32[]{:S(2)}) async-start(), calls=%async_computation.2 | async-start | bytes 4718592 | tf_op jit(solution)/shard_map/all_gather | solution.py:26
  7.9 116.8 %all-gather.3.cloned.1.call-start = ((), (), s32[]{:S(2)}) async-start(), calls=%async_computation.1 | async-start | bytes 8912896 | tf_op jit(solution)/shard_map/all_gather | solution.py:29
  8.6 717.4 %reduce-scatter.2.cloned.1.call-start = ((), (), s32[]{:S(2)}) async-start(), calls=%async_computation.3 | async-start | bytes 17825792 | tf_op jit(solution)/shard_map/reduce_scatter | solution.py:50
  124.7 5.8 copy-start
  510.2 13.3 %copy-start.1 = (f32[1024]{0:T(1024)}, f32[1024]{0:T(1024)S(1)}, u32[]{:S(2)}) copy-start(f32[1024]{0:T(1024)S(1)} %multiply_subtract_fusion) | copy-start | bytes 12292
  535.9 73.7 %copy-start.2 = (f32[512]{0:T(512)}, f32[512]{0:T(512)S(1)}, u32[]{:S(2)}) copy-start(f32[512]{0:T(512)S(1)} %multiply_subtract_fusion.4) | copy-start | bytes 6148
Sparse Core Ops, SparseCore 0:
  9.7 34.7 all-gather.4
  46.6 78.0 all-gather.2
  620.2 105.7 reduce-scatter.1
where the time goes:
time: 736 us; the launch traced here: 735 us
  blocking collectives  465 us (63%)
  waiting for transfers between devices  220 us (30%)
  matrix products  17.6 us (2%)
  other arithmetic  17.4 us (2%)
  between operations  13.8 us (2%)
    pmax x5, blocking collectives, row_logsum(): peak = lax.pmax(jnp.max(scores, axis=1), 'col')  188 us
    psum x5, blocking collectives, row_logsum(): total = lax.psum(jnp.sum(jnp.exp(scores - peak[:, None]), axis=1), 'col')  178 us
    reduce_scatter x1, waiting for transfers between devices, local(): lax.psum_scatter(partial_targets, 'col', scatter_dimension=1, tiled=True)  106 us
    all_gather x1, waiting for transfers between devices, local(): noise_whole = lax.all_gather(noise, 'col', axis=1, tiled=True)  77.1 us
    pmax x4, blocking collectives, col_logsum(): peak = lax.pmax(jnp.max(scores, axis=0), 'row')  49.7 us
    psum x4, blocking collectives, col_logsum(): total = lax.psum(jnp.sum(jnp.exp(scores - peak[None, :]), axis=0), 'row')  49.7 us
    all_gather x1, waiting for transfers between devices, local(): data_whole = lax.all_gather(data, 'row', axis=1, tiled=True)  35.8 us
  transfers between devices with their start and end apart: 3, of which 3 were waited for; matrix products, arithmetic and copies ran while one was open for 0% of the time, Pallas kernels for 0%

commit v1 on v0

--- a/solution.py
+++ b/solution.py
@@ -10,16 +10,24 @@
 EPS = 0.02
 
 
+def spread(values, axis):
+    size = lax.axis_size(axis)
+    copies = jnp.broadcast_to(values[None, None, :], (size, 1, values.shape[0]))
+    return lax.all_to_all(copies, axis, 0, 0, tiled=True)[:, 0, :]
+
+
+def lse(scores, axis):
+    peak = jnp.max(scores, axis=axis, keepdims=True)
+    total = jnp.sum(jnp.exp(scores - peak), axis=axis)
+    return jnp.squeeze(peak, axis) + jnp.log(total)
+
+
 def row_logsum(scores):
-    peak = lax.pmax(jnp.max(scores, axis=1), "col")
-    total = lax.psum(jnp.sum(jnp.exp(scores - peak[:, None]), axis=1), "col")
-    return peak + jnp.log(total)
+    return lse(spread(lse(scores, 1), "col"), 0)
 
 
 def col_logsum(scores):
-    peak = lax.pmax(jnp.max(scores, axis=0), "row")
-    total = lax.psum(jnp.sum(jnp.exp(scores - peak[None, :]), axis=0), "row")
-    return peak + jnp.log(total)
+    return lse(spread(lse(scores, 0), "row"), 0)
 
 
 def local(noise, data):

time: 736 us -> 361 us (0.49)
  blocking collectives: 465 us -> 88.4 us
    pmax x9 -> x0, blocking collectives: 238 us -> none  [the longest x5 188 us: row_logsum(): peak = lax.pmax(jnp.max(scores, axis=1), 'col')]
    psum x9 -> x0, blocking collectives: 227 us -> none  [the longest x5 178 us: row_logsum(): total = lax.psum(jnp.sum(jnp.exp(scores - peak[:, None]), axis=1), 'col')]
    all_to_all x0 -> x9, blocking collectives: none -> 88.4 us  [spread(): return lax.all_to_all(copies, axis, 0, 0, tiled=True)[:, 0, :]]
  transfers between devices with their start and end apart: 3 -> 3, of which waited for: 3 -> 3; matrix products, arithmetic and copies ran while one was open for 0% -> 1% of each run, Pallas kernels for 0% -> 0%
where the time goes in v1:
time: 361 us; the launch traced here: 360 us
  waiting for transfers between devices  221 us (61%)
  blocking collectives  88.4 us (24%)
  other arithmetic  18.1 us (5%)
  matrix products  17.6 us (5%)
  between operations  14.1 us (4%)
    reduce_scatter x1, waiting for transfers between devices, local(): lax.psum_scatter(partial_targets, 'col', scatter_dimension=1, tiled=True)  106 us
    all_to_all x9, blocking collectives, spread(): return lax.all_to_all(copies, axis, 0, 0, tiled=True)[:, 0, :]  88.4 us
    all_gather x1, waiting for transfers between devices, local(): noise_whole = lax.all_gather(noise, 'col', axis=1, tiled=True)  77.1 us
    all_gather x1, waiting for transfers between devices, local(): data_whole = lax.all_gather(data, 'row', axis=1, tiled=True)  35.8 us
    dot_general x1, matrix products, local(): jnp.dot(weights, data_whole, preferred_element_type=jnp.float32)  10.4 us
  transfers between devices with their start and end apart: 3, of which 3 were waited for; matrix products, arithmetic and copies ran while one was open for 1% of the time, Pallas kernels for 0%

profile of v1, /device:TPU:0, one launch (start us, length us, event | category | flops | bytes accessed | tf_op | source)
XLA Modules:
  0.0 359.8 jit_solution(16061514511875252491)
XLA Ops:
  7.2 0.7 all-gather.5.cloned.1.call-update
  7.9 0.7 all-gather.3.cloned.1.call-update
  8.7 35.8 %all-gather.5.cloned.1.call-done = bf16[512,4096]{1,0:T(8,128)(2,1)} async-done(((bf16[512,512]{1,0:T(8,128)(2,1)}), bf16[512,4096]{1,0:T(8,128)(2,1)}) %all-gather.5.cloned.1.call-update) | async-done | bytes 4194320 | tf_op jit(solution)/shard_map/all_gather | solution.py:34
  44.5 3.1 multiply_reduce_fusion.1
  47.6 77.1 %all-gather.3.cloned.1.call-done = bf16[1024,4096]{1,0:T(8,128)(2,1)} async-done(((bf16[1024,256]{1,0:T(8,128)(2,1)}), bf16[1024,4096]{1,0:T(8,128)(2,1)}) %all-gather.3.cloned.1.call-update) | async-done | bytes 8388624 | tf_op jit(solution)/shard_map/all_gather | solution.py:37
  124.7 5.2 %multiply_reduce_fusion = f32[1024]{0:T(1024)S(1)} fusion(bf16[1024,4096]{1,0:T(8,128)(2,1)} %all-gather.3.cloned.1.call-done), kind=kLoop, calls=%fused_computation | loop fusion | flops 12581888 | bytes 8392704 | tf_op jit(solution)/shard_map/reduce_sum | solution.py:41
  129.9 0.5 copy-done
  130.5 7.2 %fusion = (f32[1024]{0:T(1024)S(1)}, f32[1024,512]{0,1:T(8,128)S(1)}) fusion(bf16[1024,4096]{1,0:T(8,128)(2,1)S(1)} %copy-done, bf16[512,4096]{1,0:T(8,128)(2,1)} %all-gather.5.cloned.1.call-done, f32[512]{0:T(512)S(1)} %multiply_reduce_fusion.1, f32[1024]{0:T(1024)S(1)} %multiply_reduce_fusion), kind=kOutput, calls=%fused_computation.22 | convolution fusion | flops 4298636288 | bytes 14690304 | tf_op jit(solution)/shard_map/dot_general | solution.py:38
  137.6 0.4 exponential_reduce_fusion.8
  138.1 12.4 %all_to_all.45 = f32[16,1,1024]{2,1,0:T(1,128)S(1)} all-to-all(f32[16,1,1024]{2,1,0:T(1,128)S(1)} %broadcast_in_dim.18), channel_id=1, replica_groups=mesh['row'=8,'col'=16] {'col'}, dimensions={0} | all-to-all | bytes 131072 | tf_op jit(solution)/shard_map/all_to_all | solution.py:16
  150.9 0.6 exponential_reduce_fusion.7
  151.5 9.6 %all_to_all.46 = f32[8,1,512]{2,1,0:T(1,128)S(1)} all-to-all(f32[8,1,512]{2,1,0:T(1,128)S(1)} %broadcast_in_dim.19), channel_id=1, replica_groups=mesh['row'=8,'col'=16] {'row'}, dimensions={0} | all-to-all | bytes 32768 | tf_op jit(solution)/shard_map/all_to_all | solution.py:16
  161.2 0.3 fusion.2
  161.5 0.5 exponential_reduce_fusion.6
  162.0 10.8 %all_to_all.47 = f32[16,1,1024]{2,1,0:T(1,128)S(1)} all-to-all(f32[16,1,1024]{2,1,0:T(1,128)S(1)} %broadcast_in_dim.20), channel_id=1, replica_groups=mesh['row'=8,'col'=16] {'col'}, dimensions={0} | all-to-all | bytes 131072 | tf_op jit(solution)/shard_map/all_to_all | solution.py:16
  173.2 0.6 exponential_reduce_fusion.5
  173.8 7.7 %all_to_all.48 = f32[8,1,512]{2,1,0:T(1,128)S(1)} all-to-all(f32[8,1,512]{2,1,0:T(1,128)S(1)} %broadcast_in_dim.21), channel_id=1, replica_groups=mesh['row'=8,'col'=16] {'row'}, dimensions={0} | all-to-all | bytes 32768 | tf_op jit(solution)/shard_map/all_to_all | solution.py:16
  181.6 0.3 fusion.4
  181.9 0.5 exponential_reduce_fusion.4
  182.5 10.8 %all_to_all.49 = f32[16,1,1024]{2,1,0:T(1,128)S(1)} all-to-all(f32[16,1,1024]{2,1,0:T(1,128)S(1)} %broadcast_in_dim.22), channel_id=1, replica_groups=mesh['row'=8,'col'=16] {'col'}, dimensions={0} | all-to-all | bytes 131072 | tf_op jit(solution)/shard_map/all_to_all | solution.py:16
  193.6 0.6 exponential_reduce_fusion.3
  194.3 7.7 %all_to_all.50 = f32[8,1,512]{2,1,0:T(1,128)S(1)} all-to-all(f32[8,1,512]{2,1,0:T(1,128)S(1)} %broadcast_in_dim.23), channel_id=1, replica_groups=mesh['row'=8,'col'=16] {'row'}, dimensions={0} | all-to-all | bytes 32768 | tf_op jit(solution)/shard_map/all_to_all | solution.py:16
  202.0 0.3 fusion.6
  202.3 0.5 exponential_reduce_fusion.2
  202.9 10.8 %all_to_all.51 = f32[16,1,1024]{2,1,0:T(1,128)S(1)} all-to-all(f32[16,1,1024]{2,1,0:T(1,128)S(1)} %broadcast_in_dim.24), channel_id=1, replica_groups=mesh['row'=8,'col'=16] {'col'}, dimensions={0} | all-to-all | bytes 131072 | tf_op jit(solution)/shard_map/all_to_all | solution.py:16
  214.1 0.6 exponential_reduce_fusion.1
  214.7 7.7 %all_to_all.52 = f32[8,1,512]{2,1,0:T(1,128)S(1)} all-to-all(f32[8,1,512]{2,1,0:T(1,128)S(1)} %broadcast_in_dim.25), channel_id=1, replica_groups=mesh['row'=8,'col'=16] {'row'}, dimensions={0} | all-to-all | bytes 32768 | tf_op jit(solution)/shard_map/all_to_all | solution.py:16
  222.8 0.5 exponential_reduce_fusion
  223.3 10.8 %all_to_all.53 = f32[16,1,1024]{2,1,0:T(1,128)S(1)} all-to-all(f32[16,1,1024]{2,1,0:T(1,128)S(1)} %broadcast_in_dim.26), channel_id=1, replica_groups=mesh['row'=8,'col'=16] {'col'}, dimensions={0} | all-to-all | bytes 131072 | tf_op jit(solution)/shard_map/all_to_all | solution.py:16
  234.2 10.4 %fusion.9 = f32[1024,4096]{1,0:T(8,128)} fusion(bf16[512,4096]{1,0:T(8,128)(2,1)} %all-gather.5.cloned.1.call-done, f32[1024,512]{0,1:T(8,128)S(1)} %get-tuple-element.4, f32[1024]{0:T(1024)S(1)} %log_add_fusion, f32[512]{0:T(512)S(1)} %multiply_subtract_fusion.4), kind=kOutput, calls=%fused_computation.31 | convolution fusion | flops 4297064448 | bytes 23074816 | tf_op jit(solution)/shard_map/dot_general | solution.py:57
  244.7 106.5 %reduce-scatter.2.cloned.1.call-done = f32[1024,256]{1,0:T(8,128)} async-done(((f32[1024,4096]{1,0:T(8,128)}), f32[1024,256]{1,0:T(8,128)}) %reduce-scatter.2.cloned.1.call-update) | async-done | bytes 1048592 | tf_op jit(solution)/shard_map/reduce_scatter | solution.py:58
  351.2 2.1 convert_element_type.15
  (59 shorter events, 2.6 us)
Async XLA Ops:
  7.2 37.4 %all-gather.5.cloned.1.call-start = ((), (), s32[]{:S(2)}) async-start(), calls=%async_computation.11 | async-start | bytes 4718592 | tf_op jit(solution)/shard_map/all_gather | solution.py:34
  7.9 116.8 %all-gather.3.cloned.1.call-start = ((), (), s32[]{:S(2)}) async-start(), calls=%async_computation.10 | async-start | bytes 8912896 | tf_op jit(solution)/shard_map/all_gather | solution.py:37
  8.6 342.5 %reduce-scatter.2.cloned.1.call-start = ((), (), s32[]{:S(2)}) async-start(), calls=%async_computation.12 | async-start | bytes 17825792 | tf_op jit(solution)/shard_map/reduce_scatter | solution.py:58
  124.7 5.8 %copy-start = (bf16[1024,4096]{1,0:T(8,128)(2,1)S(1)}, bf16[1024,4096]{1,0:T(8,128)(2,1)}, u32[]{:S(2)}) copy-start(bf16[1024,4096]{1,0:T(8,128)(2,1)} %all-gather.3.cloned.1.call-done) | copy-start | bytes 25165828
  213.8 0.9 copy-start.1
  222.5 11.8 %copy-start.2 = (f32[512]{0:T(512)}, f32[512]{0:T(512)S(1)}, u32[]{:S(2)}) copy-start(f32[512]{0:T(512)S(1)} %multiply_subtract_fusion.4) | copy-start | bytes 6148
Sparse Core Ops, SparseCore 0:
  9.7 34.7 all-gather.4
  46.6 78.0 all-gather.2
  244.8 106.3 reduce-scatter.1

commit v2 on v1

v2 whole, which is shorter than its diff:
```python
import functools

import jax
import jax.numpy as jnp
from jax import lax
from jax.experimental import pallas as pl
from jax.experimental.pallas import tpu as pltpu
from jax.sharding import PartitionSpec as P

D = 4096
ITERS = 4
COUNT = 8192
EPS = 0.02

AXES = ("row", "col")
PLACES = [(z, c, y, x) for z in range(4) for c in range(2) for y in range(4) for x in range(4)]


def flat(z, c, y, x):
    return ((z % 4 * 2 + c % 2) * 4 + y % 4) * 4 + x % 4


def pairs(move):
    return [(flat(*p), flat(*move(*p))) for p in PLACES]


def groups(shared):
    found = {}
    for p in PLACES:
        key = tuple(v for v, name in zip(p, "zcyx") if name in shared)
        found.setdefault(key, []).append(flat(*p))
    return list(found.values())


OTHER = pairs(lambda z, c, y, x: (z, c + 1, y, x))
X_UP = pairs(lambda z, c, y, x: (z, c, y, x + 1))
X_DOWN = pairs(lambda z, c, y, x: (z, c, y, x - 1))
FIRST_UP = pairs(lambda z, c, y, x: (z + 1 - c, c, y + c, x))
FIRST_DOWN = pairs(lambda z, c, y, x: (z - 1 + c, c, y - c, x))
SECOND_UP = pairs(lambda z, c, y, x: (z + c, c, y + 1 - c, x))
SECOND_DOWN = pairs(lambda z, c, y, x: (z - c, c, y - 1 + c, x))


def send(values, where):
    return lax.ppermute(values, AXES, where)


def spread(values, size, shared):
    copies = jnp.broadcast_to(values[None, None, :], (size, 1, values.shape[0]))
    return lax.all_to_all(
        copies, AXES, 0, 0, tiled=True, axis_index_groups=groups(shared)
    )[:, 0, :]


def ring(block, up, down):
    half = block.shape[0] // 2
    below, above = send(block, up), send(block, down)
    far = jnp.concatenate([send(below[:half], up), send(above[half:], down)])
    return [block, above, far, below]


def lse(scores, axis):
    peak = jnp.max(scores, axis=axis, keepdims=True)
    total = jnp.sum(jnp.exp(scores - peak), axis=axis)
    return jnp.squeeze(peak, axis) + jnp.log(total)


def block_place(place, first, second):
    z, c, y = place[0], place[1], place[2]
    far_z = jnp.where(c == 0, first, second)
    far_y = jnp.where(c == 0, second, first)
    return lax.rem(y + far_y, 4), lax.rem(z + far_z, 4)


def gram_kernel(seconds, first_call, place, own, other, *refs):
    blocks = refs[: len(seconds)]
    gram_in, squares_in = (None, None) if first_call else refs[len(seconds) : len(seconds) + 2]
    gram, squares = refs[-2:]
    step = pl.program_id(0)

    @pl.when(step == 0)
    def _():
        gram[...] = jnp.zeros_like(gram) if first_call else gram_in[...]
        squares[...] = jnp.zeros_like(squares) if first_call else squares_in[...]

    c, x = place[1], place[3]
    for second, block in zip(seconds, blocks):
        row_group, col_group = block_place(place, step, second)
        rows = pl.ds(pl.multiple_of(row_group * 256, 256), 256)
        sums = [None, None]
        total = None
        for part in range(4):
            values = block[0, :, part * 256 : (part + 1) * 256]
            index = lax.rem(part + 4 - x, 4) * 4 + col_group
            for k, source in enumerate((own, other)):
                term = lax.dot_general(
                    source[index], values, (((1,), (1,)), ((), ())), preferred_element_type=jnp.float32
                )
                sums[k] = term if part == 0 else sums[k] + term
            wide = values.astype(jnp.float32)
            wide = wide * wide
            halves = wide[:, :128] + wide[:, 128:]
            total = halves if part == 0 else total + halves
        squares[rows, :] += total
        gram[pl.ds(pl.multiple_of(c * 256, 256), 256), rows] += sums[0]
        gram[pl.ds(pl.multiple_of(256 - c * 256, 256), 256), rows] += sums[1]


def gram_of(place, own, other, blocks, seconds, before):
    whole = lambda shape: pl.BlockSpec(shape, lambda i, place: (0,) * len(shape))
    specs = [whole((16, 256, 256))] * 2
    specs += [pl.BlockSpec((1, 256, 1024), lambda i, place: (i, 0, 0))] * len(blocks)
    outs = [((512, 1024), jnp.float32), ((1024, 128), jnp.float32)]
    operands = [own, other, *blocks]
    aliases = {}
    if before is not None:
        aliases = {1 + len(operands): 0, 2 + len(operands): 1}
        operands += before
        specs += [whole(shape) for shape, _ in outs]
    return pl.pallas_call(
        functools.partial(gram_kernel, seconds, before is None),
        out_shape=[jax.ShapeDtypeStruct(*out) for out in outs],
        grid_spec=pltpu.PrefetchScalarGridSpec(
            num_scalar_prefetch=1,
            grid=(4,),
            in_specs=specs,
            out_specs=[whole(shape) for shape, _ in outs],
        ),
        input_output_aliases=aliases,
        compiler_params=pltpu.CompilerParams(vmem_limit_bytes=40 * 2**20),
        cost_estimate=pl.CostEstimate(
            flops=len(blocks) * 4 * 2 * 512 * 256 * 1024,
            bytes_accessed=len(blocks) * 2 * 2**20 + 8 * 2**20,
            transcendentals=0,
        ),
    )(place, *operands)


def mix_kernel(place, weights, *refs):
    blocks, out, sums = refs[:4], refs[4], refs[5]
    step = pl.program_id(0)

    @pl.when(step == 0)
    def _():
        sums[...] = jnp.zeros_like(sums)

    for second, block in enumerate(blocks):
        row_group, col_group = block_place(place, step, second)
        left = weights[:, pl.ds(pl.multiple_of(row_group * 256, 256), 256)]
        for part in range(4):
            sums[col_group * 4 + part] += jnp.dot(
                left, block[0, :, part * 256 : (part + 1) * 256], preferred_element_type=jnp.float32
            )

    @pl.when(step == 3)
    def _():
        out[...] = sums[...].astype(out.dtype)


def mix(place, weights, blocks, dtype):
    whole = lambda shape: pl.BlockSpec(shape, lambda i, place: (0,) * len(shape))
    return pl.pallas_call(
        mix_kernel,
        out_shape=jax.ShapeDtypeStruct((16, 256, 256), dtype),
        grid_spec=pltpu.PrefetchScalarGridSpec(
            num_scalar_prefetch=1,
            grid=(4,),
            in_specs=[whole((256, 1024))]
            + [pl.BlockSpec((1, 256, 1024), lambda i, place: (i, 0, 0))] * 4,
            out_specs=whole((16, 256, 256)),
            scratch_shapes=[pltpu.VMEM((16, 256, 256), jnp.float32)],
        ),
        compiler_params=pltpu.CompilerParams(vmem_limit_bytes=40 * 2**20),
        cost_estimate=pl.CostEstimate(
            flops=2 * 256 * 1024 * 4096, bytes_accessed=14 * 2**20, transcendentals=0
        ),
    )(place, weights, *blocks)


def local(noise, data):
    row, col = lax.axis_index("row"), lax.axis_index("col")
    z, c, y, x = row // 2, row % 2, col // 4, col % 4
    place = jnp.stack([z, c, y, x]).astype(jnp.int32)

    halves = data.reshape(2, 256, 512)
    kept = lax.dynamic_index_in_dim(halves, c, 0, keepdims=False)
    came = send(lax.dynamic_index_in_dim(halves, 1 - c, 0, keepdims=False), OTHER)
    block = jnp.where(
        c == 0, jnp.concatenate([kept, came], 1), jnp.concatenate([came, kept], 1)
    )
    line = jnp.stack(ring(block, FIRST_UP, FIRST_DOWN))
    own = lax.all_to_all(
        noise.reshape(4, 256, 256), AXES, 0, 0, tiled=True, axis_index_groups=groups("zcx")
    )
    own = jnp.concatenate(ring(own, X_UP, X_DOWN))
    other = send(own, OTHER)
    blocks = ring(line, SECOND_UP, SECOND_DOWN)

    parts = gram_of(place, own, other, blocks[:1], (0,), None)
    parts = gram_of(place, own, other, [blocks[1], blocks[3]], (1, 3), parts)
    gram, squares = gram_of(place, own, other, blocks[2:3], (2,), parts)

    def square_sum(values):
        return jnp.sum(values.astype(jnp.float32) ** 2, axis=(0, 2))

    sq_own, sq_other = square_sum(own), square_sum(other)
    noise_sq = jnp.where(
        c == 0, jnp.concatenate([sq_own, sq_other]), jnp.concatenate([sq_other, sq_own])
    )
    data_sq = jnp.sum(squares, axis=1)
    scores = (2.0 * gram - noise_sq[:, None] - data_sq[None, :]) / (D * EPS)

    def row_lse(g):
        return lse(spread(lse(scores + g[None, :], 1), 8, "zy"), 0)

    log_count = jnp.log(float(COUNT))
    g = jnp.zeros((1024,), jnp.float32)
    for step in range(ITERS):
        f = -log_count - row_lse(g)
        g = -log_count - lse(spread(lse(scores + f[:, None], 0), 16, "cx"), 0)
    norm = row_lse(g)
    weights = jnp.exp(scores + g[None, :] - norm[:, None]).astype(jnp.bfloat16)
    weights = weights.reshape(2, 256, 1024)

    away = mix(place, lax.dynamic_index_in_dim(weights, 1 - c, 0, keepdims=False), blocks, jnp.bfloat16)
    came = send(away, OTHER)
    mine = mix(place, lax.dynamic_index_in_dim(weights, c, 0, keepdims=False), blocks, jnp.float32)
    shares = (mine + came.astype(jnp.float32)).astype(jnp.bfloat16)
    shares = lax.all_to_all(shares, "col", 0, 0, tiled=True)
    targets = jnp.sum(shares.reshape(4, 4, 256, 256).astype(jnp.float32), axis=1)
    targets = targets.reshape(1024, 256).astype(jnp.bfloat16)

    f_here = lax.dynamic_slice(f, (c * 256,), (256,))
    noise_potential = EPS * spread(f_here, 4, "zcx").reshape(1024)
    g_here = lax.dynamic_slice(g, (y * 256,), (256,))
    g_came = send(g_here, OTHER)
    data_potential = EPS * jnp.where(
        c == 0, jnp.concatenate([g_here, g_came]), jnp.concatenate([g_came, g_here])
    )
    return (targets, noise_potential, data_potential)


def solution(mesh):
    placed = (P("row", "col"), P("col", "row"))
    return jax.shard_map(
        local,
        mesh=mesh,
        in_specs=placed,
        out_specs=(P("row", "col"), P("row"), P("col")),
        check_vma=False,
    )
```

time: 361 us -> 255 us (0.71)
  waiting for transfers between devices: 221 us -> 67.9 us
  starting transfers between devices: 0.11 us -> 35.1 us
  Pallas kernels: 0 us -> 29.2 us
  matrix products: 17.6 us -> 0 us
  between operations: 14.1 us -> 1.3 us
  local copies, waits for them, and re-layouts: 0.79 us -> 12.7 us
  other arithmetic: 18.1 us -> 24.3 us
  blocking collectives: 88.4 us -> 83.5 us
    all_gather x2 -> x0, waiting for transfers between devices: 113 us -> none  [the longest x1 77.1 us: local(): noise_whole = lax.all_gather(noise, 'col', axis=1, tiled=True)]
    reduce_scatter x1 -> x0, waiting for transfers between devices: 106 us -> none  [local(): lax.psum_scatter(partial_targets, 'col', scatter_dimension=1, tiled=True)]
    all_to_all x0 -> x3, waiting for transfers between devices: none -> 38.1 us  [the longest x1 31.4 us: local(): shares = lax.all_to_all(shares, 'col', 0, 0, tiled=True)]
    ppermute x0 -> x16, waiting for transfers between devices: none -> 29.8 us  [send(): return lax.ppermute(values, AXES, where)]
    pallas_call x0 -> x5, Pallas kernels: none -> 29.2 us  [the longest x3 16.2 us: gram_of(): pl.pallas_call(functools.partial(gram_kernel, seconds, before is None), o...]
    ppermute x0 -> x16, starting transfers between devices: none -> 21.8 us  [send(): return lax.ppermute(values, AXES, where)]
    dot_general x2 -> x0, matrix products: 17.6 us -> none  [the longest x1 10.4 us: local(): jnp.dot(weights, data_whole, preferred_element_type=jnp.float32)]
    all_to_all x0 -> x3, starting transfers between devices: none -> 13.3 us  [the longest x1 5.46 us: local(): shares = lax.all_to_all(shares, 'col', 0, 0, tiled=True)]
  transfers between devices with their start and end apart: 3 -> 19, of which waited for: 3 -> 5; matrix products, arithmetic and copies ran while one was open for 1% -> 6% of each run, Pallas kernels for 0% -> 7%
where the time goes in v2:
time: 255 us; the launch traced here: 254 us
  blocking collectives  83.5 us (33%)
  waiting for transfers between devices  67.9 us (27%)
  starting transfers between devices  35.1 us (14%)
  Pallas kernels  29.2 us (11%)
  other arithmetic  24.3 us (10%)
  local copies, waits for them, and re-layouts  12.7 us (5%)
    all_to_all x9, blocking collectives, spread(): lax.all_to_all(copies, AXES, 0, 0, tiled=True, axis_index_groups=groups(s...  83.5 us
    all_to_all x1, waiting for transfers between devices, local(): shares = lax.all_to_all(shares, 'col', 0, 0, tiled=True)  31.4 us
    ppermute x16, waiting for transfers between devices, send(): return lax.ppermute(values, AXES, where)  29.8 us
    ppermute x16, starting transfers between devices, send(): return lax.ppermute(values, AXES, where)  21.8 us
    pallas_call x3, Pallas kernels, gram_of(): pl.pallas_call(functools.partial(gram_kernel, seconds, before is None), o...  16.2 us
    pallas_call x2, Pallas kernels, mix(): pl.pallas_call(mix_kernel, out_shape=jax.ShapeDtypeStruct((16, 256, 256),...  13 us
    unnamed x27, local copies, waits for them, and re-layouts  8.08 us
    reduce_sum x18, other arithmetic, lse(): total = jnp.sum(jnp.exp(scores - peak), axis=axis)  7.39 us
  transfers between devices with their start and end apart: 19, of which 5 were waited for; matrix products, arithmetic and copies ran while one was open for 6% of the time, Pallas kernels for 7%

profile of v2, /device:TPU:0, one launch (start us, length us, event | category | flops | bytes accessed | tf_op | source)
XLA Modules:
  0.0 253.9 jit_solution(17432507879304162959)
XLA Ops:
  1.8 4.6 %all-to-all-start = ((bf16[4,256,256]{2,1,0:T(8,128)(2,1)}), bf16[4,256,256]{2,1,0:T(8,128)(2,1)S(1)}, u32[]{:S(2)}, u32[]{:S(2)}) async-start(bf16[4,256,256]{2,1,0:T(8,128)(2,1)} %bitcast.84), calls=%async_computation | async-start | bytes 1048576 | tf_op jit(solution)/shard_map/all_to_all | solution.py:192
  6.5 4.1 %collective-permute-start.6 = (bf16[256,1024]{1,0:T(8,128)(2,1)S(1)}, bf16[256,1024]{1,0:T(8,128)(2,1)S(1)}, u32[]{:S(2)}, u32[]{:S(2)}) collective-permute-start(bf16[256,1024]{1,0:T(8,128)(2,1)S(1)} %maximum_select_fusion.1), channel_id=1, source_target_pairs={{0,96},{1,97},{2,98},{3,99},{4,100},{5,101},{6,102},{7,103},{8,104... | collective-permute-start | bytes 1572872 | tf_op jit(solution)/shard_map/ppermute | solution.py:45
  10.6 6.7 %all-to-all-done = bf16[4,256,256]{2,1,0:T(8,128)(2,1)S(1)} async-done(((bf16[4,256,256]{2,1,0:T(8,128)(2,1)}), bf16[4,256,256]{2,1,0:T(8,128)(2,1)S(1)}, u32[]{:S(2)}, u32[]{:S(2)}) %all-to-all-start) | async-done | bytes 524320 | tf_op jit(solution)/shard_map/all_to_all | solution.py:192
  18.8 1.7 collective-permute-start
  20.5 4.1 %collective-permute-start.9 = (bf16[128,1024]{1,0:T(8,128)(2,1)S(1)}, bf16[128,1024]{1,0:T(8,128)(2,1)S(1)}, u32[]{:S(2)}, u32[]{:S(2)}) collective-permute-start(bf16[128,1024]{1,0:T(8,128)(2,1)S(1)} %slice.27), channel_id=1, source_target_pairs={{0,96},{1,97},{2,98},{3,99},{4,100},{5,101},{6,102},{7,103},{8,104... | collective-permute-start | bytes 786440 | tf_op jit(solution)/shard_map/ppermute | solution.py:45
  25.6 5.3 %collective-permute-done.1 = bf16[4,256,256]{2,1,0:T(8,128)(2,1)S(1)} collective-permute-done((bf16[4,256,256]{2,1,0:T(8,128)(2,1)S(1)}, bf16[4,256,256]{2,1,0:T(8,128)(2,1)S(1)}, u32[]{:S(2)}, u32[]{:S(2)}) %collective-permute-start.1) | collective-permute-done | bytes 524320 | tf_op jit(solution)/shard_map/ppermute | solution.py:45
  31.4 3.0 %collective-permute-start.3 = (bf16[2,256,256]{2,1,0:T(8,128)(2,1)S(1)}, bf16[2,256,256]{2,1,0:T(8,128)(2,1)S(1)}, u32[]{:S(2)}, u32[]{:S(2)}) collective-permute-start(bf16[2,256,256]{2,1,0:T(8,128)(2,1)S(1)} %slice.25), channel_id=1, source_target_pairs={{0,3},{1,0},{2,1},{3,2},{4,7},{5,4},{6,5},{7,6},{8,11},{9,8},{10,9... | collective-permute-start | bytes 786440 | tf_op jit(solution)/shard_map/ppermute | solution.py:45
  34.5 1.6 pad_maximum_fusion.refs_0_
  36.7 2.7 %collective-permute-start.12 = (bf16[4,256,1024]{2,1,0:T(8,128)(2,1)}, bf16[4,256,1024]{2,1,0:T(8,128)(2,1)}, u32[]{:S(2)}, u32[]{:S(2)}) collective-permute-start(bf16[4,256,1024]{2,1,0:T(8,128)(2,1)} %pad_maximum_fusion.refs_0_), channel_id=1, source_target_pairs={{0,12},{1,13},{2,14},{3,15},{4,0},{5,1},{6,2},{7,3},{8,4},{9,5},{1... | collective-permute-start | bytes 6291464 | tf_op jit(solution)/shard_map/ppermute | solution.py:45
  39.6 23.9 %collective-permute-done.10.refs_1_.refs_3_ = bf16[4,256,1024]{2,1,0:T(8,128)(2,1)S(1)} collective-permute-done((bf16[4,256,1024]{2,1,0:T(8,128)(2,1)}, bf16[4,256,1024]{2,1,0:T(8,128)(2,1)S(1)}, u32[]{:S(2)}, u32[]{:S(2)}) %collective-permute-start.10) | collective-permute-done | bytes 2097184 | tf_op jit(solution)/shard_map/ppermute | solution.py:45
  67.2 3.3 %collective-permute-start.13 = (bf16[2,256,1024]{2,1,0:T(8,128)(2,1)S(1)}, bf16[2,256,1024]{2,1,0:T(8,128)(2,1)S(1)}, u32[]{:S(2)}, u32[]{:S(2)}) collective-permute-start(bf16[2,256,1024]{2,1,0:T(8,128)(2,1)S(1)} %slice.29), channel_id=1, source_target_pairs={{0,12},{1,13},{2,14},{3,15},{4,0},{5,1},{6,2},{7,3},{8,4},{9,5},{1... | collective-permute-start | bytes 3145736 | tf_op jit(solution)/shard_map/ppermute | solution.py:45
  71.1 1.6 copy-done.1
  72.7 5.2 %shard_map.49 = (f32[512,1024]{1,0:T(8,128)S(1)}, f32[1024,128]{1,0:T(8,128)S(1)}) custom-call(s32[4]{0:T(128)S(1)} %pad_add_fusion.place, bf16[16,256,256]{2,1,0:T(8,128)(2,1)S(1)} %copy-done.1, bf16[16,256,256]{2,1,0:T(8,128)(2,1)} %collective-permute-done.4.other, bf16[4,256,1024]{2,1,0:T(8,128)(2,1)} %pad_maximum_fusion.refs_0_), custom_call_target="tpu_custom_call" | custom-call | flops 1073741824 | bytes 10485760 | tf_op jit(solution)/shard_map/pallas_call | solution.py:120
  77.9 2.2 multiply_reduce_fusion
  80.1 6.3 %shard_map.50 = (f32[512,1024]{1,0:T(8,128)S(1)}, f32[1024,128]{1,0:T(8,128)S(1)}) custom-call(s32[4]{0:T(128)S(1)} %pad_add_fusion.place, bf16[16,256,256]{2,1,0:T(8,128)(2,1)S(1)} %copy-done.1, bf16[16,256,256]{2,1,0:T(8,128)(2,1)} %collective-permute-done.4.other, ...), custom_call_target="tpu_custom_call", output_to_operand_aliasing={{0}: (5, {}), {1}: (6, {})} | custom-call | flops 2147483648 | bytes 12582912 | tf_op jit(solution)/shard_map/pallas_call | solution.py:120
  87.8 4.7 %shard_map.51 = (f32[512,1024]{1,0:T(8,128)S(1)}, f32[1024,128]{1,0:T(8,128)S(1)}) custom-call(s32[4]{0:T(128)S(1)} %pad_add_fusion.place, bf16[16,256,256]{2,1,0:T(8,128)(2,1)S(1)} %copy-done.1, bf16[16,256,256]{2,1,0:T(8,128)(2,1)} %collective-permute-done.4.other, ...), custom_call_target="tpu_custom_call", output_to_operand_aliasing={{0}: (4, {}), {1}: (5, {})} | custom-call | flops 1073741824 | bytes 10485760 | tf_op jit(solution)/shard_map/pallas_call | solution.py:120
  94.1 7.6 %all_to_all.60 = f32[8,1,512]{2,1,0:T(1,128)S(1)} all-to-all(f32[8,1,512]{2,1,0:T(1,128)S(1)} %broadcast_in_dim.20), channel_id=1, replica_groups={{0,1,2,3,16,17,18,19},{4,5,6,7,20,21,22,23},{8,9,10,11,24,25,26,27},{12..., dimensions={0} | all-to-all | bytes 32768 | tf_op jit(solution)/shard_map/all_to_all | solution.py:50
  103.1 12.8 %all_to_all.61 = f32[16,1,1024]{2,1,0:T(1,128)S(1)} all-to-all(f32[16,1,1024]{2,1,0:T(1,128)S(1)} %broadcast_in_dim.21), channel_id=1, replica_groups={{0,4,8,12,32,36,40,44,64,68,72,76,96,100,104,108},{1,5,9,13,33,37,41,45..., dimensions={0} | all-to-all | bytes 131072 | tf_op jit(solution)/shard_map/all_to_all | solution.py:50
  117.6 7.6 %all_to_all.62 = f32[8,1,512]{2,1,0:T(1,128)S(1)} all-to-all(f32[8,1,512]{2,1,0:T(1,128)S(1)} %broadcast_in_dim.22), channel_id=1, replica_groups={{0,1,2,3,16,17,18,19},{4,5,6,7,20,21,22,23},{8,9,10,11,24,25,26,27},{12..., dimensions={0} | all-to-all | bytes 32768 | tf_op jit(solution)/shard_map/all_to_all | solution.py:50
  126.6 10.8 %all_to_all.63 = f32[16,1,1024]{2,1,0:T(1,128)S(1)} all-to-all(f32[16,1,1024]{2,1,0:T(1,128)S(1)} %broadcast_in_dim.23), channel_id=1, replica_groups={{0,4,8,12,32,36,40,44,64,68,72,76,96,100,104,108},{1,5,9,13,33,37,41,45..., dimensions={0} | all-to-all | bytes 131072 | tf_op jit(solution)/shard_map/all_to_all | solution.py:50
  139.1 7.6 %all_to_all.64 = f32[8,1,512]{2,1,0:T(1,128)S(1)} all-to-all(f32[8,1,512]{2,1,0:T(1,128)S(1)} %broadcast_in_dim.24), channel_id=1, replica_groups={{0,1,2,3,16,17,18,19},{4,5,6,7,20,21,22,23},{8,9,10,11,24,25,26,27},{12..., dimensions={0} | all-to-all | bytes 32768 | tf_op jit(solution)/shard_map/all_to_all | solution.py:50
  148.0 10.8 %all_to_all.65 = f32[16,1,1024]{2,1,0:T(1,128)S(1)} all-to-all(f32[16,1,1024]{2,1,0:T(1,128)S(1)} %broadcast_in_dim.25), channel_id=1, replica_groups={{0,4,8,12,32,36,40,44,64,68,72,76,96,100,104,108},{1,5,9,13,33,37,41,45..., dimensions={0} | all-to-all | bytes 131072 | tf_op jit(solution)/shard_map/all_to_all | solution.py:50
  160.5 7.6 %all_to_all.66 = f32[8,1,512]{2,1,0:T(1,128)S(1)} all-to-all(f32[8,1,512]{2,1,0:T(1,128)S(1)} %broadcast_in_dim.26), channel_id=1, replica_groups={{0,1,2,3,16,17,18,19},{4,5,6,7,20,21,22,23},{8,9,10,11,24,25,26,27},{12..., dimensions={0} | all-to-all | bytes 32768 | tf_op jit(solution)/shard_map/all_to_all | solution.py:50
  169.5 10.8 %all_to_all.67 = f32[16,1,1024]{2,1,0:T(1,128)S(1)} all-to-all(f32[16,1,1024]{2,1,0:T(1,128)S(1)} %broadcast_in_dim.27), channel_id=1, replica_groups={{0,4,8,12,32,36,40,44,64,68,72,76,96,100,104,108},{1,5,9,13,33,37,41,45..., dimensions={0} | all-to-all | bytes 131072 | tf_op jit(solution)/shard_map/all_to_all | solution.py:50
  181.9 7.6 %all_to_all.68 = f32[8,1,512]{2,1,0:T(1,128)S(1)} all-to-all(f32[8,1,512]{2,1,0:T(1,128)S(1)} %broadcast_in_dim.28), channel_id=1, replica_groups={{0,1,2,3,16,17,18,19},{4,5,6,7,20,21,22,23},{8,9,10,11,24,25,26,27},{12..., dimensions={0} | all-to-all | bytes 32768 | tf_op jit(solution)/shard_map/all_to_all | solution.py:50
  191.9 7.2 %shard_map.53 = bf16[16,256,256]{2,1,0:T(8,128)(2,1)} custom-call(s32[4]{0:T(128)S(1)} %pad_add_fusion.place, bf16[256,1024]{1,0:T(8,128)(2,1)S(1)} %get-tuple-element.15.weights, bf16[4,256,1024]{2,1,0:T(8,128)(2,1)} %pad_maximum_fusion.refs_0_, bf16[4,256,1024]{2,1,0:T(8,128)(2,1)} %collective-permute-done.12.refs_0_.refs_1_, ...), custom_call_target="tpu_custom_call" | custom-call | flops 2147483648 | bytes 14680064 | tf_op jit(solution)/shard_map/pallas_call | solution.py:162
  199.8 3.2 %all-to-all-start.11 = ((f32[4,1,256]{2,1,0:T(1,128)}), f32[4,1,256]{2,1,0:T(1,128)S(1)}, u32[]{:S(2)}, u32[]{:S(2)}) async-start(f32[4,1,256]{2,1,0:T(1,128)} %broadcast_in_dim.29), calls=%async_computation.11 | async-start | bytes 8192 | tf_op jit(solution)/shard_map/all_to_all | solution.py:50
  203.1 1.6 copy-done.8
  204.7 5.8 %shard_map.52 = f32[16,256,256]{2,1,0:T(8,128)S(1)} custom-call(s32[4]{0:T(128)S(1)} %pad_add_fusion.place, bf16[256,1024]{1,0:T(8,128)(2,1)S(1)} %get-tuple-element.16.weights, bf16[4,256,1024]{2,1,0:T(8,128)(2,1)} %pad_maximum_fusion.refs_0_, bf16[4,256,1024]{2,1,0:T(8,128)(2,1)} %collective-permute-done.12.refs_0_.refs_1_, ...), custom_call_target="tpu_custom_call" | custom-call | flops 2147483648 | bytes 14680064 | tf_op jit(solution)/shard_map/pallas_call | solution.py:162
  210.5 3.5 %add_convert_fusion = bf16[16,256,256]{2,1,0:T(8,128)(2,1)} fusion(f32[16,256,256]{2,1,0:T(8,128)S(1)} %shard_map.52, bf16[16,256,256]{2,1,0:T(8,128)(2,1)} %collective-permute-done.14), kind=kLoop, calls=%fused_computation | loop fusion | flops 3145728 | bytes 8388608 | tf_op jit(solution)/shard_map/convert_element_type | solution.py:228
  214.0 5.5 %all-to-all-start.10 = ((bf16[16,256,256]{2,1,0:T(8,128)(2,1)}), bf16[16,256,256]{2,1,0:T(8,128)(2,1)S(1)}, u32[]{:S(2)}, u32[]{:S(2)}) async-start(bf16[16,256,256]{2,1,0:T(8,128)(2,1)} %add_convert_fusion), calls=%async_computation.10 | async-start | bytes 4194304 | tf_op jit(solution)/shard_map/all_to_all | solution.py:229
  221.3 31.4 %all-to-all-done.10 = bf16[16,256,256]{2,1,0:T(8,128)(2,1)S(1)} async-done(((bf16[16,256,256]{2,1,0:T(8,128)(2,1)}), bf16[16,256,256]{2,1,0:T(8,128)(2,1)S(1)}, u32[]{:S(2)}, u32[]{:S(2)}) %all-to-all-start.10) | async-done | bytes 2097184 | tf_op jit(solution)/shard_map/all_to_all | solution.py:229
  (137 shorter events, 29.8 us)
Async XLA Ops:
  1.7 4.7 %collective-permute-start.5 = (bf16[256,512]{1,0:T(8,128)(2,1)S(1)}, bf16[256,512]{1,0:T(8,128)(2,1)S(1)}, u32[]{:S(2)}, u32[]{:S(2)}) collective-permute-start(bf16[256,512]{1,0:T(8,128)(2,1)S(1)} %get-tuple-element.18), channel_id=1, source_target_pairs={{0,16},{1,17},{2,18},{3,19},{4,20},{5,21},{6,22},{7,23},{8,24},{9,... | collective-permute-start | bytes 786440 | tf_op jit(solution)/shard_map/ppermute | solution.py:45
  1.8 15.5 %all-to-all-start = ((bf16[4,256,256]{2,1,0:T(8,128)(2,1)}), bf16[4,256,256]{2,1,0:T(8,128)(2,1)S(1)}, u32[]{:S(2)}, u32[]{:S(2)}) async-start(bf16[4,256,256]{2,1,0:T(8,128)(2,1)} %bitcast.84), calls=%async_computation | async-start | bytes 1048576 | tf_op jit(solution)/shard_map/all_to_all | solution.py:192
  6.5 14.0 %collective-permute-start.6 = (bf16[256,1024]{1,0:T(8,128)(2,1)S(1)}, bf16[256,1024]{1,0:T(8,128)(2,1)S(1)}, u32[]{:S(2)}, u32[]{:S(2)}) collective-permute-start(bf16[256,1024]{1,0:T(8,128)(2,1)S(1)} %maximum_select_fusion.1), channel_id=1, source_target_pairs={{0,96},{1,97},{2,98},{3,99},{4,100},{5,101},{6,102},{7,103},{8,104... | collective-permute-start | bytes 1572872 | tf_op jit(solution)/shard_map/ppermute | solution.py:45
  10.6 14.0 %collective-permute-start.7 = (bf16[256,1024]{1,0:T(8,128)(2,1)S(1)}, bf16[256,1024]{1,0:T(8,128)(2,1)S(1)}, u32[]{:S(2)}, u32[]{:S(2)}) collective-permute-start(bf16[256,1024]{1,0:T(8,128)(2,1)S(1)} %maximum_select_fusion.1), channel_id=1, source_target_pairs={{0,32},{1,33},{2,34},{3,35},{4,36},{5,37},{6,38},{7,39},{8,40},{9,... | collective-permute-start | bytes 1572872 | tf_op jit(solution)/shard_map/ppermute | solution.py:45
  17.3 13.7 %collective-permute-start.1 = (bf16[4,256,256]{2,1,0:T(8,128)(2,1)S(1)}, bf16[4,256,256]{2,1,0:T(8,128)(2,1)S(1)}, u32[]{:S(2)}, u32[]{:S(2)}) collective-permute-start(bf16[4,256,256]{2,1,0:T(8,128)(2,1)S(1)} %all-to-all-done), channel_id=1, source_target_pairs={{0,1},{1,2},{2,3},{3,0},{4,5},{5,6},{6,7},{7,4},{8,9},{9,10},{10,1... | collective-permute-start | bytes 1572872 | tf_op jit(solution)/shard_map/ppermute | solution.py:45
  18.8 12.6 %collective-permute-start = (bf16[4,256,256]{2,1,0:T(8,128)(2,1)S(1)}, bf16[4,256,256]{2,1,0:T(8,128)(2,1)S(1)}, u32[]{:S(2)}, u32[]{:S(2)}) collective-permute-start(bf16[4,256,256]{2,1,0:T(8,128)(2,1)S(1)} %all-to-all-done), channel_id=1, source_target_pairs={{0,3},{1,0},{2,1},{3,2},{4,7},{5,4},{6,5},{7,6},{8,11},{9,8},{10,9... | collective-permute-start | bytes 1572872 | tf_op jit(solution)/shard_map/ppermute | solution.py:45
  20.5 13.9 %collective-permute-start.9 = (bf16[128,1024]{1,0:T(8,128)(2,1)S(1)}, bf16[128,1024]{1,0:T(8,128)(2,1)S(1)}, u32[]{:S(2)}, u32[]{:S(2)}) collective-permute-start(bf16[128,1024]{1,0:T(8,128)(2,1)S(1)} %slice.27), channel_id=1, source_target_pairs={{0,96},{1,97},{2,98},{3,99},{4,100},{5,101},{6,102},{7,103},{8,104... | collective-permute-start | bytes 786440 | tf_op jit(solution)/shard_map/ppermute | solution.py:45
  24.7 0.8 copy-start.9
  24.7 9.7 %collective-permute-start.8 = (bf16[128,1024]{1,0:T(8,128)(2,1)S(1)}, bf16[128,1024]{1,0:T(8,128)(2,1)S(1)}, u32[]{:S(2)}, u32[]{:S(2)}) collective-permute-start(bf16[128,1024]{1,0:T(8,128)(2,1)S(1)} %slice.26), channel_id=1, source_target_pairs={{0,32},{1,33},{2,34},{3,35},{4,36},{5,37},{6,38},{7,39},{8,40},{9,... | collective-permute-start | bytes 786440 | tf_op jit(solution)/shard_map/ppermute | solution.py:45
  25.6 8.9 %copy-start.10 = (bf16[256,1024]{1,0:T(8,128)(2,1)S(1)}, bf16[256,1024]{1,0:T(8,128)(2,1)}, u32[]{:S(2)}) copy-start(bf16[256,1024]{1,0:T(8,128)(2,1)} %copy-done.9) | copy-start | bytes 1572868
  31.0 8.4 %collective-permute-start.2 = (bf16[2,256,256]{2,1,0:T(8,128)(2,1)S(1)}, bf16[2,256,256]{2,1,0:T(8,128)(2,1)S(1)}, u32[]{:S(2)}, u32[]{:S(2)}) collective-permute-start(bf16[2,256,256]{2,1,0:T(8,128)(2,1)S(1)} %slice.24), channel_id=1, source_target_pairs={{0,1},{1,2},{2,3},{3,0},{4,5},{5,6},{6,7},{7,4},{8,9},{9,10},{10,1... | collective-permute-start | bytes 786440 | tf_op jit(solution)/shard_map/ppermute | solution.py:45
  31.4 8.1 %collective-permute-start.3 = (bf16[2,256,256]{2,1,0:T(8,128)(2,1)S(1)}, bf16[2,256,256]{2,1,0:T(8,128)(2,1)S(1)}, u32[]{:S(2)}, u32[]{:S(2)}) collective-permute-start(bf16[2,256,256]{2,1,0:T(8,128)(2,1)S(1)} %slice.25), channel_id=1, source_target_pairs={{0,3},{1,0},{2,1},{3,2},{4,7},{5,4},{6,5},{7,6},{8,11},{9,8},{10,9... | collective-permute-start | bytes 786440 | tf_op jit(solution)/shard_map/ppermute | solution.py:45
  36.1 27.5 %collective-permute-start.10 = (bf16[4,256,1024]{2,1,0:T(8,128)(2,1)}, bf16[4,256,1024]{2,1,0:T(8,128)(2,1)S(1)}, u32[]{:S(2)}, u32[]{:S(2)}) collective-permute-start(bf16[4,256,1024]{2,1,0:T(8,128)(2,1)} %pad_maximum_fusion.refs_0_), channel_id=1, source_target_pairs={{0,4},{1,5},{2,6},{3,7},{4,8},{5,9},{6,10},{7,11},{8,12},{9,13},{1... | collective-permute-start | bytes 6291464 | tf_op jit(solution)/shard_map/ppermute | solution.py:45
  36.7 29.2 %collective-permute-start.12 = (bf16[4,256,1024]{2,1,0:T(8,128)(2,1)}, bf16[4,256,1024]{2,1,0:T(8,128)(2,1)}, u32[]{:S(2)}, u32[]{:S(2)}) collective-permute-start(bf16[4,256,1024]{2,1,0:T(8,128)(2,1)} %pad_maximum_fusion.refs_0_), channel_id=1, source_target_pairs={{0,12},{1,13},{2,14},{3,15},{4,0},{5,1},{6,2},{7,3},{8,4},{9,5},{1... | collective-permute-start | bytes 6291464 | tf_op jit(solution)/shard_map/ppermute | solution.py:45
  39.5 31.1 %copy-start = (bf16[16,256,256]{2,1,0:T(8,128)(2,1)}, bf16[16,256,256]{2,1,0:T(8,128)(2,1)S(1)}, u32[]{:S(2)}) copy-start(bf16[16,256,256]{2,1,0:T(8,128)(2,1)S(1)} %constant_dynamic-update-slice_fusion.own) | copy-start | bytes 6291460
  39.5 31.6 %collective-permute-start.4 = (bf16[16,256,256]{2,1,0:T(8,128)(2,1)S(1)}, bf16[16,256,256]{2,1,0:T(8,128)(2,1)}, u32[]{:S(2)}, u32[]{:S(2)}) collective-permute-start(bf16[16,256,256]{2,1,0:T(8,128)(2,1)S(1)} %constant_dynamic-update-slice_fusion.own), channel_id=1, source_target_pairs={{0,16},{1,17},{2,18},{3,19},{4,20},{5,21},{6,22},{7,23},{8,24},{9,... | collective-permute-start | bytes 6291464 | tf_op jit(solution)/shard_map/ppermute | solution.py:45
  64.6 1.3 copy-start.5
  65.9 20.5 %collective-permute-start.11 = (bf16[2,256,1024]{2,1,0:T(8,128)(2,1)}, bf16[2,256,1024]{2,1,0:T(8,128)(2,1)}, u32[]{:S(2)}, u32[]{:S(2)}) collective-permute-start(bf16[2,256,1024]{2,1,0:T(8,128)(2,1)} %slice.28), channel_id=1, source_target_pairs={{0,4},{1,5},{2,6},{3,7},{4,8},{5,9},{6,10},{7,11},{8,12},{9,13},{1... | collective-permute-start | bytes 3145736 | tf_op jit(solution)/shard_map/ppermute | solution.py:45
  67.2 20.5 %collective-permute-start.13 = (bf16[2,256,1024]{2,1,0:T(8,128)(2,1)S(1)}, bf16[2,256,1024]{2,1,0:T(8,128)(2,1)S(1)}, u32[]{:S(2)}, u32[]{:S(2)}) collective-permute-start(bf16[2,256,1024]{2,1,0:T(8,128)(2,1)S(1)} %slice.29), channel_id=1, source_target_pairs={{0,12},{1,13},{2,14},{3,15},{4,0},{5,1},{6,2},{7,3},{8,4},{9,5},{1... | collective-permute-start | bytes 3145736 | tf_op jit(solution)/shard_map/ppermute | solution.py:45
  71.1 1.6 copy-start.1
  77.9 2.3 copy-start.6
  87.8 4.7 %copy-start.2 = (bf16[4,256,1024]{2,1,0:T(8,128)(2,1)}, bf16[4,256,1024]{2,1,0:T(8,128)(2,1)S(1)}, u32[]{:S(2)}) copy-start(bf16[4,256,1024]{2,1,0:T(8,128)(2,1)S(1)} %constant_dynamic-update-slice_fusion.5.refs_0_.refs_2_) | copy-start | bytes 6291460
  189.7 1.6 copy-start.3
  189.7 2.2 copy-start.7
  191.9 11.2 %copy-start.4 = (bf16[4,256,1024]{2,1,0:T(8,128)(2,1)S(1)}, bf16[4,256,1024]{2,1,0:T(8,128)(2,1)}, u32[]{:S(2)}) copy-start(bf16[4,256,1024]{2,1,0:T(8,128)(2,1)} %copy-done.2) | copy-start | bytes 6291460
  199.1 11.4 %collective-permute-start.14 = (bf16[16,256,256]{2,1,0:T(8,128)(2,1)}, bf16[16,256,256]{2,1,0:T(8,128)(2,1)}, u32[]{:S(2)}, u32[]{:S(2)}) collective-permute-start(bf16[16,256,256]{2,1,0:T(8,128)(2,1)} %shard_map.53), channel_id=1, source_target_pairs={{0,16},{1,17},{2,18},{3,19},{4,20},{5,21},{6,22},{7,23},{8,24},{9,... | collective-permute-start | bytes 6291464 | tf_op jit(solution)/shard_map/ppermute | solution.py:45
  199.8 14.2 %all-to-all-start.11 = ((f32[4,1,256]{2,1,0:T(1,128)}), f32[4,1,256]{2,1,0:T(1,128)S(1)}, u32[]{:S(2)}, u32[]{:S(2)}) async-start(f32[4,1,256]{2,1,0:T(1,128)} %broadcast_in_dim.29), calls=%async_computation.11 | async-start | bytes 8192 | tf_op jit(solution)/shard_map/all_to_all | solution.py:50
  203.1 1.6 copy-start.8
  214.0 38.7 %all-to-all-start.10 = ((bf16[16,256,256]{2,1,0:T(8,128)(2,1)}), bf16[16,256,256]{2,1,0:T(8,128)(2,1)S(1)}, u32[]{:S(2)}, u32[]{:S(2)}) async-start(bf16[16,256,256]{2,1,0:T(8,128)(2,1)} %add_convert_fusion), calls=%async_computation.10 | async-start | bytes 4194304 | tf_op jit(solution)/shard_map/all_to_all | solution.py:229
  219.6 1.2 collective-permute-start.15

commit v3 on v1

v3 whole, which is shorter than its diff:
```python
import functools

import jax
import jax.numpy as jnp
from jax import lax
from jax.experimental import pallas as pl
from jax.experimental.pallas import tpu as pltpu
from jax.sharding import PartitionSpec as P

D = 4096
ITERS = 4
COUNT = 8192
EPS = 0.02

AXES = ("row", "col")
PLACES = [(z, c, y, x) for z in range(4) for c in range(2) for y in range(4) for x in range(4)]


def flat(z, c, y, x):
    return ((z % 4 * 2 + c % 2) * 4 + y % 4) * 4 + x % 4


def pairs(move):
    return [(flat(*p), flat(*move(*p))) for p in PLACES]


def groups(shared):
    found = {}
    for p in PLACES:
        key = tuple(v for v, name in zip(p, "zcyx") if name in shared)
        found.setdefault(key, []).append(flat(*p))
    return list(found.values())


OTHER = pairs(lambda z, c, y, x: (z, c + 1, y, x))
FIRST_UP = pairs(lambda z, c, y, x: (z + 1 - c, c, y + c, x))
FIRST_DOWN = pairs(lambda z, c, y, x: (z - 1 + c, c, y - c, x))
FIRST_TWO = pairs(lambda z, c, y, x: (z + 2 - 2 * c, c, y + 2 * c, x))
SECOND_UP = pairs(lambda z, c, y, x: (z + c, c, y + 1 - c, x))
SECOND_DOWN = pairs(lambda z, c, y, x: (z - c, c, y - 1 + c, x))


def send(values, where):
    return lax.ppermute(values, AXES, where)


def spread(values, size, shared):
    copies = jnp.broadcast_to(values[None, None, :], (size, 1, values.shape[0]))
    return lax.all_to_all(
        copies, AXES, 0, 0, tiled=True, axis_index_groups=groups(shared)
    )[:, 0, :]


def lse(scores, axis):
    peak = jnp.max(scores, axis=axis, keepdims=True)
    total = jnp.sum(jnp.exp(scores - peak), axis=axis)
    return jnp.squeeze(peak, axis) + jnp.log(total)


def place_of(place, piece):
    z, c, y = place[0], place[1], place[2]
    first, second = piece
    far_z = jnp.where(c == 0, first, second)
    far_y = jnp.where(c == 0, second, first)
    return lax.rem(y + far_y, 4), lax.rem(z + far_z, 4)


HIGHEST = lax.Precision.HIGHEST
BLOCKS = 8


def gram_kernel(pieces, sides, first_call, last_call, place, *refs):
    count = len(pieces)
    sources, held = refs[: len(sides)], refs[len(sides) : len(sides) + count]
    outs, state_in = refs[-3:], refs[-6:-3]
    c = place[1]
    halves = [pl.ds(pl.multiple_of(k, 256), 256) for k in (c * 256, 256 - c * 256)]
    gram, squares, noise_squares = outs
    if first_call:
        gram[...] = jnp.zeros_like(gram)
        squares[...] = jnp.zeros_like(squares)
        noise_squares[...] = jnp.zeros_like(noise_squares)
    else:
        for k in range(3):
            outs[k][...] = state_in[k][...]
    if not last_call:
        total = jnp.zeros((256, 128), jnp.float32)
        for k in range(16):
            wide = sources[0][k].astype(jnp.float32)
            wide = wide * wide
            total = total + wide[:, :128] + wide[:, 128:]
        noise_squares[halves[sides[0]], :] = total
    for k, pair in enumerate(pieces):
        for side, where in enumerate(pair):
            row_group, col_group = place_of(place, where)
            rows = pl.ds(pl.multiple_of(row_group * 256, 256), 256)
            sums = [None] * len(sides)
            total = None
            for part in range(4):
                values = held[k][side * 256 : side * 256 + 256, part * 256 : part * 256 + 256]
                for n in range(len(sides)):
                    term = lax.dot_general(
                        sources[n][part * 4 + col_group],
                        values,
                        (((1,), (1,)), ((), ())),
                        preferred_element_type=jnp.float32,
                    )
                    sums[n] = term if part == 0 else sums[n] + term
                if sides[0] == 0:
                    wide = values.astype(jnp.float32)
                    wide = wide * wide
                    folded = wide[:, :128] + wide[:, 128:]
                    total = folded if part == 0 else total + folded
            if sides[0] == 0:
                squares[rows, :] += total
            for n, half in enumerate(sides):
                gram[halves[half], rows] += sums[n]
    if last_call:
        data_sq = lax.dot_general(
            jnp.ones((8, 128), jnp.float32),
            squares[...],
            (((1,), (1,)), ((), ())),
            precision=HIGHEST,
            preferred_element_type=jnp.float32,
        )[0:1, :]
        noise_sq = jnp.sum(noise_squares[...], axis=1, keepdims=True)
        gram[...] = (2.0 * gram[...] - noise_sq - data_sq) * (1.0 / (D * EPS))


def gram_of(place, sources, sides, arrays, pieces, before, last_call):
    outs = [(512, 1024), (1024, 128), (512, 128)]
    count = len(arrays)
    operands = [*sources, *arrays, *(before or [])]
    vmem = pl.BlockSpec(memory_space=pltpu.VMEM)
    aliases = {} if before is None else {len(operands) - 2 + k: k for k in range(3)}
    return pl.pallas_call(
        functools.partial(gram_kernel, pieces, sides, before is None, last_call),
        out_shape=[jax.ShapeDtypeStruct(shape, jnp.float32) for shape in outs],
        in_specs=[pl.BlockSpec(memory_space=pltpu.SMEM)] + [vmem] * len(operands),
        out_specs=[vmem] * 3,
        input_output_aliases=aliases,
        compiler_params=pltpu.CompilerParams(vmem_limit_bytes=28 * 2**20),
        cost_estimate=pl.CostEstimate(
            flops=count * len(sides) * 2 * 512 * 256 * 1024,
            bytes_accessed=count * 2**20 + 8 * 2**20,
            transcendentals=0,
        ),
    )(place, *operands)


def mix_kernel(pieces, away, place, weights, *refs):
    held, out, buffer, sems = refs[:BLOCKS], refs[-3], refs[-2], refs[-1]
    copies = []
    for k, pair in enumerate(pieces):
        for side, where in enumerate(pair):
            row_group, col_group = place_of(place, where)
            rows = pl.ds(pl.multiple_of(row_group * 256, 256), 256)
            columns = pl.ds(pl.multiple_of(col_group * 1024, 1024), 1024)
            copies.append(
                pltpu.make_async_copy(
                    held[k].at[pl.ds(side * 256, 256)], buffer.at[rows, columns], sems.at[2 * k + side]
                )
            )
    for copy in copies:
        copy.start()
    half = place[1] if not away else 1 - place[1]
    left = weights[pl.ds(pl.multiple_of(half * 256, 256), 256), :]
    for copy in copies:
        copy.wait()
    for n in range(16):
        total = jnp.dot(left, buffer[:, n * 256 : n * 256 + 256], preferred_element_type=jnp.float32)
        if not away:
            total = total + refs[BLOCKS][n].astype(jnp.float32)
        out[n] = total.astype(out.dtype)


def mix(place, weights, arrays, pieces, came):
    vmem = pl.BlockSpec(memory_space=pltpu.VMEM)
    operands = [weights, *arrays, *([] if came is None else [came])]
    return pl.pallas_call(
        functools.partial(mix_kernel, pieces, came is None),
        out_shape=jax.ShapeDtypeStruct((16, 256, 256), jnp.bfloat16),
        in_specs=[pl.BlockSpec(memory_space=pltpu.SMEM), vmem]
        + [pl.BlockSpec(memory_space=pl.ANY)] * BLOCKS
        + [vmem] * (came is not None),
        out_specs=vmem,
        scratch_shapes=[
            pltpu.VMEM((1024, 4096), jnp.bfloat16),
            pltpu.SemaphoreType.DMA((2 * BLOCKS,)),
        ],
        compiler_params=pltpu.CompilerParams(vmem_limit_bytes=32 * 2**20),
        cost_estimate=pl.CostEstimate(
            flops=2 * 256 * 1024 * 4096, bytes_accessed=14 * 2**20, transcendentals=0
        ),
    )(place, *operands)


def local(noise, data):
    row, col = lax.axis_index("row"), lax.axis_index("col")
    z, c, y, x = row // 2, row % 2, col // 4, col % 4
    place = jnp.stack([z, c, y, x]).astype(jnp.int32)

    halves = data.reshape(2, 256, 512)
    kept = lax.dynamic_index_in_dim(halves, c, 0, keepdims=False)
    came = send(lax.dynamic_index_in_dim(halves, 1 - c, 0, keepdims=False), OTHER)
    block = jnp.where(
        c == 0, jnp.concatenate([kept, came], 1), jnp.concatenate([came, kept], 1)
    )
    below, above, far = lax.optimization_barrier(
        (send(block, FIRST_UP), send(block, FIRST_DOWN), send(block, FIRST_TWO))
    )
    own = lax.all_to_all(
        noise.reshape(4, 256, 256), AXES, 0, 0, tiled=True, axis_index_groups=groups("zcx")
    )
    own = lax.all_to_all(
        jnp.broadcast_to(own[None], (4, 4, 256, 256)).reshape(4, 1024, 256),
        AXES,
        0,
        0,
        tiled=True,
        axis_index_groups=groups("zcy"),
    ).reshape(16, 256, 256)
    one, two = jnp.concatenate([block, below]), jnp.concatenate([above, far])
    one_below, two_above = send(one, SECOND_UP), send(two, SECOND_DOWN)
    one_above, two_below = send(one, SECOND_DOWN), send(two, SECOND_UP)
    one_below, two_above, one_above, two_below, own = lax.optimization_barrier(
        (one_below, two_above, one_above, two_below, own)
    )
    other = send(own, OTHER)
    one_far, two_far = send(one_below, SECOND_UP), send(two_above, SECOND_DOWN)

    arrays = [one, two, one_above, two_below, one_below, two_above, one_far, two_far]
    pieces = [
        [(first, second) for first in ((0, 3), (1, 2))[k % 2]] for k, second in enumerate((0, 0, 1, 3, 3, 1, 2, 2))
    ]
    state = gram_of(place, [own], (0,), arrays[:6], pieces[:6], None, False)
    state = gram_of(place, [other], (1,), arrays[:6], pieces[:6], state, False)
    scores = gram_of(place, [own, other], (0, 1), arrays[6:], pieces[6:], state, True)[0]

    def row_exchange(g, extra):
        mine = lse(scores + g[None, :], 1)
        shared = spread(jnp.concatenate([mine, extra]), 8, "zy")
        return lse(shared[:, :512], 0), shared[:, 512:]

    def col_exchange(f, extra):
        mine = lse(scores + f[:, None], 0)
        shared = spread(jnp.concatenate([mine, extra]), 16, "cx")
        return lse(shared[:, :1024], 0), shared[:, 1024:]

    log_count = jnp.log(float(COUNT))
    nothing = jnp.zeros((0,), jnp.float32)
    g = jnp.zeros((1024,), jnp.float32)
    for step in range(ITERS):
        f = -log_count - row_exchange(g, nothing)[0]
        total, all_f = col_exchange(f, nothing if step < ITERS - 1 else f)
        g = -log_count - total
    norm, all_g = row_exchange(g, lax.dynamic_slice(g, (y * 256,), (256,)))
    weights = jnp.exp(scores + g[None, :] - norm[:, None]).astype(jnp.bfloat16)
    away = mix(place, weights, arrays, pieces, None)
    shares = mix(place, weights, arrays, pieces, send(away, OTHER))
    noise_potential = EPS * lax.dynamic_slice(all_f, (z * 4, c * 256), (4, 256)).reshape(1024)
    data_potential = EPS * lax.dynamic_index_in_dim(
        all_g.reshape(2, 4, 256), x, 1, keepdims=False
    ).reshape(512)
    shares, noise_potential, data_potential = lax.optimization_barrier(
        (shares, noise_potential, data_potential)
    )
    shares = lax.all_to_all(shares, "col", 0, 0, tiled=True)
    targets = jnp.sum(shares.reshape(4, 4, 256, 256).astype(jnp.float32), axis=1)
    targets = targets.reshape(1024, 256).astype(jnp.bfloat16)

    return (targets, noise_potential, data_potential)


def solution(mesh):
    placed = (P("row", "col"), P("col", "row"))
    return jax.shard_map(
        local,
        mesh=mesh,
        in_specs=placed,
        out_specs=(P("row", "col"), P("row"), P("col")),
        check_vma=False,
    )
```

time: 361 us -> 229 us (0.63)
  waiting for transfers between devices: 221 us -> 38.7 us
  Pallas kernels: 0 us -> 29.7 us
  starting transfers between devices: 0.11 us -> 29.2 us
  blocking collectives: 88.4 us -> 107 us
  matrix products: 17.6 us -> 0 us
  between operations: 14.1 us -> 1.2 us
  local copies, waits for them, and re-layouts: 0.79 us -> 12.3 us
  other arithmetic: 18.1 us -> 9.43 us
    all_gather x2 -> x0, waiting for transfers between devices: 113 us -> none  [the longest x1 77.1 us: local(): noise_whole = lax.all_gather(noise, 'col', axis=1, tiled=True)]
    reduce_scatter x1 -> x0, waiting for transfers between devices: 106 us -> none  [local(): lax.psum_scatter(partial_targets, 'col', scatter_dimension=1, tiled=True)]
    pallas_call x0 -> x5, Pallas kernels: none -> 29.7 us  [the longest x3 16.1 us: gram_of(): pl.pallas_call(functools.partial(gram_kernel, pieces, sides, before is No...]
    ppermute x0 -> x12, waiting for transfers between devices: none -> 26.1 us  [send(): return lax.ppermute(values, AXES, where)]
    all_to_all x9, blocking collectives: 88.4 us -> 107 us  [the longest x8 75.6 us: spread(): lax.all_to_all(copies, AXES, 0, 0, tiled=True, axis_index_groups=groups(s...]
    dot_general x2 -> x0, matrix products: 17.6 us -> none  [the longest x1 10.4 us: local(): jnp.dot(weights, data_whole, preferred_element_type=jnp.float32)]
    ppermute x0 -> x12, starting transfers between devices: none -> 16.7 us  [send(): return lax.ppermute(values, AXES, where)]
    all_to_all x0 -> x3, waiting for transfers between devices: none -> 12.6 us  [the longest x1 7.77 us: spread(): lax.all_to_all(copies, AXES, 0, 0, tiled=True, axis_index_groups=groups(s...]
  transfers between devices with their start and end apart: 3 -> 15, of which waited for: 3 -> 7; matrix products, arithmetic and copies ran while one was open for 1% -> 1% of each run, Pallas kernels for 0% -> 5%
where the time goes in v3:
time: 229 us; the launch traced here: 228 us
  blocking collectives  107 us (47%)
  waiting for transfers between devices  38.7 us (17%)
  Pallas kernels  29.7 us (13%)
  starting transfers between devices  29.2 us (13%)
  local copies, waits for them, and re-layouts  12.3 us (5%)
  other arithmetic  9.43 us (4%)
    all_to_all x8, blocking collectives, spread(): lax.all_to_all(copies, AXES, 0, 0, tiled=True, axis_index_groups=groups(s...  75.6 us
    all_to_all x1, blocking collectives, local(): shares = lax.all_to_all(shares, 'col', 0, 0, tiled=True)  31.8 us
    ppermute x12, waiting for transfers between devices, send(): return lax.ppermute(values, AXES, where)  26.1 us
    ppermute x12, starting transfers between devices, send(): return lax.ppermute(values, AXES, where)  16.7 us
    pallas_call x3, Pallas kernels, gram_of(): pl.pallas_call(functools.partial(gram_kernel, pieces, sides, before is No...  16.1 us
    pallas_call x2, Pallas kernels, mix(): pl.pallas_call(functools.partial(mix_kernel, pieces, came is None), out_s...  13.6 us
    unnamed x36, local copies, waits for them, and re-layouts  8.76 us
    all_to_all x1, waiting for transfers between devices, spread(): lax.all_to_all(copies, AXES, 0, 0, tiled=True, axis_index_groups=groups(s...  7.77 us
  transfers between devices with their start and end apart: 15, of which 7 were waited for; matrix products, arithmetic and copies ran while one was open for 1% of the time, Pallas kernels for 5%

profile of v3, /device:TPU:0, one launch (start us, length us, event | category | flops | bytes accessed | tf_op | source)
XLA Modules:
  0.0 227.9 jit_solution(3939907733135437119)
XLA Ops:
  1.8 4.6 %all-to-all-start = ((bf16[4,256,256]{2,1,0:T(8,128)(2,1)}), bf16[4,256,256]{2,1,0:T(8,128)(2,1)S(1)}, u32[]{:S(2)}, u32[]{:S(2)}) async-start(bf16[4,256,256]{2,1,0:T(8,128)(2,1)} %bitcast.73), calls=%async_computation | async-start | bytes 1048576 | tf_op jit(solution)/shard_map/all_to_all | solution.py:212
  6.5 4.0 %collective-permute-start.3 = (bf16[256,1024]{1,0:T(8,128)(2,1)S(1)}, bf16[256,1024]{1,0:T(8,128)(2,1)S(1)}, u32[]{:S(2)}, u32[]{:S(2)}) collective-permute-start(bf16[256,1024]{1,0:T(8,128)(2,1)S(1)} %maximum_select_fusion), channel_id=1, source_target_pairs={{0,64},{1,65},{2,66},{3,67},{4,68},{5,69},{6,70},{7,71},{8,72},{9,... | collective-permute-start | bytes 1572872 | tf_op jit(solution)/shard_map/ppermute | solution.py:44
  11.2 1.3 collective-permute-start.1
  12.5 4.8 %all-to-all-done = bf16[4,256,256]{2,1,0:T(8,128)(2,1)S(1)} async-done(((bf16[4,256,256]{2,1,0:T(8,128)(2,1)}), bf16[4,256,256]{2,1,0:T(8,128)(2,1)S(1)}, u32[]{:S(2)}, u32[]{:S(2)}) %all-to-all-start) | async-done | bytes 524320 | tf_op jit(solution)/shard_map/all_to_all | solution.py:212
  17.3 1.4 broadcast_in_dim.23
  18.8 4.4 %all-to-all-start.1 = ((bf16[4,1024,256]{2,1,0:T(8,128)(2,1)}), bf16[4,1024,256]{2,1,0:T(8,128)(2,1)}, u32[]{:S(2)}, u32[]{:S(2)}) async-start(bf16[4,1024,256]{2,1,0:T(8,128)(2,1)} %broadcast_in_dim.23), calls=%async_computation.1 | async-start | bytes 4194304 | tf_op jit(solution)/shard_map/all_to_all | solution.py:215
  24.4 2.1 collective-permute-start.7
  26.5 1.3 collective-permute-start.5
  27.9 2.0 collective-permute-start.6
  30.0 10.5 %collective-permute-done.7.refs_4_.refs_3_ = bf16[512,1024]{1,0:T(8,128)(2,1)S(1)} collective-permute-done((bf16[512,1024]{1,0:T(8,128)(2,1)S(1)}, bf16[512,1024]{1,0:T(8,128)(2,1)S(1)}, u32[]{:S(2)}, u32[]{:S(2)}) %collective-permute-start.7) | collective-permute-done | bytes 1048608 | tf_op jit(solution)/shard_map/ppermute | solution.py:44
  41.7 11.1 %collective-permute-done.6.refs_3_.refs_2_ = bf16[512,1024]{1,0:T(8,128)(2,1)S(1)} collective-permute-done((bf16[512,1024]{1,0:T(8,128)(2,1)S(1)}, bf16[512,1024]{1,0:T(8,128)(2,1)S(1)}, u32[]{:S(2)}, u32[]{:S(2)}) %collective-permute-start.6) | collective-permute-done | bytes 1048608 | tf_op jit(solution)/shard_map/ppermute | solution.py:44
  53.8 1.7 collective-permute-start.8
  55.9 2.8 %collective-permute-start.10 = (bf16[512,1024]{1,0:T(8,128)(2,1)}, bf16[512,1024]{1,0:T(8,128)(2,1)}, u32[]{:S(2)}, u32[]{:S(2)}) collective-permute-start(bf16[512,1024]{1,0:T(8,128)(2,1)} %collective-permute-done.5.refs_6_.refs_5_), channel_id=1, source_target_pairs={{0,12},{1,13},{2,14},{3,15},{4,0},{5,1},{6,2},{7,3},{8,4},{9,5},{1... | collective-permute-start | bytes 3145736 | tf_op jit(solution)/shard_map/ppermute | solution.py:44
  58.8 1.2 copy-done.1
  62.5 5.5 %shard_map.49 = (f32[512,1024]{1,0:T(8,128)S(1)}, f32[1024,128]{1,0:T(8,128)S(1)}, f32[512,128]{1,0:T(8,128)S(1)}) custom-call(s32[4]{0:T(128)S(1)} %pad_add_fusion.place, bf16[16,256,256]{2,1,0:T(8,128)(2,1)} %bitcast.9.refs_0_, bf16[512,1024]{1,0:T(8,128)(2,1)S(1)} %pad_maximum_fusion.refs_1_.refs_0_, bf16[512,1024]{1,0:T(8,128)(2,1)S(1)} %copy-done.1, ...), custom_call_target="tpu_custom_call" | custom-call | flops 1610612736 | bytes 14680064 | tf_op jit(solution)/shard_map/pallas_call | solution.py:136
  68.1 5.1 %shard_map.50 = (f32[512,1024]{1,0:T(8,128)S(1)}, f32[1024,128]{1,0:T(8,128)S(1)}, f32[512,128]{1,0:T(8,128)S(1)}) custom-call(s32[4]{0:T(128)S(1)} %pad_add_fusion.place, bf16[16,256,256]{2,1,0:T(8,128)(2,1)} %collective-permute-done.8.refs_0_.refs_1_, ...), custom_call_target="tpu_custom_call", output_to_operand_aliasing={{0}: (8, {}), {1}: (9, {}), {2}: (10, {})} | custom-call | flops 1610612736 | bytes 14680064 | tf_op jit(solution)/shard_map/pallas_call | solution.py:136
  73.2 5.5 %shard_map.51 = (f32[512,1024]{1,0:T(8,128)S(1)}, f32[1024,128]{1,0:T(8,128)S(1)}, f32[512,128]{1,0:T(8,128)S(1)}) custom-call(s32[4]{0:T(128)S(1)} %pad_add_fusion.place, bf16[16,256,256]{2,1,0:T(8,128)(2,1)} %bitcast.9.refs_0_, ...), custom_call_target="tpu_custom_call", output_to_operand_aliasing={{0}: (5, {}), {1}: (6, {}), {2}: (7, {})} | custom-call | flops 1073741824 | bytes 10485760 | tf_op jit(solution)/shard_map/pallas_call | solution.py:136
  79.4 9.5 %all_to_all.60 = f32[8,1,512]{2,1,0:T(1,128)S(1)} all-to-all(f32[8,1,512]{2,1,0:T(1,128)S(1)} %broadcast_in_dim.24), channel_id=1, replica_groups={{0,1,2,3,16,17,18,19},{4,5,6,7,20,21,22,23},{8,9,10,11,24,25,26,27},{12..., dimensions={0} | all-to-all | bytes 32768 | tf_op jit(solution)/shard_map/all_to_all | solution.py:49
  89.7 13.6 %all_to_all.61 = f32[16,1,1024]{2,1,0:T(1,128)S(1)} all-to-all(f32[16,1,1024]{2,1,0:T(1,128)S(1)} %broadcast_in_dim.25), channel_id=1, replica_groups={{0,4,8,12,32,36,40,44,64,68,72,76,96,100,104,108},{1,5,9,13,33,37,41,45..., dimensions={0} | all-to-all | bytes 131072 | tf_op jit(solution)/shard_map/all_to_all | solution.py:49
  104.2 7.6 %all_to_all.62 = f32[8,1,512]{2,1,0:T(1,128)S(1)} all-to-all(f32[8,1,512]{2,1,0:T(1,128)S(1)} %broadcast_in_dim.26), channel_id=1, replica_groups={{0,1,2,3,16,17,18,19},{4,5,6,7,20,21,22,23},{8,9,10,11,24,25,26,27},{12..., dimensions={0} | all-to-all | bytes 32768 | tf_op jit(solution)/shard_map/all_to_all | solution.py:49
  112.7 10.8 %all_to_all.63 = f32[16,1,1024]{2,1,0:T(1,128)S(1)} all-to-all(f32[16,1,1024]{2,1,0:T(1,128)S(1)} %broadcast_in_dim.27), channel_id=1, replica_groups={{0,4,8,12,32,36,40,44,64,68,72,76,96,100,104,108},{1,5,9,13,33,37,41,45..., dimensions={0} | all-to-all | bytes 131072 | tf_op jit(solution)/shard_map/all_to_all | solution.py:49
  124.4 7.6 %all_to_all.64 = f32[8,1,512]{2,1,0:T(1,128)S(1)} all-to-all(f32[8,1,512]{2,1,0:T(1,128)S(1)} %broadcast_in_dim.28), channel_id=1, replica_groups={{0,1,2,3,16,17,18,19},{4,5,6,7,20,21,22,23},{8,9,10,11,24,25,26,27},{12..., dimensions={0} | all-to-all | bytes 32768 | tf_op jit(solution)/shard_map/all_to_all | solution.py:49
  132.8 10.8 %all_to_all.65 = f32[16,1,1024]{2,1,0:T(1,128)S(1)} all-to-all(f32[16,1,1024]{2,1,0:T(1,128)S(1)} %broadcast_in_dim.29), channel_id=1, replica_groups={{0,4,8,12,32,36,40,44,64,68,72,76,96,100,104,108},{1,5,9,13,33,37,41,45..., dimensions={0} | all-to-all | bytes 131072 | tf_op jit(solution)/shard_map/all_to_all | solution.py:49
  144.5 7.6 %all_to_all.66 = f32[8,1,512]{2,1,0:T(1,128)S(1)} all-to-all(f32[8,1,512]{2,1,0:T(1,128)S(1)} %broadcast_in_dim.30), channel_id=1, replica_groups={{0,1,2,3,16,17,18,19},{4,5,6,7,20,21,22,23},{8,9,10,11,24,25,26,27},{12..., dimensions={0} | all-to-all | bytes 32768 | tf_op jit(solution)/shard_map/all_to_all | solution.py:49
  153.6 3.5 %all-to-all-start.9 = ((f32[16,1,1536]{2,1,0:T(1,128)}), f32[16,1,1536]{2,1,0:T(1,128)S(1)}, u32[]{:S(2)}, u32[]{:S(2)}) async-start(f32[16,1,1536]{2,1,0:T(1,128)} %broadcast_in_dim.31), calls=%async_computation.9 | async-start | bytes 196608 | tf_op jit(solution)/shard_map/all_to_all | solution.py:49
  157.1 7.8 %all-to-all-done.9 = f32[16,1,1536]{2,1,0:T(1,128)S(1)} async-done(((f32[16,1,1536]{2,1,0:T(1,128)}), f32[16,1,1536]{2,1,0:T(1,128)S(1)}, u32[]{:S(2)}, u32[]{:S(2)}) %all-to-all-start.9) | async-done | bytes 98336 | tf_op jit(solution)/shard_map/all_to_all | solution.py:49
  165.8 7.9 %all_to_all.67 = f32[8,1,768]{2,1,0:T(1,128)S(1)} all-to-all(f32[8,1,768]{2,1,0:T(1,128)S(1)} %broadcast_in_dim.32), channel_id=1, replica_groups={{0,1,2,3,16,17,18,19},{4,5,6,7,20,21,22,23},{8,9,10,11,24,25,26,27},{12..., dimensions={0} | all-to-all | bytes 49152 | tf_op jit(solution)/shard_map/all_to_all | solution.py:49
  174.3 6.9 %shard_map.52 = bf16[16,256,256]{2,1,0:T(8,128)(2,1)} custom-call(s32[4]{0:T(128)S(1)} %pad_add_fusion.place, bf16[512,1024]{1,0:T(8,128)(2,1)S(1)} %exponential_convert_fusion.weights, bf16[512,1024]{1,0:T(8,128)(2,1)S(1)} %pad_maximum_fusion.refs_1_.refs_0_, bf16[512,1024]{1,0:T(8,128)(2,1)S(1)} %copy-done.3, bf16[512,1024]{1,0:T(8,128)(2,1)S(1)} %copy-done.12, ...), custom_call_target="tpu_custom_call" | custom-call | flops 2147483648 | bytes 14680064 | tf_op jit(solution)/shard_map/pallas_call | solution.py:180
  182.7 3.1 %collective-permute-done.11.refs_8_ = bf16[16,256,256]{2,1,0:T(8,128)(2,1)} collective-permute-done((bf16[16,256,256]{2,1,0:T(8,128)(2,1)}, bf16[16,256,256]{2,1,0:T(8,128)(2,1)}, u32[]{:S(2)}, u32[]{:S(2)}) %collective-permute-start.11) | collective-permute-done | bytes 2097184 | tf_op jit(solution)/shard_map/ppermute | solution.py:44
  185.8 1.2 copy-done.13
  188.2 6.7 %shard_map.53 = bf16[16,256,256]{2,1,0:T(8,128)(2,1)S(1)} custom-call(s32[4]{0:T(128)S(1)} %pad_add_fusion.place, bf16[512,1024]{1,0:T(8,128)(2,1)S(1)} %copy-done.15, bf16[512,1024]{1,0:T(8,128)(2,1)S(1)} %pad_maximum_fusion.refs_1_.refs_0_, bf16[512,1024]{1,0:T(8,128)(2,1)S(1)} %copy-done.4, bf16[512,1024]{1,0:T(8,128)(2,1)S(1)} %copy-done.13, ...), custom_call_target="tpu_custom_call" | custom-call | flops 2147483648 | bytes 14680064 | tf_op jit(solution)/shard_map/pallas_call | solution.py:180
  194.9 31.8 %all_to_all.68 = bf16[16,256,256]{2,1,0:T(8,128)(2,1)S(1)} all-to-all(bf16[16,256,256]{2,1,0:T(8,128)(2,1)S(1)} %shard_map.53), channel_id=1, replica_groups=mesh['row'=8,'col'=16] {'col'}, dimensions={0} | all-to-all | bytes 4194304 | tf_op jit(solution)/shard_map/all_to_all | solution.py:268
  (127 shorter events, 20.6 us)
Async XLA Ops:
  1.7 4.7 %collective-permute-start = (bf16[256,512]{1,0:T(8,128)(2,1)S(1)}, bf16[256,512]{1,0:T(8,128)(2,1)S(1)}, u32[]{:S(2)}, u32[]{:S(2)}) collective-permute-start(bf16[256,512]{1,0:T(8,128)(2,1)S(1)} %get-tuple-element.40), channel_id=1, source_target_pairs={{0,16},{1,17},{2,18},{3,19},{4,20},{5,21},{6,22},{7,23},{8,24},{9,... | collective-permute-start | bytes 786440 | tf_op jit(solution)/shard_map/ppermute | solution.py:44
  1.8 15.5 %all-to-all-start = ((bf16[4,256,256]{2,1,0:T(8,128)(2,1)}), bf16[4,256,256]{2,1,0:T(8,128)(2,1)S(1)}, u32[]{:S(2)}, u32[]{:S(2)}) async-start(bf16[4,256,256]{2,1,0:T(8,128)(2,1)} %bitcast.73), calls=%async_computation | async-start | bytes 1048576 | tf_op jit(solution)/shard_map/all_to_all | solution.py:212
  6.5 16.7 %collective-permute-start.3 = (bf16[256,1024]{1,0:T(8,128)(2,1)S(1)}, bf16[256,1024]{1,0:T(8,128)(2,1)S(1)}, u32[]{:S(2)}, u32[]{:S(2)}) collective-permute-start(bf16[256,1024]{1,0:T(8,128)(2,1)S(1)} %maximum_select_fusion), channel_id=1, source_target_pairs={{0,64},{1,65},{2,66},{3,67},{4,68},{5,69},{6,70},{7,71},{8,72},{9,... | collective-permute-start | bytes 1572872 | tf_op jit(solution)/shard_map/ppermute | solution.py:44
  10.5 13.8 %collective-permute-start.2 = (bf16[256,1024]{1,0:T(8,128)(2,1)S(1)}, bf16[256,1024]{1,0:T(8,128)(2,1)S(1)}, u32[]{:S(2)}, u32[]{:S(2)}) collective-permute-start(bf16[256,1024]{1,0:T(8,128)(2,1)S(1)} %maximum_select_fusion), channel_id=1, source_target_pairs={{0,96},{1,97},{2,98},{3,99},{4,100},{5,101},{6,102},{7,103},{8,104... | collective-permute-start | bytes 1572872 | tf_op jit(solution)/shard_map/ppermute | solution.py:44
  11.2 13.1 %collective-permute-start.1 = (bf16[256,1024]{1,0:T(8,128)(2,1)S(1)}, bf16[256,1024]{1,0:T(8,128)(2,1)S(1)}, u32[]{:S(2)}, u32[]{:S(2)}) collective-permute-start(bf16[256,1024]{1,0:T(8,128)(2,1)S(1)} %maximum_select_fusion), channel_id=1, source_target_pairs={{0,32},{1,33},{2,34},{3,35},{4,36},{5,37},{6,38},{7,39},{8,40},{9,... | collective-permute-start | bytes 1572872 | tf_op jit(solution)/shard_map/ppermute | solution.py:44
  18.8 35.1 %all-to-all-start.1 = ((bf16[4,1024,256]{2,1,0:T(8,128)(2,1)}), bf16[4,1024,256]{2,1,0:T(8,128)(2,1)}, u32[]{:S(2)}, u32[]{:S(2)}) async-start(bf16[4,1024,256]{2,1,0:T(8,128)(2,1)} %broadcast_in_dim.23), calls=%async_computation.1 | async-start | bytes 4194304 | tf_op jit(solution)/shard_map/all_to_all | solution.py:215
  24.4 28.5 %copy-start = (bf16[512,1024]{1,0:T(8,128)(2,1)}, bf16[512,1024]{1,0:T(8,128)(2,1)S(1)}, u32[]{:S(2)}) copy-start(bf16[512,1024]{1,0:T(8,128)(2,1)S(1)} %constant_dynamic-update-slice_fusion.refs_2_.refs_1_) | copy-start | bytes 3145732
  24.4 16.1 %collective-permute-start.7 = (bf16[512,1024]{1,0:T(8,128)(2,1)S(1)}, bf16[512,1024]{1,0:T(8,128)(2,1)S(1)}, u32[]{:S(2)}, u32[]{:S(2)}) collective-permute-start(bf16[512,1024]{1,0:T(8,128)(2,1)S(1)} %constant_dynamic-update-slice_fusion.refs_2_.refs_1_), channel_id=1, source_target_pairs={{0,4},{1,5},{2,6},{3,7},{4,8},{5,9},{6,10},{7,11},{8,12},{9,13},{1... | collective-permute-start | bytes 3145736 | tf_op jit(solution)/shard_map/ppermute | solution.py:44
  26.5 15.2 %collective-permute-start.5 = (bf16[512,1024]{1,0:T(8,128)(2,1)S(1)}, bf16[512,1024]{1,0:T(8,128)(2,1)}, u32[]{:S(2)}, u32[]{:S(2)}) collective-permute-start(bf16[512,1024]{1,0:T(8,128)(2,1)S(1)} %constant_dynamic-update-slice_fusion.refs_2_.refs_1_), channel_id=1, source_target_pairs={{0,12},{1,13},{2,14},{3,15},{4,0},{5,1},{6,2},{7,3},{8,4},{9,5},{1... | collective-permute-start | bytes 3145736 | tf_op jit(solution)/shard_map/ppermute | solution.py:44
  27.9 25.0 %collective-permute-start.6 = (bf16[512,1024]{1,0:T(8,128)(2,1)S(1)}, bf16[512,1024]{1,0:T(8,128)(2,1)S(1)}, u32[]{:S(2)}, u32[]{:S(2)}) collective-permute-start(bf16[512,1024]{1,0:T(8,128)(2,1)S(1)} %pad_maximum_fusion.refs_1_.refs_0_), channel_id=1, source_target_pairs={{0,12},{1,13},{2,14},{3,15},{4,0},{5,1},{6,2},{7,3},{8,4},{9,5},{1... | collective-permute-start | bytes 3145736 | tf_op jit(solution)/shard_map/ppermute | solution.py:44
  29.9 23.9 %collective-permute-start.4 = (bf16[512,1024]{1,0:T(8,128)(2,1)S(1)}, bf16[512,1024]{1,0:T(8,128)(2,1)}, u32[]{:S(2)}, u32[]{:S(2)}) collective-permute-start(bf16[512,1024]{1,0:T(8,128)(2,1)S(1)} %pad_maximum_fusion.refs_1_.refs_0_), channel_id=1, source_target_pairs={{0,4},{1,5},{2,6},{3,7},{4,8},{5,9},{6,10},{7,11},{8,12},{9,13},{1... | collective-permute-start | bytes 3145736 | tf_op jit(solution)/shard_map/ppermute | solution.py:44
  40.5 1.0 copy-start.5
  52.8 1.0 copy-start.9
  53.8 14.2 %collective-permute-start.8 = (bf16[16,256,256]{2,1,0:T(8,128)(2,1)}, bf16[16,256,256]{2,1,0:T(8,128)(2,1)}, u32[]{:S(2)}, u32[]{:S(2)}) collective-permute-start(bf16[16,256,256]{2,1,0:T(8,128)(2,1)} %bitcast.9.refs_0_), channel_id=1, source_target_pairs={{0,16},{1,17},{2,18},{3,19},{4,20},{5,21},{6,22},{7,23},{8,24},{9,... | collective-permute-start | bytes 6291464 | tf_op jit(solution)/shard_map/ppermute | solution.py:44
  55.5 17.7 %collective-permute-start.9 = (bf16[512,1024]{1,0:T(8,128)(2,1)}, bf16[512,1024]{1,0:T(8,128)(2,1)}, u32[]{:S(2)}, u32[]{:S(2)}) collective-permute-start(bf16[512,1024]{1,0:T(8,128)(2,1)} %collective-permute-done.4.refs_5_.refs_4_), channel_id=1, source_target_pairs={{0,4},{1,5},{2,6},{3,7},{4,8},{5,9},{6,10},{7,11},{8,12},{9,13},{1... | collective-permute-start | bytes 3145736 | tf_op jit(solution)/shard_map/ppermute | solution.py:44
  55.9 17.3 %collective-permute-start.10 = (bf16[512,1024]{1,0:T(8,128)(2,1)}, bf16[512,1024]{1,0:T(8,128)(2,1)}, u32[]{:S(2)}, u32[]{:S(2)}) collective-permute-start(bf16[512,1024]{1,0:T(8,128)(2,1)} %collective-permute-done.5.refs_6_.refs_5_), channel_id=1, source_target_pairs={{0,12},{1,13},{2,14},{3,15},{4,0},{5,1},{6,2},{7,3},{8,4},{9,5},{1... | collective-permute-start | bytes 3145736 | tf_op jit(solution)/shard_map/ppermute | solution.py:44
  58.8 1.2 copy-start.1
  60.1 1.2 copy-start.6
  61.3 1.2 copy-start.10
  62.5 5.6 %copy-start.2 = (bf16[512,1024]{1,0:T(8,128)(2,1)S(1)}, bf16[512,1024]{1,0:T(8,128)(2,1)}, u32[]{:S(2)}) copy-start(bf16[512,1024]{1,0:T(8,128)(2,1)} %copy-done) | copy-start | bytes 3145732
  62.5 5.6 %copy-start.11 = (bf16[512,1024]{1,0:T(8,128)(2,1)S(1)}, bf16[512,1024]{1,0:T(8,128)(2,1)}, u32[]{:S(2)}) copy-start(bf16[512,1024]{1,0:T(8,128)(2,1)} %copy-done.9) | copy-start | bytes 3145732
  153.6 11.3 %all-to-all-start.9 = ((f32[16,1,1536]{2,1,0:T(1,128)}), f32[16,1,1536]{2,1,0:T(1,128)S(1)}, u32[]{:S(2)}, u32[]{:S(2)}) async-start(f32[16,1,1536]{2,1,0:T(1,128)} %broadcast_in_dim.31), calls=%async_computation.9 | async-start | bytes 196608 | tf_op jit(solution)/shard_map/all_to_all | solution.py:49
  165.8 8.4 %copy-start.3 = (bf16[512,1024]{1,0:T(8,128)(2,1)S(1)}, bf16[512,1024]{1,0:T(8,128)(2,1)}, u32[]{:S(2)}) copy-start(bf16[512,1024]{1,0:T(8,128)(2,1)} %copy-done) | copy-start | bytes 3145732
  165.8 8.4 %copy-start.7 = (bf16[512,1024]{1,0:T(8,128)(2,1)S(1)}, bf16[512,1024]{1,0:T(8,128)(2,1)}, u32[]{:S(2)}) copy-start(bf16[512,1024]{1,0:T(8,128)(2,1)} %copy-done.5) | copy-start | bytes 3145732
  165.8 8.4 %copy-start.12 = (bf16[512,1024]{1,0:T(8,128)(2,1)S(1)}, bf16[512,1024]{1,0:T(8,128)(2,1)}, u32[]{:S(2)}) copy-start(bf16[512,1024]{1,0:T(8,128)(2,1)} %copy-done.9) | copy-start | bytes 3145732
  174.2 7.0 %copy-start.14 = (bf16[512,1024]{1,0:T(8,128)(2,1)}, bf16[512,1024]{1,0:T(8,128)(2,1)S(1)}, u32[]{:S(2)}) copy-start(bf16[512,1024]{1,0:T(8,128)(2,1)S(1)} %exponential_convert_fusion.weights) | copy-start | bytes 3145732
  174.2 11.6 %copy-start.4 = (bf16[512,1024]{1,0:T(8,128)(2,1)S(1)}, bf16[512,1024]{1,0:T(8,128)(2,1)}, u32[]{:S(2)}) copy-start(bf16[512,1024]{1,0:T(8,128)(2,1)} %copy-done) | copy-start | bytes 3145732
  174.2 11.5 %copy-start.8 = (bf16[512,1024]{1,0:T(8,128)(2,1)S(1)}, bf16[512,1024]{1,0:T(8,128)(2,1)}, u32[]{:S(2)}) copy-start(bf16[512,1024]{1,0:T(8,128)(2,1)} %copy-done.5) | copy-start | bytes 3145732
  181.2 4.6 %collective-permute-start.11 = (bf16[16,256,256]{2,1,0:T(8,128)(2,1)}, bf16[16,256,256]{2,1,0:T(8,128)(2,1)}, u32[]{:S(2)}, u32[]{:S(2)}) collective-permute-start(bf16[16,256,256]{2,1,0:T(8,128)(2,1)} %shard_map.52), channel_id=1, source_target_pairs={{0,16},{1,17},{2,18},{3,19},{4,20},{5,21},{6,22},{7,23},{8,24},{9,... | collective-permute-start | bytes 6291464 | tf_op jit(solution)/shard_map/ppermute | solution.py:44
  185.8 1.2 copy-start.13
  187.0 1.2 copy-start.15

commit v4 on v3

--- a/solution.py
+++ b/solution.py
@@ -65,7 +65,6 @@
     return lax.rem(y + far_y, 4), lax.rem(z + far_z, 4)
 
 
-HIGHEST = lax.Precision.HIGHEST
 BLOCKS = 8
 
 
@@ -84,12 +83,11 @@
         for k in range(3):
             outs[k][...] = state_in[k][...]
     if not last_call:
-        total = jnp.zeros((256, 128), jnp.float32)
+        total = jnp.zeros((8, 256), jnp.float32)
         for k in range(16):
             wide = sources[0][k].astype(jnp.float32)
-            wide = wide * wide
-            total = total + wide[:, :128] + wide[:, 128:]
-        noise_squares[halves[sides[0]], :] = total
+            total = total + jnp.sum((wide * wide).reshape(32, 8, 256), axis=0)
+        noise_squares[:, halves[sides[0]]] = total
     for k, pair in enumerate(pieces):
         for side, where in enumerate(pair):
             row_group, col_group = place_of(place, where)
@@ -99,11 +97,8 @@
             for part in range(4):
                 values = held[k][side * 256 : side * 256 + 256, part * 256 : part * 256 + 256]
                 for n in range(len(sides)):
-                    term = lax.dot_general(
-                        sources[n][part * 4 + col_group],
-                        values,
-                        (((1,), (1,)), ((), ())),
-                        preferred_element_type=jnp.float32,
+                    term = jnp.dot(
+                        values, sources[n][part * 4 + col_group], preferred_element_type=jnp.float32
                     )
                     sums[n] = term if part == 0 else sums[n] + term
                 if sides[0] == 0:
@@ -114,21 +109,15 @@
             if sides[0] == 0:
                 squares[rows, :] += total
             for n, half in enumerate(sides):
-                gram[halves[half], rows] += sums[n]
+                gram[rows, halves[half]] += sums[n]
     if last_call:
-        data_sq = lax.dot_general(
-            jnp.ones((8, 128), jnp.float32),
-            squares[...],
-            (((1,), (1,)), ((), ())),
-            precision=HIGHEST,
-            preferred_element_type=jnp.float32,
-        )[0:1, :]
-        noise_sq = jnp.sum(noise_squares[...], axis=1, keepdims=True)
+        data_sq = jnp.sum(squares[...], axis=1, keepdims=True)
+        noise_sq = jnp.sum(noise_squares[...], axis=0, keepdims=True)
         gram[...] = (2.0 * gram[...] - noise_sq - data_sq) * (1.0 / (D * EPS))
 
 
 def gram_of(place, sources, sides, arrays, pieces, before, last_call):
-    outs = [(512, 1024), (1024, 128), (512, 128)]
+    outs = [(1024, 512), (1024, 128), (8, 512)]
     count = len(arrays)
     operands = [*sources, *arrays, *(before or [])]
     vmem = pl.BlockSpec(memory_space=pltpu.VMEM)
@@ -148,51 +137,72 @@
     )(place, *operands)
 
 
-def mix_kernel(pieces, away, place, weights, *refs):
-    held, out, buffer, sems = refs[:BLOCKS], refs[-3], refs[-2], refs[-1]
-    copies = []
-    for k, pair in enumerate(pieces):
-        for side, where in enumerate(pair):
-            row_group, col_group = place_of(place, where)
-            rows = pl.ds(pl.multiple_of(row_group * 256, 256), 256)
-            columns = pl.ds(pl.multiple_of(col_group * 1024, 1024), 1024)
-            copies.append(
-                pltpu.make_async_copy(
-                    held[k].at[pl.ds(side * 256, 256)], buffer.at[rows, columns], sems.at[2 * k + side]
+def mix_kernel(pieces, place, my_weights, other_weights, *refs):
+    held, (out, buffer, left, sems) = refs[: 2 * BLOCKS], refs[2 * BLOCKS :]
+    z, c, y = place[0], place[1], place[2]
+    copies = {}
+    for slot in range(2):
+        for k, pair in enumerate(pieces):
+            for side, where in enumerate(pair):
+                far_z = jnp.where(c == slot, where[0], where[1])
+                far_y = jnp.where(c == slot, where[1], where[0])
+                rows = pl.ds(pl.multiple_of(slot * 1024 + lax.rem(y + far_y, 4) * 256, 256), 256)
+                columns = pl.ds(pl.multiple_of(far_z * 1024, 1024), 1024)
+                copies[slot, where] = pltpu.make_async_copy(
+                    held[slot * BLOCKS + k].at[pl.ds(side * 256, 256)],
+                    buffer.at[rows, columns],
+                    sems.at[slot * 2 * BLOCKS + 2 * k + side],
                 )
-            )
-    for copy in copies:
-        copy.start()
-    half = place[1] if not away else 1 - place[1]
-    left = weights[pl.ds(pl.multiple_of(half * 256, 256), 256), :]
-    for copy in copies:
-        copy.wait()
-    for n in range(16):
-        total = jnp.dot(left, buffer[:, n * 256 : n * 256 + 256], preferred_element_type=jnp.float32)
-        if not away:
-            total = total + refs[BLOCKS][n].astype(jnp.float32)
-        out[n] = total.astype(out.dtype)
-
-
-def mix(place, weights, arrays, pieces, came):
+    order = [
+        [
+            [(slot, (far, k) if slot == core else (k, far)) for slot in range(2) for k in range(4)]
+            for core in range(2)
+        ]
+        for far in range(4)
+    ]
+    for core in range(2):
+
+        @pl.when(c == core)
+        def _():
+            for group in order:
+                for name in group[core]:
+                    copies[name].start()
+
+    left[:, :1024] = my_weights[...].T
+    left[:, 1024:] = other_weights[...].T
+    for far, group in enumerate(order):
+        for core in range(2):
+
+            @pl.when(c == core)
+            def _():
+                for name in group[core]:
+                    copies[name].wait()
+
+        first = lax.rem(z + far, 4) * 4
+        for part in range(4):
+            values = buffer[:, (far * 4 + part) * 256 : (far * 4 + part + 1) * 256]
+            total = jnp.dot(left[...], values, preferred_element_type=jnp.float32)
+            out[first + part] = total.astype(out.dtype)
+
+
+def mix(place, weights, arrays, pieces):
     vmem = pl.BlockSpec(memory_space=pltpu.VMEM)
-    operands = [weights, *arrays, *([] if came is None else [came])]
     return pl.pallas_call(
-        functools.partial(mix_kernel, pieces, came is None),
+        functools.partial(mix_kernel, pieces),
         out_shape=jax.ShapeDtypeStruct((16, 256, 256), jnp.bfloat16),
-        in_specs=[pl.BlockSpec(memory_space=pltpu.SMEM), vmem]
-        + [pl.BlockSpec(memory_space=pl.ANY)] * BLOCKS
-        + [vmem] * (came is not None),
+        in_specs=[pl.BlockSpec(memory_space=pltpu.SMEM), vmem, vmem]
+        + [pl.BlockSpec(memory_space=pl.ANY)] * 2 * BLOCKS,
         out_specs=vmem,
         scratch_shapes=[
-            pltpu.VMEM((1024, 4096), jnp.bfloat16),
-            pltpu.SemaphoreType.DMA((2 * BLOCKS,)),
+            pltpu.VMEM((2048, 4096), jnp.bfloat16),
+            pltpu.VMEM((256, 2048), jnp.bfloat16),
+            pltpu.SemaphoreType.DMA((4 * BLOCKS,)),
         ],
-        compiler_params=pltpu.CompilerParams(vmem_limit_bytes=32 * 2**20),
+        compiler_params=pltpu.CompilerParams(vmem_limit_bytes=36 * 2**20),
         cost_estimate=pl.CostEstimate(
-            flops=2 * 256 * 1024 * 4096, bytes_accessed=14 * 2**20, transcendentals=0
+            flops=2 * 256 * 2048 * 4096, bytes_accessed=20 * 2**20, transcendentals=0
         ),
-    )(place, *operands)
+    )(place, *weights, *arrays)
 
 
 def local(noise, data):
@@ -210,7 +220,7 @@
         (send(block, FIRST_UP), send(block, FIRST_DOWN), send(block, FIRST_TWO))
     )
     own = lax.all_to_all(
-        noise.reshape(4, 256, 256), AXES, 0, 0, tiled=True, axis_index_groups=groups("zcx")
+        jnp.swapaxes(noise.reshape(4, 256, 256), 1, 2), AXES, 0, 0, tiled=True, axis_index_groups=groups("zcx")
     )
     own = lax.all_to_all(
         jnp.broadcast_to(own[None], (4, 4, 256, 256)).reshape(4, 1024, 256),
@@ -237,13 +247,17 @@
     state = gram_of(place, [other], (1,), arrays[:6], pieces[:6], state, False)
     scores = gram_of(place, [own, other], (0, 1), arrays[6:], pieces[6:], state, True)[0]
 
+    my_scores = lax.dynamic_slice(scores, (0, c * 256), (1024, 256))
+    scores_away = lax.dynamic_slice(scores, (0, 256 - c * 256), (1024, 256))
+    received = []
+
     def row_exchange(g, extra):
-        mine = lse(scores + g[None, :], 1)
+        mine = lse(scores + g[:, None], 0)
         shared = spread(jnp.concatenate([mine, extra]), 8, "zy")
         return lse(shared[:, :512], 0), shared[:, 512:]
 
     def col_exchange(f, extra):
-        mine = lse(scores + f[:, None], 0)
+        mine = lse(scores + f[None, :], 1)
         shared = spread(jnp.concatenate([mine, extra]), 16, "cx")
         return lse(shared[:, :1024], 0), shared[:, 1024:]
 
@@ -254,14 +268,23 @@
         f = -log_count - row_exchange(g, nothing)[0]
         total, all_f = col_exchange(f, nothing if step < ITERS - 1 else f)
         g = -log_count - total
-    norm, all_g = row_exchange(g, lax.dynamic_slice(g, (y * 256,), (256,)))
-    weights = jnp.exp(scores + g[None, :] - norm[:, None]).astype(jnp.bfloat16)
-    away = mix(place, weights, arrays, pieces, None)
-    shares = mix(place, weights, arrays, pieces, send(away, OTHER))
+        if step < ITERS - 1:
+            queue = [scores_away, *arrays[2:], *arrays[:2]][3 * step : 3 * step + 3]
+            g, *queue = lax.optimization_barrier((g, *[send(values, OTHER) for values in queue]))
+            received += queue
+    norm, all_g = row_exchange(g, g)
+    all_g = lax.dynamic_index_in_dim(all_g.reshape(2, 4, 1024), x, 1, keepdims=False)
+    g_other = lax.dynamic_index_in_dim(all_g, 1 - c, 0, keepdims=False)
+    norm = lax.dynamic_slice(norm, (c * 256,), (256,))
+    other_scores, *other_arrays = received
+    other_arrays = other_arrays[6:] + other_arrays[:6]
+    weights = [
+        jnp.exp(part + potential[:, None] - norm[None, :]).astype(jnp.bfloat16)
+        for part, potential in ((my_scores, g), (other_scores, g_other))
+    ]
+    shares = mix(place, weights, arrays + other_arrays, pieces)
     noise_potential = EPS * lax.dynamic_slice(all_f, (z * 4, c * 256), (4, 256)).reshape(1024)
-    data_potential = EPS * lax.dynamic_index_in_dim(
-        all_g.reshape(2, 4, 256), x, 1, keepdims=False
-    ).reshape(512)
+    data_potential = EPS * lax.dynamic_slice(all_g, (0, y * 256), (2, 256)).reshape(512)
     shares, noise_potential, data_potential = lax.optimization_barrier(
         (shares, noise_potential, data_potential)
     )

time: 229 us -> 225 us (0.983)
  blocking collectives: 107 us -> 71.8 us
  waiting for transfers between devices: 38.7 us -> 56.8 us
  starting transfers between devices: 29.2 us -> 46.6 us
  Pallas kernels: 29.7 us -> 25.3 us
    all_to_all x8 -> x4, blocking collectives: 75.6 us -> 39.5 us  [spread(): lax.all_to_all(copies, AXES, 0, 0, tiled=True, axis_index_groups=groups(s...]
    all_to_all x1 -> x5, waiting for transfers between devices: 7.77 us -> 24.5 us  [spread(): lax.all_to_all(copies, AXES, 0, 0, tiled=True, axis_index_groups=groups(s...]
    all_to_all x1 -> x5, starting transfers between devices: 3.51 us -> 17.8 us  [spread(): lax.all_to_all(copies, AXES, 0, 0, tiled=True, axis_index_groups=groups(s...]
    unnamed x36 -> x14, local copies, waits for them, and re-layouts: 8.76 us -> 2.66 us
    pallas_call x2 -> x1, Pallas kernels: 13.6 us -> 9.32 us  [mix(): pl.pallas_call(functools.partial(mix_kernel, pieces), out_shape=jax.Shape...]
    ppermute x12 -> x20, starting transfers between devices: 16.7 us -> 19.8 us  [send(): return lax.ppermute(values, AXES, where)]
    broadcast_in_dim x9, local copies, waits for them, and re-layouts: 0.87 us -> 3.33 us  [spread(): copies = jnp.broadcast_to(values[None, None, :], (size, 1, values.shape[0]))]
    ppermute x12 -> x20, waiting for transfers between devices: 26.1 us -> 27.5 us  [send(): return lax.ppermute(values, AXES, where)]
  transfers between devices with their start and end apart: 15 -> 27, of which waited for: 7 -> 12; matrix products, arithmetic and copies ran while one was open for 1% -> 4% of each run, Pallas kernels for 5% -> 7%
where the time goes in v4:
time: 225 us; the launch traced here: 224 us
  blocking collectives  71.8 us (32%)
  waiting for transfers between devices  56.8 us (25%)
  starting transfers between devices  46.6 us (21%)
  Pallas kernels  25.3 us (11%)
  local copies, waits for them, and re-layouts  11.1 us (5%)
  other arithmetic  10.8 us (5%)
    all_to_all x4, blocking collectives, spread(): lax.all_to_all(copies, AXES, 0, 0, tiled=True, axis_index_groups=groups(s...  39.5 us
    all_to_all x1, blocking collectives, local(): shares = lax.all_to_all(shares, 'col', 0, 0, tiled=True)  32.3 us
    ppermute x20, waiting for transfers between devices, send(): return lax.ppermute(values, AXES, where)  27.5 us
    all_to_all x5, waiting for transfers between devices, spread(): lax.all_to_all(copies, AXES, 0, 0, tiled=True, axis_index_groups=groups(s...  24.5 us
    ppermute x20, starting transfers between devices, send(): return lax.ppermute(values, AXES, where)  19.8 us
    all_to_all x5, starting transfers between devices, spread(): lax.all_to_all(copies, AXES, 0, 0, tiled=True, axis_index_groups=groups(s...  17.8 us
    pallas_call x3, Pallas kernels, gram_of(): pl.pallas_call(functools.partial(gram_kernel, pieces, sides, before is No...  16 us
    pallas_call x1, Pallas kernels, mix(): pl.pallas_call(functools.partial(mix_kernel, pieces), out_shape=jax.Shape...  9.32 us
  transfers between devices with their start and end apart: 27, of which 12 were waited for; matrix products, arithmetic and copies ran while one was open for 4% of the time, Pallas kernels for 7%

profile of v4, /device:TPU:0, one launch (start us, length us, event | category | flops | bytes accessed | tf_op | source)
XLA Modules:
  0.0 223.7 jit_solution(5583923856858575968)
XLA Ops:
  1.8 4.6 %all-to-all-start = ((bf16[4,256,256]{1,2,0:T(8,128)(2,1)}), bf16[4,256,256]{1,2,0:T(8,128)(2,1)S(1)}, u32[]{:S(2)}, u32[]{:S(2)}) async-start(bf16[4,256,256]{1,2,0:T(8,128)(2,1)} %bitcast.76), calls=%async_computation | async-start | bytes 1048576 | tf_op jit(solution)/shard_map/all_to_all | solution.py:222
  6.5 2.0 collective-permute-start.1
  8.5 2.2 collective-permute-start.2
  10.7 1.8 collective-permute-start.3
  12.5 4.8 %all-to-all-done = bf16[4,256,256]{1,2,0:T(8,128)(2,1)S(1)} async-done(((bf16[4,256,256]{1,2,0:T(8,128)(2,1)}), bf16[4,256,256]{1,2,0:T(8,128)(2,1)S(1)}, u32[]{:S(2)}, u32[]{:S(2)}) %all-to-all-start) | async-done | bytes 524320 | tf_op jit(solution)/shard_map/all_to_all | solution.py:222
  19.0 4.4 %all-to-all-start.1 = ((bf16[4,1024,256]{2,1,0:T(8,128)(2,1)}), bf16[4,1024,256]{2,1,0:T(8,128)(2,1)}, u32[]{:S(2)}, u32[]{:S(2)}) async-start(bf16[4,1024,256]{2,1,0:T(8,128)(2,1)} %broadcast_in_dim.23), calls=%async_computation.1 | async-start | bytes 4194304 | tf_op jit(solution)/shard_map/all_to_all | solution.py:225
  26.2 3.3 %collective-permute-start.5 = (bf16[512,1024]{1,0:T(8,128)(2,1)S(1)}, bf16[512,1024]{1,0:T(8,128)(2,1)}, u32[]{:S(2)}, u32[]{:S(2)}) collective-permute-start(bf16[512,1024]{1,0:T(8,128)(2,1)S(1)} %constant_dynamic-update-slice_fusion.refs_2_.refs_1_), channel_id=1, source_target_pairs={{0,12},{1,13},{2,14},{3,15},{4,0},{5,1},{6,2},{7,3},{8,4},{9,5},{1... | collective-permute-start | bytes 3145736 | tf_op jit(solution)/shard_map/ppermute | solution.py:44
  30.4 2.5 %collective-permute-start.6 = (bf16[512,1024]{1,0:T(8,128)(2,1)S(1)}, bf16[512,1024]{1,0:T(8,128)(2,1)}, u32[]{:S(2)}, u32[]{:S(2)}) collective-permute-start(bf16[512,1024]{1,0:T(8,128)(2,1)S(1)} %pad_maximum_fusion.refs_1_.refs_0_), channel_id=1, source_target_pairs={{0,12},{1,13},{2,14},{3,15},{4,0},{5,1},{6,2},{7,3},{8,4},{9,5},{1... | collective-permute-start | bytes 3145736 | tf_op jit(solution)/shard_map/ppermute | solution.py:44
  32.9 8.9 %collective-permute-done.5.refs_6_.refs_5_ = bf16[512,1024]{1,0:T(8,128)(2,1)} collective-permute-done((bf16[512,1024]{1,0:T(8,128)(2,1)S(1)}, bf16[512,1024]{1,0:T(8,128)(2,1)}, u32[]{:S(2)}, u32[]{:S(2)}) %collective-permute-start.5) | collective-permute-done | bytes 1048608 | tf_op jit(solution)/shard_map/ppermute | solution.py:44
  41.8 3.8 %collective-permute-done.7.refs_4_.refs_3_ = bf16[512,1024]{1,0:T(8,128)(2,1)} collective-permute-done((bf16[512,1024]{1,0:T(8,128)(2,1)S(1)}, bf16[512,1024]{1,0:T(8,128)(2,1)}, u32[]{:S(2)}, u32[]{:S(2)}) %collective-permute-start.7) | collective-permute-done | bytes 1048608 | tf_op jit(solution)/shard_map/ppermute | solution.py:44
  45.6 11.2 %collective-permute-done.4.refs_5_.refs_4_ = bf16[512,1024]{1,0:T(8,128)(2,1)} collective-permute-done((bf16[512,1024]{1,0:T(8,128)(2,1)S(1)}, bf16[512,1024]{1,0:T(8,128)(2,1)}, u32[]{:S(2)}, u32[]{:S(2)}) %collective-permute-start.4) | collective-permute-done | bytes 1048608 | tf_op jit(solution)/shard_map/ppermute | solution.py:44
  56.8 2.1 collective-permute-start.8
  62.8 5.6 %shard_map.49 = (f32[1024,512]{1,0:T(8,128)S(1)}, f32[1024,128]{1,0:T(8,128)S(1)}, f32[8,512]{1,0:T(8,128)S(1)}) custom-call(s32[4]{0:T(128)S(1)} %pad_add_fusion.place, bf16[16,256,256]{2,1,0:T(8,128)(2,1)} %bitcast.10.refs_0_, bf16[512,1024]{1,0:T(8,128)(2,1)S(1)} %pad_maximum_fusion.refs_1_.refs_0_, bf16[512,1024]{1,0:T(8,128)(2,1)S(1)} %copy-done.1, ...), custom_call_target="tpu_custom_call" | custom-call | flops 1610612736 | bytes 14680064 | tf_op jit(solution)/shard_map/pallas_call | solution.py:125
  68.4 5.1 %shard_map.50 = (f32[1024,512]{1,0:T(8,128)S(1)}, f32[1024,128]{1,0:T(8,128)S(1)}, f32[8,512]{1,0:T(8,128)S(1)}) custom-call(s32[4]{0:T(128)S(1)} %pad_add_fusion.place, bf16[16,256,256]{2,1,0:T(8,128)(2,1)} %collective-permute-done.8.refs_0_.refs_1_, ...), custom_call_target="tpu_custom_call", output_to_operand_aliasing={{0}: (8, {}), {1}: (9, {}), {2}: (10, {})} | custom-call | flops 1610612736 | bytes 14680064 | tf_op jit(solution)/shard_map/pallas_call | solution.py:125
  74.0 2.4 %collective-permute-done.9.refs_2_.refs_6_ = bf16[512,1024]{1,0:T(8,128)(2,1)} collective-permute-done((bf16[512,1024]{1,0:T(8,128)(2,1)}, bf16[512,1024]{1,0:T(8,128)(2,1)}, u32[]{:S(2)}, u32[]{:S(2)}) %collective-permute-start.9) | collective-permute-done | bytes 1048608 | tf_op jit(solution)/shard_map/ppermute | solution.py:44
  76.4 5.2 %shard_map.51 = (f32[1024,512]{1,0:T(8,128)S(1)}, f32[1024,128]{1,0:T(8,128)S(1)}, f32[8,512]{1,0:T(8,128)S(1)}) custom-call(s32[4]{0:T(128)S(1)} %pad_add_fusion.place, bf16[16,256,256]{2,1,0:T(8,128)(2,1)} %bitcast.10.refs_0_, ...), custom_call_target="tpu_custom_call", output_to_operand_aliasing={{0}: (5, {}), {1}: (6, {}), {2}: (7, {})} | custom-call | flops 1073741824 | bytes 10485760 | tf_op jit(solution)/shard_map/pallas_call | solution.py:125
  82.8 4.3 %all-to-all-start.2 = ((f32[8,1,512]{2,1,0:T(1,128)}), f32[8,1,512]{2,1,0:T(1,128)S(1)}, u32[]{:S(2)}, u32[]{:S(2)}) async-start(f32[8,1,512]{2,1,0:T(1,128)} %broadcast_in_dim.24), calls=%async_computation.2 | async-start | bytes 32768 | tf_op jit(solution)/shard_map/all_to_all | solution.py:49
  88.7 3.7 %all-to-all-done.2 = f32[8,1,512]{2,1,0:T(1,128)S(1)} async-done(((f32[8,1,512]{2,1,0:T(1,128)}), f32[8,1,512]{2,1,0:T(1,128)S(1)}, u32[]{:S(2)}, u32[]{:S(2)}) %all-to-all-start.2) | async-done | bytes 16416 | tf_op jit(solution)/shard_map/all_to_all | solution.py:49
  93.4 10.2 %all_to_all.60 = f32[16,1,1024]{2,1,0:T(1,128)S(1)} all-to-all(f32[16,1,1024]{2,1,0:T(1,128)S(1)} %broadcast_in_dim.25), channel_id=1, replica_groups={{0,4,8,12,32,36,40,44,64,68,72,76,96,100,104,108},{1,5,9,13,33,37,41,45..., dimensions={0} | all-to-all | bytes 131072 | tf_op jit(solution)/shard_map/all_to_all | solution.py:49
  105.0 3.3 %all-to-all-start.4 = ((f32[8,1,512]{2,1,0:T(1,128)}), f32[8,1,512]{2,1,0:T(1,128)S(1)}, u32[]{:S(2)}, u32[]{:S(2)}) async-start(f32[8,1,512]{2,1,0:T(1,128)} %broadcast_in_dim.26), calls=%async_computation.4 | async-start | bytes 32768 | tf_op jit(solution)/shard_map/all_to_all | solution.py:49
  109.3 4.3 %all-to-all-done.4 = f32[8,1,512]{2,1,0:T(1,128)S(1)} async-done(((f32[8,1,512]{2,1,0:T(1,128)}), f32[8,1,512]{2,1,0:T(1,128)S(1)}, u32[]{:S(2)}, u32[]{:S(2)}) %all-to-all-start.4) | async-done | bytes 16416 | tf_op jit(solution)/shard_map/all_to_all | solution.py:49
  114.5 10.8 %all_to_all.61 = f32[16,1,1024]{2,1,0:T(1,128)S(1)} all-to-all(f32[16,1,1024]{2,1,0:T(1,128)S(1)} %broadcast_in_dim.27), channel_id=1, replica_groups={{0,4,8,12,32,36,40,44,64,68,72,76,96,100,104,108},{1,5,9,13,33,37,41,45..., dimensions={0} | all-to-all | bytes 131072 | tf_op jit(solution)/shard_map/all_to_all | solution.py:49
  126.8 3.3 %all-to-all-start.6 = ((f32[8,1,512]{2,1,0:T(1,128)}), f32[8,1,512]{2,1,0:T(1,128)S(1)}, u32[]{:S(2)}, u32[]{:S(2)}) async-start(f32[8,1,512]{2,1,0:T(1,128)} %broadcast_in_dim.28), calls=%async_computation.6 | async-start | bytes 32768 | tf_op jit(solution)/shard_map/all_to_all | solution.py:49
  131.1 4.3 %all-to-all-done.6 = f32[8,1,512]{2,1,0:T(1,128)S(1)} async-done(((f32[8,1,512]{2,1,0:T(1,128)}), f32[8,1,512]{2,1,0:T(1,128)S(1)}, u32[]{:S(2)}, u32[]{:S(2)}) %all-to-all-start.6) | async-done | bytes 16416 | tf_op jit(solution)/shard_map/all_to_all | solution.py:49
  136.3 10.8 %all_to_all.62 = f32[16,1,1024]{2,1,0:T(1,128)S(1)} all-to-all(f32[16,1,1024]{2,1,0:T(1,128)S(1)} %broadcast_in_dim.29), channel_id=1, replica_groups={{0,4,8,12,32,36,40,44,64,68,72,76,96,100,104,108},{1,5,9,13,33,37,41,45..., dimensions={0} | all-to-all | bytes 131072 | tf_op jit(solution)/shard_map/all_to_all | solution.py:49
  147.9 7.6 %all_to_all.63 = f32[8,1,512]{2,1,0:T(1,128)S(1)} all-to-all(f32[8,1,512]{2,1,0:T(1,128)S(1)} %broadcast_in_dim.30), channel_id=1, replica_groups={{0,1,2,3,16,17,18,19},{4,5,6,7,20,21,22,23},{8,9,10,11,24,25,26,27},{12..., dimensions={0} | all-to-all | bytes 32768 | tf_op jit(solution)/shard_map/all_to_all | solution.py:49
  157.1 3.5 %all-to-all-start.9 = ((f32[16,1,1536]{2,1,0:T(1,128)}), f32[16,1,1536]{2,1,0:T(1,128)S(1)}, u32[]{:S(2)}, u32[]{:S(2)}) async-start(f32[16,1,1536]{2,1,0:T(1,128)} %broadcast_in_dim.31), calls=%async_computation.9 | async-start | bytes 196608 | tf_op jit(solution)/shard_map/all_to_all | solution.py:49
  160.7 7.7 %all-to-all-done.9 = f32[16,1,1536]{2,1,0:T(1,128)S(1)} async-done(((f32[16,1,1536]{2,1,0:T(1,128)}), f32[16,1,1536]{2,1,0:T(1,128)S(1)}, u32[]{:S(2)}, u32[]{:S(2)}) %all-to-all-start.9) | async-done | bytes 98336 | tf_op jit(solution)/shard_map/all_to_all | solution.py:49
  169.8 3.3 %all-to-all-start.10 = ((f32[8,1,1536]{2,1,0:T(1,128)}), f32[8,1,1536]{2,1,0:T(1,128)S(1)}, u32[]{:S(2)}, u32[]{:S(2)}) async-start(f32[8,1,1536]{2,1,0:T(1,128)} %broadcast_in_dim.32), calls=%async_computation.10 | async-start | bytes 98304 | tf_op jit(solution)/shard_map/all_to_all | solution.py:49
  173.9 4.6 %all-to-all-done.10 = f32[8,1,1536]{2,1,0:T(1,128)S(1)} async-done(((f32[8,1,1536]{2,1,0:T(1,128)}), f32[8,1,1536]{2,1,0:T(1,128)S(1)}, u32[]{:S(2)}, u32[]{:S(2)}) %all-to-all-start.10) | async-done | bytes 49184 | tf_op jit(solution)/shard_map/all_to_all | solution.py:49
  180.9 9.3 %shard_map.52 = bf16[16,256,256]{2,1,0:T(8,128)(2,1)} custom-call(s32[4]{0:T(128)S(1)} %pad_add_fusion.place, bf16[1024,256]{1,0:T(8,128)(2,1)S(1)} %get-tuple-element.66.my_weights, bf16[1024,256]{1,0:T(8,128)(2,1)S(1)} %get-tuple-element.65.other_weights, bf16[512,1024]{1,0:T(8,128)(2,1)S(1)} %pad_maximum_fusion.refs_1_.refs_0_, ...), custom_call_target="tpu_custom_call" | custom-call | flops 4294967296 | bytes 20971520 | tf_op jit(solution)/shard_map/pallas_call | solution.py:190
  190.2 32.3 %all_to_all.64 = bf16[16,256,256]{2,1,0:T(8,128)(2,1)S(1)} all-to-all(bf16[16,256,256]{2,1,0:T(8,128)(2,1)} %shard_map.52), channel_id=1, replica_groups=mesh['row'=8,'col'=16] {'col'}, dimensions={0} | all-to-all | bytes 4194304 | tf_op jit(solution)/shard_map/all_to_all | solution.py:291
  (127 shorter events, 29.0 us)
Async XLA Ops:
  1.7 4.7 %collective-permute-start = (bf16[256,512]{1,0:T(8,128)(2,1)S(1)}, bf16[256,512]{1,0:T(8,128)(2,1)S(1)}, u32[]{:S(2)}, u32[]{:S(2)}) collective-permute-start(bf16[256,512]{1,0:T(8,128)(2,1)S(1)} %get-tuple-element.64), channel_id=1, source_target_pairs={{0,16},{1,17},{2,18},{3,19},{4,20},{5,21},{6,22},{7,23},{8,24},{9,... | collective-permute-start | bytes 786440 | tf_op jit(solution)/shard_map/ppermute | solution.py:44
  1.8 15.5 %all-to-all-start = ((bf16[4,256,256]{1,2,0:T(8,128)(2,1)}), bf16[4,256,256]{1,2,0:T(8,128)(2,1)S(1)}, u32[]{:S(2)}, u32[]{:S(2)}) async-start(bf16[4,256,256]{1,2,0:T(8,128)(2,1)} %bitcast.76), calls=%async_computation | async-start | bytes 1048576 | tf_op jit(solution)/shard_map/all_to_all | solution.py:222
  6.5 16.9 %collective-permute-start.1 = (bf16[256,1024]{1,0:T(8,128)(2,1)S(1)}, bf16[256,1024]{1,0:T(8,128)(2,1)S(1)}, u32[]{:S(2)}, u32[]{:S(2)}) collective-permute-start(bf16[256,1024]{1,0:T(8,128)(2,1)S(1)} %maximum_select_fusion), channel_id=1, source_target_pairs={{0,32},{1,33},{2,34},{3,35},{4,36},{5,37},{6,38},{7,39},{8,40},{9,... | collective-permute-start | bytes 1572872 | tf_op jit(solution)/shard_map/ppermute | solution.py:44
  8.5 15.0 %collective-permute-start.2 = (bf16[256,1024]{1,0:T(8,128)(2,1)S(1)}, bf16[256,1024]{1,0:T(8,128)(2,1)S(1)}, u32[]{:S(2)}, u32[]{:S(2)}) collective-permute-start(bf16[256,1024]{1,0:T(8,128)(2,1)S(1)} %maximum_select_fusion), channel_id=1, source_target_pairs={{0,96},{1,97},{2,98},{3,99},{4,100},{5,101},{6,102},{7,103},{8,104... | collective-permute-start | bytes 1572872 | tf_op jit(solution)/shard_map/ppermute | solution.py:44
  10.7 14.3 %collective-permute-start.3 = (bf16[256,1024]{1,0:T(8,128)(2,1)S(1)}, bf16[256,1024]{1,0:T(8,128)(2,1)}, u32[]{:S(2)}, u32[]{:S(2)}) collective-permute-start(bf16[256,1024]{1,0:T(8,128)(2,1)S(1)} %maximum_select_fusion), channel_id=1, source_target_pairs={{0,64},{1,65},{2,66},{3,67},{4,68},{5,69},{6,70},{7,71},{8,72},{9,... | collective-permute-start | bytes 1572872 | tf_op jit(solution)/shard_map/ppermute | solution.py:44
  19.0 37.8 %all-to-all-start.1 = ((bf16[4,1024,256]{2,1,0:T(8,128)(2,1)}), bf16[4,1024,256]{2,1,0:T(8,128)(2,1)}, u32[]{:S(2)}, u32[]{:S(2)}) async-start(bf16[4,1024,256]{2,1,0:T(8,128)(2,1)} %broadcast_in_dim.23), calls=%async_computation.1 | async-start | bytes 4194304 | tf_op jit(solution)/shard_map/all_to_all | solution.py:225
  23.5 0.8 copy-start.3
  25.0 4.5 %copy-start.4 = (bf16[256,1024]{1,0:T(8,128)(2,1)S(1)}, bf16[256,1024]{1,0:T(8,128)(2,1)}, u32[]{:S(2)}) copy-start(bf16[256,1024]{1,0:T(8,128)(2,1)} %copy-done.3) | copy-start | bytes 1572868
  26.1 34.9 %copy-start = (bf16[512,1024]{1,0:T(8,128)(2,1)}, bf16[512,1024]{1,0:T(8,128)(2,1)S(1)}, u32[]{:S(2)}) copy-start(bf16[512,1024]{1,0:T(8,128)(2,1)S(1)} %constant_dynamic-update-slice_fusion.refs_2_.refs_1_) | copy-start | bytes 3145732
  26.2 15.6 %collective-permute-start.5 = (bf16[512,1024]{1,0:T(8,128)(2,1)S(1)}, bf16[512,1024]{1,0:T(8,128)(2,1)}, u32[]{:S(2)}, u32[]{:S(2)}) collective-permute-start(bf16[512,1024]{1,0:T(8,128)(2,1)S(1)} %constant_dynamic-update-slice_fusion.refs_2_.refs_1_), channel_id=1, source_target_pairs={{0,12},{1,13},{2,14},{3,15},{4,0},{5,1},{6,2},{7,3},{8,4},{9,5},{1... | collective-permute-start | bytes 3145736 | tf_op jit(solution)/shard_map/ppermute | solution.py:44
  29.5 16.1 %collective-permute-start.7 = (bf16[512,1024]{1,0:T(8,128)(2,1)S(1)}, bf16[512,1024]{1,0:T(8,128)(2,1)}, u32[]{:S(2)}, u32[]{:S(2)}) collective-permute-start(bf16[512,1024]{1,0:T(8,128)(2,1)S(1)} %constant_dynamic-update-slice_fusion.refs_2_.refs_1_), channel_id=1, source_target_pairs={{0,4},{1,5},{2,6},{3,7},{4,8},{5,9},{6,10},{7,11},{8,12},{9,13},{1... | collective-permute-start | bytes 3145736 | tf_op jit(solution)/shard_map/ppermute | solution.py:44
  29.5 27.3 %collective-permute-start.4 = (bf16[512,1024]{1,0:T(8,128)(2,1)S(1)}, bf16[512,1024]{1,0:T(8,128)(2,1)}, u32[]{:S(2)}, u32[]{:S(2)}) collective-permute-start(bf16[512,1024]{1,0:T(8,128)(2,1)S(1)} %pad_maximum_fusion.refs_1_.refs_0_), channel_id=1, source_target_pairs={{0,4},{1,5},{2,6},{3,7},{4,8},{5,9},{6,10},{7,11},{8,12},{9,13},{1... | collective-permute-start | bytes 3145736 | tf_op jit(solution)/shard_map/ppermute | solution.py:44
  30.4 26.4 %collective-permute-start.6 = (bf16[512,1024]{1,0:T(8,128)(2,1)S(1)}, bf16[512,1024]{1,0:T(8,128)(2,1)}, u32[]{:S(2)}, u32[]{:S(2)}) collective-permute-start(bf16[512,1024]{1,0:T(8,128)(2,1)S(1)} %pad_maximum_fusion.refs_1_.refs_0_), channel_id=1, source_target_pairs={{0,12},{1,13},{2,14},{3,15},{4,0},{5,1},{6,2},{7,3},{8,4},{9,5},{1... | collective-permute-start | bytes 3145736 | tf_op jit(solution)/shard_map/ppermute | solution.py:44
  56.8 11.6 %collective-permute-start.8 = (bf16[16,256,256]{2,1,0:T(8,128)(2,1)}, bf16[16,256,256]{2,1,0:T(8,128)(2,1)}, u32[]{:S(2)}, u32[]{:S(2)}) collective-permute-start(bf16[16,256,256]{2,1,0:T(8,128)(2,1)} %bitcast.10.refs_0_), channel_id=1, source_target_pairs={{0,16},{1,17},{2,18},{3,19},{4,20},{5,21},{6,22},{7,23},{8,24},{9,... | collective-permute-start | bytes 6291464 | tf_op jit(solution)/shard_map/ppermute | solution.py:44
  58.9 15.1 %collective-permute-start.10 = (bf16[512,1024]{1,0:T(8,128)(2,1)}, bf16[512,1024]{1,0:T(8,128)(2,1)}, u32[]{:S(2)}, u32[]{:S(2)}) collective-permute-start(bf16[512,1024]{1,0:T(8,128)(2,1)} %collective-permute-done.5.refs_6_.refs_5_), channel_id=1, source_target_pairs={{0,12},{1,13},{2,14},{3,15},{4,0},{5,1},{6,2},{7,3},{8,4},{9,5},{1... | collective-permute-start | bytes 3145736 | tf_op jit(solution)/shard_map/ppermute | solution.py:44
  60.1 16.3 %collective-permute-start.9 = (bf16[512,1024]{1,0:T(8,128)(2,1)}, bf16[512,1024]{1,0:T(8,128)(2,1)}, u32[]{:S(2)}, u32[]{:S(2)}) collective-permute-start(bf16[512,1024]{1,0:T(8,128)(2,1)} %collective-permute-done.4.refs_5_.refs_4_), channel_id=1, source_target_pairs={{0,4},{1,5},{2,6},{3,7},{4,8},{5,9},{6,10},{7,11},{8,12},{9,13},{1... | collective-permute-start | bytes 3145736 | tf_op jit(solution)/shard_map/ppermute | solution.py:44
  61.0 42.7 %collective-permute-start.12 = (bf16[512,1024]{1,0:T(8,128)(2,1)}, bf16[512,1024]{1,0:T(8,128)(2,1)}, u32[]{:S(2)}, u32[]{:S(2)}) collective-permute-start(bf16[512,1024]{1,0:T(8,128)(2,1)} %collective-permute-done.6.refs_3_.refs_2_), channel_id=1, source_target_pairs={{0,16},{1,17},{2,18},{3,19},{4,20},{5,21},{6,22},{7,23},{8,24},{9,... | collective-permute-start | bytes 3145736 | tf_op jit(solution)/shard_map/ppermute | solution.py:44
  61.1 42.7 %collective-permute-start.13 = (bf16[512,1024]{1,0:T(8,128)(2,1)}, bf16[512,1024]{1,0:T(8,128)(2,1)}, u32[]{:S(2)}, u32[]{:S(2)}) collective-permute-start(bf16[512,1024]{1,0:T(8,128)(2,1)} %collective-permute-done.7.refs_4_.refs_3_), channel_id=1, source_target_pairs={{0,16},{1,17},{2,18},{3,19},{4,20},{5,21},{6,22},{7,23},{8,24},{9,... | collective-permute-start | bytes 3145736 | tf_op jit(solution)/shard_map/ppermute | solution.py:44
  61.6 1.2 copy-start.1
  82.8 9.6 %all-to-all-start.2 = ((f32[8,1,512]{2,1,0:T(1,128)}), f32[8,1,512]{2,1,0:T(1,128)S(1)}, u32[]{:S(2)}, u32[]{:S(2)}) async-start(f32[8,1,512]{2,1,0:T(1,128)} %broadcast_in_dim.24), calls=%async_computation.2 | async-start | bytes 32768 | tf_op jit(solution)/shard_map/all_to_all | solution.py:49
  88.2 15.5 %collective-permute-start.11 = (f32[1024,256]{1,0:T(8,128)}, f32[1024,256]{1,0:T(8,128)}, u32[]{:S(2)}, u32[]{:S(2)}) collective-permute-start(f32[1024,256]{1,0:T(8,128)} %constant_dynamic-slice_fusion.1), channel_id=1, source_target_pairs={{0,16},{1,17},{2,18},{3,19},{4,20},{5,21},{6,22},{7,23},{8,24},{9,... | collective-permute-start | bytes 3145736 | tf_op jit(solution)/shard_map/ppermute | solution.py:44
  105.0 8.5 %all-to-all-start.4 = ((f32[8,1,512]{2,1,0:T(1,128)}), f32[8,1,512]{2,1,0:T(1,128)S(1)}, u32[]{:S(2)}, u32[]{:S(2)}) async-start(f32[8,1,512]{2,1,0:T(1,128)} %broadcast_in_dim.26), calls=%async_computation.4 | async-start | bytes 32768 | tf_op jit(solution)/shard_map/all_to_all | solution.py:49
  108.4 17.1 %collective-permute-start.14 = (bf16[512,1024]{1,0:T(8,128)(2,1)}, bf16[512,1024]{1,0:T(8,128)(2,1)}, u32[]{:S(2)}, u32[]{:S(2)}) collective-permute-start(bf16[512,1024]{1,0:T(8,128)(2,1)} %collective-permute-done.4.refs_5_.refs_4_), channel_id=1, source_target_pairs={{0,16},{1,17},{2,18},{3,19},{4,20},{5,21},{6,22},{7,23},{8,24},{9,... | collective-permute-start | bytes 3145736 | tf_op jit(solution)/shard_map/ppermute | solution.py:44
  108.8 16.7 %collective-permute-start.15 = (bf16[512,1024]{1,0:T(8,128)(2,1)}, bf16[512,1024]{1,0:T(8,128)(2,1)}, u32[]{:S(2)}, u32[]{:S(2)}) collective-permute-start(bf16[512,1024]{1,0:T(8,128)(2,1)} %collective-permute-done.5.refs_6_.refs_5_), channel_id=1, source_target_pairs={{0,16},{1,17},{2,18},{3,19},{4,20},{5,21},{6,22},{7,23},{8,24},{9,... | collective-permute-start | bytes 3145736 | tf_op jit(solution)/shard_map/ppermute | solution.py:44
  109.0 16.5 %collective-permute-start.16 = (bf16[512,1024]{1,0:T(8,128)(2,1)}, bf16[512,1024]{1,0:T(8,128)(2,1)}, u32[]{:S(2)}, u32[]{:S(2)}) collective-permute-start(bf16[512,1024]{1,0:T(8,128)(2,1)} %collective-permute-done.9.refs_2_.refs_6_), channel_id=1, source_target_pairs={{0,16},{1,17},{2,18},{3,19},{4,20},{5,21},{6,22},{7,23},{8,24},{9,... | collective-permute-start | bytes 3145736 | tf_op jit(solution)/shard_map/ppermute | solution.py:44
  126.8 8.5 %all-to-all-start.6 = ((f32[8,1,512]{2,1,0:T(1,128)}), f32[8,1,512]{2,1,0:T(1,128)S(1)}, u32[]{:S(2)}, u32[]{:S(2)}) async-start(f32[8,1,512]{2,1,0:T(1,128)} %broadcast_in_dim.28), calls=%async_computation.6 | async-start | bytes 32768 | tf_op jit(solution)/shard_map/all_to_all | solution.py:49
  130.1 17.0 %collective-permute-start.19 = (bf16[512,1024]{1,0:T(8,128)(2,1)}, bf16[512,1024]{1,0:T(8,128)(2,1)}, u32[]{:S(2)}, u32[]{:S(2)}) collective-permute-start(bf16[512,1024]{1,0:T(8,128)(2,1)} %copy-done), channel_id=1, source_target_pairs={{0,16},{1,17},{2,18},{3,19},{4,20},{5,21},{6,22},{7,23},{8,24},{9,... | collective-permute-start | bytes 3145736 | tf_op jit(solution)/shard_map/ppermute | solution.py:44
  130.5 16.6 %collective-permute-start.18 = (bf16[512,1024]{1,0:T(8,128)(2,1)S(1)}, bf16[512,1024]{1,0:T(8,128)(2,1)}, u32[]{:S(2)}, u32[]{:S(2)}) collective-permute-start(bf16[512,1024]{1,0:T(8,128)(2,1)S(1)} %pad_maximum_fusion.refs_1_.refs_0_), channel_id=1, source_target_pairs={{0,16},{1,17},{2,18},{3,19},{4,20},{5,21},{6,22},{7,23},{8,24},{9,... | collective-permute-start | bytes 3145736 | tf_op jit(solution)/shard_map/ppermute | solution.py:44
  130.7 16.5 %collective-permute-start.17 = (bf16[512,1024]{1,0:T(8,128)(2,1)}, bf16[512,1024]{1,0:T(8,128)(2,1)}, u32[]{:S(2)}, u32[]{:S(2)}) collective-permute-start(bf16[512,1024]{1,0:T(8,128)(2,1)} %collective-permute-done.10.refs_3_.refs_7_), channel_id=1, source_target_pairs={{0,16},{1,17},{2,18},{3,19},{4,20},{5,21},{6,22},{7,23},{8,24},{9,... | collective-permute-start | bytes 3145736 | tf_op jit(solution)/shard_map/ppermute | solution.py:44
  157.1 11.3 %all-to-all-start.9 = ((f32[16,1,1536]{2,1,0:T(1,128)}), f32[16,1,1536]{2,1,0:T(1,128)S(1)}, u32[]{:S(2)}, u32[]{:S(2)}) async-start(f32[16,1,1536]{2,1,0:T(1,128)} %broadcast_in_dim.31), calls=%async_computation.9 | async-start | bytes 196608 | tf_op jit(solution)/shard_map/all_to_all | solution.py:49
  169.8 8.6 %all-to-all-start.10 = ((f32[8,1,1536]{2,1,0:T(1,128)}), f32[8,1,1536]{2,1,0:T(1,128)S(1)}, u32[]{:S(2)}, u32[]{:S(2)}) async-start(f32[8,1,1536]{2,1,0:T(1,128)} %broadcast_in_dim.32), calls=%async_computation.10 | async-start | bytes 98304 | tf_op jit(solution)/shard_map/all_to_all | solution.py:49
  178.6 2.3 %copy-start.2 = (bf16[512,1024]{1,0:T(8,128)(2,1)S(1)}, bf16[512,1024]{1,0:T(8,128)(2,1)}, u32[]{:S(2)}) copy-start(bf16[512,1024]{1,0:T(8,128)(2,1)} %copy-done) | copy-start | bytes 3145732

commit v5 on v4

--- a/solution.py
+++ b/solution.py
@@ -212,7 +212,8 @@
 
     halves = data.reshape(2, 256, 512)
     kept = lax.dynamic_index_in_dim(halves, c, 0, keepdims=False)
-    came = send(lax.dynamic_index_in_dim(halves, 1 - c, 0, keepdims=False), OTHER)
+    came = send(halves, OTHER)
+    came = lax.dynamic_index_in_dim(came, c, 0, keepdims=False)
     block = jnp.where(
         c == 0, jnp.concatenate([kept, came], 1), jnp.concatenate([came, kept], 1)
     )
@@ -269,7 +270,7 @@
         total, all_f = col_exchange(f, nothing if step < ITERS - 1 else f)
         g = -log_count - total
         if step < ITERS - 1:
-            queue = [scores_away, *arrays[2:], *arrays[:2]][3 * step : 3 * step + 3]
+            queue = [scores_away, *arrays[2:], *arrays[:2]][(0, 5, 9)[step] : (5, 9, 9)[step]]
             g, *queue = lax.optimization_barrier((g, *[send(values, OTHER) for values in queue]))
             received += queue
     norm, all_g = row_exchange(g, g)

time: 225 us -> 222 us (0.987)
  blocking collectives: 71.8 us -> 79.4 us
  waiting for transfers between devices: 56.8 us -> 52.3 us
  starting transfers between devices: 46.6 us -> 42.2 us
    all_to_all x1, waiting for transfers between devices: 0.01 us -> 15 us  [local(): lax.all_to_all(jnp.broadcast_to(own[None], (4, 4, 256, 256)).reshape(4, 1...]
    ppermute x20, waiting for transfers between devices: 27.5 us -> 13.6 us  [send(): return lax.ppermute(values, AXES, where)]
    all_to_all x4 -> x5, blocking collectives: 39.5 us -> 47.1 us  [spread(): lax.all_to_all(copies, AXES, 0, 0, tiled=True, axis_index_groups=groups(s...]
    all_to_all x5 -> x4, waiting for transfers between devices: 24.5 us -> 19.9 us  [spread(): lax.all_to_all(copies, AXES, 0, 0, tiled=True, axis_index_groups=groups(s...]
    all_to_all x5 -> x4, starting transfers between devices: 17.8 us -> 14.7 us  [spread(): lax.all_to_all(copies, AXES, 0, 0, tiled=True, axis_index_groups=groups(s...]
  transfers between devices with their start and end apart: 27 -> 26, of which waited for: 12 -> 11; matrix products, arithmetic and copies ran while one was open for 4% -> 4% of each run, Pallas kernels for 7% -> 7%
where the time goes in v5:
time: 222 us; the launch traced here: 221 us
  blocking collectives  79.4 us (36%)
  waiting for transfers between devices  52.3 us (24%)
  starting transfers between devices  42.2 us (19%)
  Pallas kernels  25.3 us (11%)
  other arithmetic  10.8 us (5%)
  local copies, waits for them, and re-layouts  9.79 us (4%)
    all_to_all x5, blocking collectives, spread(): lax.all_to_all(copies, AXES, 0, 0, tiled=True, axis_index_groups=groups(s...  47.1 us
    all_to_all x1, blocking collectives, local(): shares = lax.all_to_all(shares, 'col', 0, 0, tiled=True)  32.3 us
    all_to_all x4, waiting for transfers between devices, spread(): lax.all_to_all(copies, AXES, 0, 0, tiled=True, axis_index_groups=groups(s...  19.9 us
    ppermute x20, starting transfers between devices, send(): return lax.ppermute(values, AXES, where)  18.5 us
    pallas_call x3, Pallas kernels, gram_of(): pl.pallas_call(functools.partial(gram_kernel, pieces, sides, before is No...  16 us
    all_to_all x1, waiting for transfers between devices, local(): lax.all_to_all(jnp.broadcast_to(own[None], (4, 4, 256, 256)).reshape(4, 1...  15 us
    all_to_all x4, starting transfers between devices, spread(): lax.all_to_all(copies, AXES, 0, 0, tiled=True, axis_index_groups=groups(s...  14.7 us
    ppermute x20, waiting for transfers between devices, send(): return lax.ppermute(values, AXES, where)  13.6 us
  transfers between devices with their start and end apart: 26, of which 11 were waited for; matrix products, arithmetic and copies ran while one was open for 4% of the time, Pallas kernels for 7%

profile of v5, /device:TPU:0, one launch (start us, length us, event | category | flops | bytes accessed | tf_op | source)
XLA Modules:
  0.0 221.1 jit_solution(10424079350724773566)
XLA Ops:
  0.7 4.6 %all-to-all-start = ((bf16[4,256,256]{1,2,0:T(8,128)(2,1)}), bf16[4,256,256]{1,2,0:T(8,128)(2,1)S(1)}, u32[]{:S(2)}, u32[]{:S(2)}) async-start(bf16[4,256,256]{1,2,0:T(8,128)(2,1)} %bitcast.75), calls=%async_computation | async-start | bytes 1048576 | tf_op jit(solution)/shard_map/all_to_all | solution.py:223
  6.4 2.0 collective-permute-start.1
  8.4 2.2 collective-permute-start.2
  10.6 1.8 collective-permute-start.3
  12.4 3.8 %all-to-all-done = bf16[4,256,256]{1,2,0:T(8,128)(2,1)S(1)} async-done(((bf16[4,256,256]{1,2,0:T(8,128)(2,1)}), bf16[4,256,256]{1,2,0:T(8,128)(2,1)S(1)}, u32[]{:S(2)}, u32[]{:S(2)}) %all-to-all-start) | async-done | bytes 524320 | tf_op jit(solution)/shard_map/all_to_all | solution.py:223
  16.4 1.5 broadcast_in_dim.23
  17.9 4.4 %all-to-all-start.1 = ((bf16[4,1024,256]{2,1,0:T(8,128)(2,1)}), bf16[4,1024,256]{2,1,0:T(8,128)(2,1)}, u32[]{:S(2)}, u32[]{:S(2)}) async-start(bf16[4,1024,256]{2,1,0:T(8,128)(2,1)} %broadcast_in_dim.23), calls=%async_computation.1 | async-start | bytes 4194304 | tf_op jit(solution)/shard_map/all_to_all | solution.py:226
  23.1 1.7 collective-permute-done.3
  26.1 3.3 %collective-permute-start.5 = (bf16[512,1024]{1,0:T(8,128)(2,1)S(1)}, bf16[512,1024]{1,0:T(8,128)(2,1)}, u32[]{:S(2)}, u32[]{:S(2)}) collective-permute-start(bf16[512,1024]{1,0:T(8,128)(2,1)S(1)} %constant_dynamic-update-slice_fusion.refs_2_.refs_1_), channel_id=1, source_target_pairs={{0,12},{1,13},{2,14},{3,15},{4,0},{5,1},{6,2},{7,3},{8,4},{9,5},{1... | collective-permute-start | bytes 3145736 | tf_op jit(solution)/shard_map/ppermute | solution.py:44
  30.3 2.5 %collective-permute-start.6 = (bf16[512,1024]{1,0:T(8,128)(2,1)S(1)}, bf16[512,1024]{1,0:T(8,128)(2,1)}, u32[]{:S(2)}, u32[]{:S(2)}) collective-permute-start(bf16[512,1024]{1,0:T(8,128)(2,1)S(1)} %pad_maximum_fusion.refs_1_.refs_0_), channel_id=1, source_target_pairs={{0,12},{1,13},{2,14},{3,15},{4,0},{5,1},{6,2},{7,3},{8,4},{9,5},{1... | collective-permute-start | bytes 3145736 | tf_op jit(solution)/shard_map/ppermute | solution.py:44
  32.8 15.0 %all-to-all-done.1 = bf16[4,1024,256]{2,1,0:T(8,128)(2,1)} async-done(((bf16[4,1024,256]{2,1,0:T(8,128)(2,1)}), bf16[4,1024,256]{2,1,0:T(8,128)(2,1)}, u32[]{:S(2)}, u32[]{:S(2)}) %all-to-all-start.1) | async-done | bytes 2097184 | tf_op jit(solution)/shard_map/all_to_all | solution.py:226
  47.8 8.9 %collective-permute-done.4.refs_5_.refs_4_ = bf16[512,1024]{1,0:T(8,128)(2,1)} collective-permute-done((bf16[512,1024]{1,0:T(8,128)(2,1)S(1)}, bf16[512,1024]{1,0:T(8,128)(2,1)}, u32[]{:S(2)}, u32[]{:S(2)}) %collective-permute-start.4) | collective-permute-done | bytes 1048608 | tf_op jit(solution)/shard_map/ppermute | solution.py:44
  61.7 5.6 %shard_map.49 = (f32[1024,512]{1,0:T(8,128)S(1)}, f32[1024,128]{1,0:T(8,128)S(1)}, f32[8,512]{1,0:T(8,128)S(1)}) custom-call(s32[4]{0:T(128)S(1)} %pad_add_fusion.place, bf16[16,256,256]{2,1,0:T(8,128)(2,1)} %bitcast.10.refs_0_, bf16[512,1024]{1,0:T(8,128)(2,1)S(1)} %pad_maximum_fusion.refs_1_.refs_0_, bf16[512,1024]{1,0:T(8,128)(2,1)S(1)} %copy-done.1, ...), custom_call_target="tpu_custom_call" | custom-call | flops 1610612736 | bytes 14680064 | tf_op jit(solution)/shard_map/pallas_call | solution.py:125
  67.4 5.1 %shard_map.50 = (f32[1024,512]{1,0:T(8,128)S(1)}, f32[1024,128]{1,0:T(8,128)S(1)}, f32[8,512]{1,0:T(8,128)S(1)}) custom-call(s32[4]{0:T(128)S(1)} %pad_add_fusion.place, bf16[16,256,256]{2,1,0:T(8,128)(2,1)} %collective-permute-done.8.refs_0_.refs_1_, ...), custom_call_target="tpu_custom_call", output_to_operand_aliasing={{0}: (8, {}), {1}: (9, {}), {2}: (10, {})} | custom-call | flops 1610612736 | bytes 14680064 | tf_op jit(solution)/shard_map/pallas_call | solution.py:125
  73.3 2.0 collective-permute-done.9.refs_2_.refs_6_
  75.3 5.2 %shard_map.51 = (f32[1024,512]{1,0:T(8,128)S(1)}, f32[1024,128]{1,0:T(8,128)S(1)}, f32[8,512]{1,0:T(8,128)S(1)}) custom-call(s32[4]{0:T(128)S(1)} %pad_add_fusion.place, bf16[16,256,256]{2,1,0:T(8,128)(2,1)} %bitcast.10.refs_0_, ...), custom_call_target="tpu_custom_call", output_to_operand_aliasing={{0}: (5, {}), {1}: (6, {}), {2}: (7, {})} | custom-call | flops 1073741824 | bytes 10485760 | tf_op jit(solution)/shard_map/pallas_call | solution.py:125
  81.8 4.3 %all-to-all-start.2 = ((f32[8,1,512]{2,1,0:T(1,128)}), f32[8,1,512]{2,1,0:T(1,128)S(1)}, u32[]{:S(2)}, u32[]{:S(2)}) async-start(f32[8,1,512]{2,1,0:T(1,128)} %broadcast_in_dim.24), calls=%async_computation.2 | async-start | bytes 32768 | tf_op jit(solution)/shard_map/all_to_all | solution.py:49
  87.6 3.7 %all-to-all-done.2 = f32[8,1,512]{2,1,0:T(1,128)S(1)} async-done(((f32[8,1,512]{2,1,0:T(1,128)}), f32[8,1,512]{2,1,0:T(1,128)S(1)}, u32[]{:S(2)}, u32[]{:S(2)}) %all-to-all-start.2) | async-done | bytes 16416 | tf_op jit(solution)/shard_map/all_to_all | solution.py:49
  92.3 10.2 %all_to_all.60 = f32[16,1,1024]{2,1,0:T(1,128)S(1)} all-to-all(f32[16,1,1024]{2,1,0:T(1,128)S(1)} %broadcast_in_dim.25), channel_id=1, replica_groups={{0,4,8,12,32,36,40,44,64,68,72,76,96,100,104,108},{1,5,9,13,33,37,41,45..., dimensions={0} | all-to-all | bytes 131072 | tf_op jit(solution)/shard_map/all_to_all | solution.py:49
  104.0 3.3 %all-to-all-start.4 = ((f32[8,1,512]{2,1,0:T(1,128)}), f32[8,1,512]{2,1,0:T(1,128)S(1)}, u32[]{:S(2)}, u32[]{:S(2)}) async-start(f32[8,1,512]{2,1,0:T(1,128)} %broadcast_in_dim.26), calls=%async_computation.4 | async-start | bytes 32768 | tf_op jit(solution)/shard_map/all_to_all | solution.py:49
  108.4 4.1 %all-to-all-done.4 = f32[8,1,512]{2,1,0:T(1,128)S(1)} async-done(((f32[8,1,512]{2,1,0:T(1,128)}), f32[8,1,512]{2,1,0:T(1,128)S(1)}, u32[]{:S(2)}, u32[]{:S(2)}) %all-to-all-start.4) | async-done | bytes 16416 | tf_op jit(solution)/shard_map/all_to_all | solution.py:49
  113.4 10.8 %all_to_all.61 = f32[16,1,1024]{2,1,0:T(1,128)S(1)} all-to-all(f32[16,1,1024]{2,1,0:T(1,128)S(1)} %broadcast_in_dim.27), channel_id=1, replica_groups={{0,4,8,12,32,36,40,44,64,68,72,76,96,100,104,108},{1,5,9,13,33,37,41,45..., dimensions={0} | all-to-all | bytes 131072 | tf_op jit(solution)/shard_map/all_to_all | solution.py:49
  125.1 7.6 %all_to_all.62 = f32[8,1,512]{2,1,0:T(1,128)S(1)} all-to-all(f32[8,1,512]{2,1,0:T(1,128)S(1)} %broadcast_in_dim.28), channel_id=1, replica_groups={{0,1,2,3,16,17,18,19},{4,5,6,7,20,21,22,23},{8,9,10,11,24,25,26,27},{12..., dimensions={0} | all-to-all | bytes 32768 | tf_op jit(solution)/shard_map/all_to_all | solution.py:49
  133.7 10.8 %all_to_all.63 = f32[16,1,1024]{2,1,0:T(1,128)S(1)} all-to-all(f32[16,1,1024]{2,1,0:T(1,128)S(1)} %broadcast_in_dim.29), channel_id=1, replica_groups={{0,4,8,12,32,36,40,44,64,68,72,76,96,100,104,108},{1,5,9,13,33,37,41,45..., dimensions={0} | all-to-all | bytes 131072 | tf_op jit(solution)/shard_map/all_to_all | solution.py:49
  145.3 7.6 %all_to_all.64 = f32[8,1,512]{2,1,0:T(1,128)S(1)} all-to-all(f32[8,1,512]{2,1,0:T(1,128)S(1)} %broadcast_in_dim.30), channel_id=1, replica_groups={{0,1,2,3,16,17,18,19},{4,5,6,7,20,21,22,23},{8,9,10,11,24,25,26,27},{12..., dimensions={0} | all-to-all | bytes 32768 | tf_op jit(solution)/shard_map/all_to_all | solution.py:49
  154.5 3.7 %all-to-all-start.9 = ((f32[16,1,1536]{2,1,0:T(1,128)}), f32[16,1,1536]{2,1,0:T(1,128)S(1)}, u32[]{:S(2)}, u32[]{:S(2)}) async-start(f32[16,1,1536]{2,1,0:T(1,128)} %broadcast_in_dim.31), calls=%async_computation.9 | async-start | bytes 196608 | tf_op jit(solution)/shard_map/all_to_all | solution.py:49
  158.3 7.5 %all-to-all-done.9 = f32[16,1,1536]{2,1,0:T(1,128)S(1)} async-done(((f32[16,1,1536]{2,1,0:T(1,128)}), f32[16,1,1536]{2,1,0:T(1,128)S(1)}, u32[]{:S(2)}, u32[]{:S(2)}) %all-to-all-start.9) | async-done | bytes 98336 | tf_op jit(solution)/shard_map/all_to_all | solution.py:49
  167.2 3.3 %all-to-all-start.10 = ((f32[8,1,1536]{2,1,0:T(1,128)}), f32[8,1,1536]{2,1,0:T(1,128)S(1)}, u32[]{:S(2)}, u32[]{:S(2)}) async-start(f32[8,1,1536]{2,1,0:T(1,128)} %broadcast_in_dim.32), calls=%async_computation.10 | async-start | bytes 98304 | tf_op jit(solution)/shard_map/all_to_all | solution.py:49
  171.3 4.6 %all-to-all-done.10 = f32[8,1,1536]{2,1,0:T(1,128)S(1)} async-done(((f32[8,1,1536]{2,1,0:T(1,128)}), f32[8,1,1536]{2,1,0:T(1,128)S(1)}, u32[]{:S(2)}, u32[]{:S(2)}) %all-to-all-start.10) | async-done | bytes 49184 | tf_op jit(solution)/shard_map/all_to_all | solution.py:49
  176.7 1.6 exponential_convert_fusion
  178.3 9.3 %shard_map.52 = bf16[16,256,256]{2,1,0:T(8,128)(2,1)} custom-call(s32[4]{0:T(128)S(1)} %pad_add_fusion.place, bf16[1024,256]{1,0:T(8,128)(2,1)S(1)} %get-tuple-element.62.my_weights, bf16[1024,256]{1,0:T(8,128)(2,1)S(1)} %get-tuple-element.61.other_weights, bf16[512,1024]{1,0:T(8,128)(2,1)S(1)} %pad_maximum_fusion.refs_1_.refs_0_, ...), custom_call_target="tpu_custom_call" | custom-call | flops 4294967296 | bytes 20971520 | tf_op jit(solution)/shard_map/pallas_call | solution.py:190
  187.6 32.3 %all_to_all.65 = bf16[16,256,256]{2,1,0:T(8,128)(2,1)S(1)} all-to-all(bf16[16,256,256]{2,1,0:T(8,128)(2,1)} %shard_map.52), channel_id=1, replica_groups=mesh['row'=8,'col'=16] {'col'}, dimensions={0} | all-to-all | bytes 4194304 | tf_op jit(solution)/shard_map/all_to_all | solution.py:292
  (127 shorter events, 25.2 us)
Async XLA Ops:
  0.6 5.6 %collective-permute-start = (bf16[2,256,512]{2,1,0:T(8,128)(2,1)}, bf16[2,256,512]{2,1,0:T(8,128)(2,1)S(1)}, u32[]{:S(2)}, u32[]{:S(2)}) collective-permute-start(bf16[2,256,512]{2,1,0:T(8,128)(2,1)} %bitcast.79), channel_id=1, source_target_pairs={{0,16},{1,17},{2,18},{3,19},{4,20},{5,21},{6,22},{7,23},{8,24},{9,... | collective-permute-start | bytes 1572872 | tf_op jit(solution)/shard_map/ppermute | solution.py:44
  0.7 15.5 %all-to-all-start = ((bf16[4,256,256]{1,2,0:T(8,128)(2,1)}), bf16[4,256,256]{1,2,0:T(8,128)(2,1)S(1)}, u32[]{:S(2)}, u32[]{:S(2)}) async-start(bf16[4,256,256]{1,2,0:T(8,128)(2,1)} %bitcast.75), calls=%async_computation | async-start | bytes 1048576 | tf_op jit(solution)/shard_map/all_to_all | solution.py:223
  6.4 15.9 %collective-permute-start.1 = (bf16[256,1024]{1,0:T(8,128)(2,1)S(1)}, bf16[256,1024]{1,0:T(8,128)(2,1)S(1)}, u32[]{:S(2)}, u32[]{:S(2)}) collective-permute-start(bf16[256,1024]{1,0:T(8,128)(2,1)S(1)} %maximum_select_fusion), channel_id=1, source_target_pairs={{0,32},{1,33},{2,34},{3,35},{4,36},{5,37},{6,38},{7,39},{8,40},{9,... | collective-permute-start | bytes 1572872 | tf_op jit(solution)/shard_map/ppermute | solution.py:44
  8.4 14.6 %collective-permute-start.2 = (bf16[256,1024]{1,0:T(8,128)(2,1)S(1)}, bf16[256,1024]{1,0:T(8,128)(2,1)S(1)}, u32[]{:S(2)}, u32[]{:S(2)}) collective-permute-start(bf16[256,1024]{1,0:T(8,128)(2,1)S(1)} %maximum_select_fusion), channel_id=1, source_target_pairs={{0,96},{1,97},{2,98},{3,99},{4,100},{5,101},{6,102},{7,103},{8,104... | collective-permute-start | bytes 1572872 | tf_op jit(solution)/shard_map/ppermute | solution.py:44
  10.6 14.3 %collective-permute-start.3 = (bf16[256,1024]{1,0:T(8,128)(2,1)S(1)}, bf16[256,1024]{1,0:T(8,128)(2,1)}, u32[]{:S(2)}, u32[]{:S(2)}) collective-permute-start(bf16[256,1024]{1,0:T(8,128)(2,1)S(1)} %maximum_select_fusion), channel_id=1, source_target_pairs={{0,64},{1,65},{2,66},{3,67},{4,68},{5,69},{6,70},{7,71},{8,72},{9,... | collective-permute-start | bytes 1572872 | tf_op jit(solution)/shard_map/ppermute | solution.py:44
  17.9 29.9 %all-to-all-start.1 = ((bf16[4,1024,256]{2,1,0:T(8,128)(2,1)}), bf16[4,1024,256]{2,1,0:T(8,128)(2,1)}, u32[]{:S(2)}, u32[]{:S(2)}) async-start(bf16[4,1024,256]{2,1,0:T(8,128)(2,1)} %broadcast_in_dim.23), calls=%async_computation.1 | async-start | bytes 4194304 | tf_op jit(solution)/shard_map/all_to_all | solution.py:226
  22.3 0.8 copy-start.3
  24.9 4.5 %copy-start.4 = (bf16[256,1024]{1,0:T(8,128)(2,1)S(1)}, bf16[256,1024]{1,0:T(8,128)(2,1)}, u32[]{:S(2)}) copy-start(bf16[256,1024]{1,0:T(8,128)(2,1)} %copy-done.3) | copy-start | bytes 1572868
  26.1 33.9 %copy-start = (bf16[512,1024]{1,0:T(8,128)(2,1)}, bf16[512,1024]{1,0:T(8,128)(2,1)S(1)}, u32[]{:S(2)}) copy-start(bf16[512,1024]{1,0:T(8,128)(2,1)S(1)} %constant_dynamic-update-slice_fusion.refs_2_.refs_1_) | copy-start | bytes 3145732
  26.1 21.8 %collective-permute-start.5 = (bf16[512,1024]{1,0:T(8,128)(2,1)S(1)}, bf16[512,1024]{1,0:T(8,128)(2,1)}, u32[]{:S(2)}, u32[]{:S(2)}) collective-permute-start(bf16[512,1024]{1,0:T(8,128)(2,1)S(1)} %constant_dynamic-update-slice_fusion.refs_2_.refs_1_), channel_id=1, source_target_pairs={{0,12},{1,13},{2,14},{3,15},{4,0},{5,1},{6,2},{7,3},{8,4},{9,5},{1... | collective-permute-start | bytes 3145736 | tf_op jit(solution)/shard_map/ppermute | solution.py:44
  29.4 18.5 %collective-permute-start.7 = (bf16[512,1024]{1,0:T(8,128)(2,1)S(1)}, bf16[512,1024]{1,0:T(8,128)(2,1)}, u32[]{:S(2)}, u32[]{:S(2)}) collective-permute-start(bf16[512,1024]{1,0:T(8,128)(2,1)S(1)} %constant_dynamic-update-slice_fusion.refs_2_.refs_1_), channel_id=1, source_target_pairs={{0,4},{1,5},{2,6},{3,7},{4,8},{5,9},{6,10},{7,11},{8,12},{9,13},{1... | collective-permute-start | bytes 3145736 | tf_op jit(solution)/shard_map/ppermute | solution.py:44
  29.4 27.3 %collective-permute-start.4 = (bf16[512,1024]{1,0:T(8,128)(2,1)S(1)}, bf16[512,1024]{1,0:T(8,128)(2,1)}, u32[]{:S(2)}, u32[]{:S(2)}) collective-permute-start(bf16[512,1024]{1,0:T(8,128)(2,1)S(1)} %pad_maximum_fusion.refs_1_.refs_0_), channel_id=1, source_target_pairs={{0,4},{1,5},{2,6},{3,7},{4,8},{5,9},{6,10},{7,11},{8,12},{9,13},{1... | collective-permute-start | bytes 3145736 | tf_op jit(solution)/shard_map/ppermute | solution.py:44
  30.3 26.4 %collective-permute-start.6 = (bf16[512,1024]{1,0:T(8,128)(2,1)S(1)}, bf16[512,1024]{1,0:T(8,128)(2,1)}, u32[]{:S(2)}, u32[]{:S(2)}) collective-permute-start(bf16[512,1024]{1,0:T(8,128)(2,1)S(1)} %pad_maximum_fusion.refs_1_.refs_0_), channel_id=1, source_target_pairs={{0,12},{1,13},{2,14},{3,15},{4,0},{5,1},{6,2},{7,3},{8,4},{9,5},{1... | collective-permute-start | bytes 3145736 | tf_op jit(solution)/shard_map/ppermute | solution.py:44
  56.7 10.6 %collective-permute-start.8 = (bf16[16,256,256]{2,1,0:T(8,128)(2,1)}, bf16[16,256,256]{2,1,0:T(8,128)(2,1)}, u32[]{:S(2)}, u32[]{:S(2)}) collective-permute-start(bf16[16,256,256]{2,1,0:T(8,128)(2,1)} %bitcast.10.refs_0_), channel_id=1, source_target_pairs={{0,16},{1,17},{2,18},{3,19},{4,20},{5,21},{6,22},{7,23},{8,24},{9,... | collective-permute-start | bytes 6291464 | tf_op jit(solution)/shard_map/ppermute | solution.py:44
  57.8 15.1 %collective-permute-start.10 = (bf16[512,1024]{1,0:T(8,128)(2,1)}, bf16[512,1024]{1,0:T(8,128)(2,1)}, u32[]{:S(2)}, u32[]{:S(2)}) collective-permute-start(bf16[512,1024]{1,0:T(8,128)(2,1)} %collective-permute-done.5.refs_6_.refs_5_), channel_id=1, source_target_pairs={{0,12},{1,13},{2,14},{3,15},{4,0},{5,1},{6,2},{7,3},{8,4},{9,5},{1... | collective-permute-start | bytes 3145736 | tf_op jit(solution)/shard_map/ppermute | solution.py:44
  59.0 16.3 %collective-permute-start.9 = (bf16[512,1024]{1,0:T(8,128)(2,1)}, bf16[512,1024]{1,0:T(8,128)(2,1)}, u32[]{:S(2)}, u32[]{:S(2)}) collective-permute-start(bf16[512,1024]{1,0:T(8,128)(2,1)} %collective-permute-done.4.refs_5_.refs_4_), channel_id=1, source_target_pairs={{0,4},{1,5},{2,6},{3,7},{4,8},{5,9},{6,10},{7,11},{8,12},{9,13},{1... | collective-permute-start | bytes 3145736 | tf_op jit(solution)/shard_map/ppermute | solution.py:44
  59.9 42.7 %collective-permute-start.12 = (bf16[512,1024]{1,0:T(8,128)(2,1)}, bf16[512,1024]{1,0:T(8,128)(2,1)}, u32[]{:S(2)}, u32[]{:S(2)}) collective-permute-start(bf16[512,1024]{1,0:T(8,128)(2,1)} %collective-permute-done.6.refs_3_.refs_2_), channel_id=1, source_target_pairs={{0,16},{1,17},{2,18},{3,19},{4,20},{5,21},{6,22},{7,23},{8,24},{9,... | collective-permute-start | bytes 3145736 | tf_op jit(solution)/shard_map/ppermute | solution.py:44
  60.0 42.7 %collective-permute-start.13 = (bf16[512,1024]{1,0:T(8,128)(2,1)}, bf16[512,1024]{1,0:T(8,128)(2,1)}, u32[]{:S(2)}, u32[]{:S(2)}) collective-permute-start(bf16[512,1024]{1,0:T(8,128)(2,1)} %collective-permute-done.7.refs_4_.refs_3_), channel_id=1, source_target_pairs={{0,16},{1,17},{2,18},{3,19},{4,20},{5,21},{6,22},{7,23},{8,24},{9,... | collective-permute-start | bytes 3145736 | tf_op jit(solution)/shard_map/ppermute | solution.py:44
  60.5 1.2 copy-start.1
  67.3 35.3 %collective-permute-start.14 = (bf16[512,1024]{1,0:T(8,128)(2,1)}, bf16[512,1024]{1,0:T(8,128)(2,1)}, u32[]{:S(2)}, u32[]{:S(2)}) collective-permute-start(bf16[512,1024]{1,0:T(8,128)(2,1)} %collective-permute-done.4.refs_5_.refs_4_), channel_id=1, source_target_pairs={{0,16},{1,17},{2,18},{3,19},{4,20},{5,21},{6,22},{7,23},{8,24},{9,... | collective-permute-start | bytes 3145736 | tf_op jit(solution)/shard_map/ppermute | solution.py:44
  72.9 29.7 %collective-permute-start.15 = (bf16[512,1024]{1,0:T(8,128)(2,1)}, bf16[512,1024]{1,0:T(8,128)(2,1)}, u32[]{:S(2)}, u32[]{:S(2)}) collective-permute-start(bf16[512,1024]{1,0:T(8,128)(2,1)} %collective-permute-done.5.refs_6_.refs_5_), channel_id=1, source_target_pairs={{0,16},{1,17},{2,18},{3,19},{4,20},{5,21},{6,22},{7,23},{8,24},{9,... | collective-permute-start | bytes 3145736 | tf_op jit(solution)/shard_map/ppermute | solution.py:44
  81.8 9.6 %all-to-all-start.2 = ((f32[8,1,512]{2,1,0:T(1,128)}), f32[8,1,512]{2,1,0:T(1,128)S(1)}, u32[]{:S(2)}, u32[]{:S(2)}) async-start(f32[8,1,512]{2,1,0:T(1,128)} %broadcast_in_dim.24), calls=%async_computation.2 | async-start | bytes 32768 | tf_op jit(solution)/shard_map/all_to_all | solution.py:49
  87.1 15.5 %collective-permute-start.11 = (f32[1024,256]{1,0:T(8,128)}, f32[1024,256]{1,0:T(8,128)}, u32[]{:S(2)}, u32[]{:S(2)}) collective-permute-start(f32[1024,256]{1,0:T(8,128)} %constant_dynamic-slice_fusion.1), channel_id=1, source_target_pairs={{0,16},{1,17},{2,18},{3,19},{4,20},{5,21},{6,22},{7,23},{8,24},{9,... | collective-permute-start | bytes 3145736 | tf_op jit(solution)/shard_map/ppermute | solution.py:44
  104.0 8.5 %all-to-all-start.4 = ((f32[8,1,512]{2,1,0:T(1,128)}), f32[8,1,512]{2,1,0:T(1,128)S(1)}, u32[]{:S(2)}, u32[]{:S(2)}) async-start(f32[8,1,512]{2,1,0:T(1,128)} %broadcast_in_dim.26), calls=%async_computation.4 | async-start | bytes 32768 | tf_op jit(solution)/shard_map/all_to_all | solution.py:49
  107.3 17.1 %collective-permute-start.19 = (bf16[512,1024]{1,0:T(8,128)(2,1)}, bf16[512,1024]{1,0:T(8,128)(2,1)}, u32[]{:S(2)}, u32[]{:S(2)}) collective-permute-start(bf16[512,1024]{1,0:T(8,128)(2,1)} %copy-done), channel_id=1, source_target_pairs={{0,16},{1,17},{2,18},{3,19},{4,20},{5,21},{6,22},{7,23},{8,24},{9,... | collective-permute-start | bytes 3145736 | tf_op jit(solution)/shard_map/ppermute | solution.py:44
  107.7 16.7 %collective-permute-start.18 = (bf16[512,1024]{1,0:T(8,128)(2,1)S(1)}, bf16[512,1024]{1,0:T(8,128)(2,1)}, u32[]{:S(2)}, u32[]{:S(2)}) collective-permute-start(bf16[512,1024]{1,0:T(8,128)(2,1)S(1)} %pad_maximum_fusion.refs_1_.refs_0_), channel_id=1, source_target_pairs={{0,16},{1,17},{2,18},{3,19},{4,20},{5,21},{6,22},{7,23},{8,24},{9,... | collective-permute-start | bytes 3145736 | tf_op jit(solution)/shard_map/ppermute | solution.py:44
  107.9 16.5 %collective-permute-start.16 = (bf16[512,1024]{1,0:T(8,128)(2,1)}, bf16[512,1024]{1,0:T(8,128)(2,1)}, u32[]{:S(2)}, u32[]{:S(2)}) collective-permute-start(bf16[512,1024]{1,0:T(8,128)(2,1)} %collective-permute-done.9.refs_2_.refs_6_), channel_id=1, source_target_pairs={{0,16},{1,17},{2,18},{3,19},{4,20},{5,21},{6,22},{7,23},{8,24},{9,... | collective-permute-start | bytes 3145736 | tf_op jit(solution)/shard_map/ppermute | solution.py:44
  108.2 16.2 %collective-permute-start.17 = (bf16[512,1024]{1,0:T(8,128)(2,1)}, bf16[512,1024]{1,0:T(8,128)(2,1)}, u32[]{:S(2)}, u32[]{:S(2)}) collective-permute-start(bf16[512,1024]{1,0:T(8,128)(2,1)} %collective-permute-done.10.refs_3_.refs_7_), channel_id=1, source_target_pairs={{0,16},{1,17},{2,18},{3,19},{4,20},{5,21},{6,22},{7,23},{8,24},{9,... | collective-permute-start | bytes 3145736 | tf_op jit(solution)/shard_map/ppermute | solution.py:44
  154.5 11.3 %all-to-all-start.9 = ((f32[16,1,1536]{2,1,0:T(1,128)}), f32[16,1,1536]{2,1,0:T(1,128)S(1)}, u32[]{:S(2)}, u32[]{:S(2)}) async-start(f32[16,1,1536]{2,1,0:T(1,128)} %broadcast_in_dim.31), calls=%async_computation.9 | async-start | bytes 196608 | tf_op jit(solution)/shard_map/all_to_all | solution.py:49
  167.2 8.6 %all-to-all-start.10 = ((f32[8,1,1536]{2,1,0:T(1,128)}), f32[8,1,1536]{2,1,0:T(1,128)S(1)}, u32[]{:S(2)}, u32[]{:S(2)}) async-start(f32[8,1,1536]{2,1,0:T(1,128)} %broadcast_in_dim.32), calls=%async_computation.10 | async-start | bytes 98304 | tf_op jit(solution)/shard_map/all_to_all | solution.py:49
  176.0 2.3 %copy-start.2 = (bf16[512,1024]{1,0:T(8,128)(2,1)S(1)}, bf16[512,1024]{1,0:T(8,128)(2,1)}, u32[]{:S(2)}) copy-start(bf16[512,1024]{1,0:T(8,128)(2,1)} %copy-done) | copy-start | bytes 3145732

commit v6 on v5

--- a/solution.py
+++ b/solution.py
@@ -273,6 +273,8 @@
             queue = [scores_away, *arrays[2:], *arrays[:2]][(0, 5, 9)[step] : (5, 9, 9)[step]]
             g, *queue = lax.optimization_barrier((g, *[send(values, OTHER) for values in queue]))
             received += queue
+        if step == 0:
+            g, my_scores = lax.optimization_barrier((g, my_scores))
     norm, all_g = row_exchange(g, g)
     all_g = lax.dynamic_index_in_dim(all_g.reshape(2, 4, 1024), x, 1, keepdims=False)
     g_other = lax.dynamic_index_in_dim(all_g, 1 - c, 0, keepdims=False)

time: 222 us -> 222 us (level)
  no operation moved by 1% of the time
where the time goes in v6:
time: 222 us; the launch traced here: 221 us
  blocking collectives  79.4 us (36%)
  waiting for transfers between devices  52 us (23%)
  starting transfers between devices  42.2 us (19%)
  Pallas kernels  25.4 us (11%)
  other arithmetic  11.2 us (5%)
  local copies, waits for them, and re-layouts  10.1 us (5%)
    all_to_all x5, blocking collectives, spread(): lax.all_to_all(copies, AXES, 0, 0, tiled=True, axis_index_groups=groups(s...  47.1 us
    all_to_all x1, blocking collectives, local(): shares = lax.all_to_all(shares, 'col', 0, 0, tiled=True)  32.3 us
    all_to_all x4, waiting for transfers between devices, spread(): lax.all_to_all(copies, AXES, 0, 0, tiled=True, axis_index_groups=groups(s...  19.4 us
    ppermute x20, starting transfers between devices, send(): return lax.ppermute(values, AXES, where)  18.5 us
    pallas_call x3, Pallas kernels, gram_of(): pl.pallas_call(functools.partial(gram_kernel, pieces, sides, before is No...  16 us
    all_to_all x1, waiting for transfers between devices, local(): lax.all_to_all(jnp.broadcast_to(own[None], (4, 4, 256, 256)).reshape(4, 1...  14.9 us
    all_to_all x4, starting transfers between devices, spread(): lax.all_to_all(copies, AXES, 0, 0, tiled=True, axis_index_groups=groups(s...  14.7 us
    ppermute x20, waiting for transfers between devices, send(): return lax.ppermute(values, AXES, where)  13.9 us
  transfers between devices with their start and end apart: 26, of which 11 were waited for; matrix products, arithmetic and copies ran while one was open for 4% of the time, Pallas kernels for 7%

profile of v6, /device:TPU:0, one launch (start us, length us, event | category | flops | bytes accessed | tf_op | source)
XLA Modules:
  0.0 221.5 jit_solution(13487144094251652753)
XLA Ops:
  0.7 4.6 %all-to-all-start = ((bf16[4,256,256]{1,2,0:T(8,128)(2,1)}), bf16[4,256,256]{1,2,0:T(8,128)(2,1)S(1)}, u32[]{:S(2)}, u32[]{:S(2)}) async-start(bf16[4,256,256]{1,2,0:T(8,128)(2,1)} %bitcast.75), calls=%async_computation | async-start | bytes 1048576 | tf_op jit(solution)/shard_map/all_to_all | solution.py:223
  6.4 2.0 collective-permute-start.1
  8.4 2.2 collective-permute-start.2
  10.6 1.8 collective-permute-start.3
  12.4 3.8 %all-to-all-done = bf16[4,256,256]{1,2,0:T(8,128)(2,1)S(1)} async-done(((bf16[4,256,256]{1,2,0:T(8,128)(2,1)}), bf16[4,256,256]{1,2,0:T(8,128)(2,1)S(1)}, u32[]{:S(2)}, u32[]{:S(2)}) %all-to-all-start) | async-done | bytes 524320 | tf_op jit(solution)/shard_map/all_to_all | solution.py:223
  17.8 4.4 %all-to-all-start.1 = ((bf16[4,1024,256]{2,1,0:T(8,128)(2,1)}), bf16[4,1024,256]{2,1,0:T(8,128)(2,1)}, u32[]{:S(2)}, u32[]{:S(2)}) async-start(bf16[4,1024,256]{2,1,0:T(8,128)(2,1)} %broadcast_in_dim.23), calls=%async_computation.1 | async-start | bytes 4194304 | tf_op jit(solution)/shard_map/all_to_all | solution.py:226
  23.1 1.8 collective-permute-done.3
  26.1 3.3 %collective-permute-start.5 = (bf16[512,1024]{1,0:T(8,128)(2,1)S(1)}, bf16[512,1024]{1,0:T(8,128)(2,1)}, u32[]{:S(2)}, u32[]{:S(2)}) collective-permute-start(bf16[512,1024]{1,0:T(8,128)(2,1)S(1)} %constant_dynamic-update-slice_fusion.refs_2_.refs_1_), channel_id=1, source_target_pairs={{0,12},{1,13},{2,14},{3,15},{4,0},{5,1},{6,2},{7,3},{8,4},{9,5},{1... | collective-permute-start | bytes 3145736 | tf_op jit(solution)/shard_map/ppermute | solution.py:44
  30.3 2.5 %collective-permute-start.6 = (bf16[512,1024]{1,0:T(8,128)(2,1)S(1)}, bf16[512,1024]{1,0:T(8,128)(2,1)}, u32[]{:S(2)}, u32[]{:S(2)}) collective-permute-start(bf16[512,1024]{1,0:T(8,128)(2,1)S(1)} %pad_maximum_fusion.refs_1_.refs_0_), channel_id=1, source_target_pairs={{0,12},{1,13},{2,14},{3,15},{4,0},{5,1},{6,2},{7,3},{8,4},{9,5},{1... | collective-permute-start | bytes 3145736 | tf_op jit(solution)/shard_map/ppermute | solution.py:44
  32.8 14.9 %all-to-all-done.1 = bf16[4,1024,256]{2,1,0:T(8,128)(2,1)} async-done(((bf16[4,1024,256]{2,1,0:T(8,128)(2,1)}), bf16[4,1024,256]{2,1,0:T(8,128)(2,1)}, u32[]{:S(2)}, u32[]{:S(2)}) %all-to-all-start.1) | async-done | bytes 2097184 | tf_op jit(solution)/shard_map/all_to_all | solution.py:226
  47.8 9.0 %collective-permute-done.4.refs_5_.refs_4_ = bf16[512,1024]{1,0:T(8,128)(2,1)} collective-permute-done((bf16[512,1024]{1,0:T(8,128)(2,1)S(1)}, bf16[512,1024]{1,0:T(8,128)(2,1)}, u32[]{:S(2)}, u32[]{:S(2)}) %collective-permute-start.4) | collective-permute-done | bytes 1048608 | tf_op jit(solution)/shard_map/ppermute | solution.py:44
  61.7 5.6 %shard_map.49 = (f32[1024,512]{1,0:T(8,128)S(1)}, f32[1024,128]{1,0:T(8,128)S(1)}, f32[8,512]{1,0:T(8,128)S(1)}) custom-call(s32[4]{0:T(128)S(1)} %pad_add_fusion.place, bf16[16,256,256]{2,1,0:T(8,128)(2,1)} %bitcast.10.refs_0_, bf16[512,1024]{1,0:T(8,128)(2,1)S(1)} %pad_maximum_fusion.refs_1_.refs_0_, bf16[512,1024]{1,0:T(8,128)(2,1)S(1)} %copy-done.1, ...), custom_call_target="tpu_custom_call" | custom-call | flops 1610612736 | bytes 14680064 | tf_op jit(solution)/shard_map/pallas_call | solution.py:125
  67.4 5.1 %shard_map.50 = (f32[1024,512]{1,0:T(8,128)S(1)}, f32[1024,128]{1,0:T(8,128)S(1)}, f32[8,512]{1,0:T(8,128)S(1)}) custom-call(s32[4]{0:T(128)S(1)} %pad_add_fusion.place, bf16[16,256,256]{2,1,0:T(8,128)(2,1)} %collective-permute-done.8.refs_0_.refs_1_, ...), custom_call_target="tpu_custom_call", output_to_operand_aliasing={{0}: (8, {}), {1}: (9, {}), {2}: (10, {})} | custom-call | flops 1610612736 | bytes 14680064 | tf_op jit(solution)/shard_map/pallas_call | solution.py:125
  73.3 2.0 collective-permute-done.9.refs_2_.refs_6_
  75.3 5.2 %shard_map.51 = (f32[1024,512]{1,0:T(8,128)S(1)}, f32[1024,128]{1,0:T(8,128)S(1)}, f32[8,512]{1,0:T(8,128)S(1)}) custom-call(s32[4]{0:T(128)S(1)} %pad_add_fusion.place, bf16[16,256,256]{2,1,0:T(8,128)(2,1)} %bitcast.10.refs_0_, ...), custom_call_target="tpu_custom_call", output_to_operand_aliasing={{0}: (5, {}), {1}: (6, {}), {2}: (7, {})} | custom-call | flops 1073741824 | bytes 10485760 | tf_op jit(solution)/shard_map/pallas_call | solution.py:125
  81.8 4.3 %all-to-all-start.2 = ((f32[8,1,512]{2,1,0:T(1,128)}), f32[8,1,512]{2,1,0:T(1,128)S(1)}, u32[]{:S(2)}, u32[]{:S(2)}) async-start(f32[8,1,512]{2,1,0:T(1,128)} %broadcast_in_dim.24), calls=%async_computation.2 | async-start | bytes 32768 | tf_op jit(solution)/shard_map/all_to_all | solution.py:49
  86.1 1.6 constant_dynamic-slice_fusion.1
  88.1 3.2 %all-to-all-done.2 = f32[8,1,512]{2,1,0:T(1,128)S(1)} async-done(((f32[8,1,512]{2,1,0:T(1,128)}), f32[8,1,512]{2,1,0:T(1,128)S(1)}, u32[]{:S(2)}, u32[]{:S(2)}) %all-to-all-start.2) | async-done | bytes 16416 | tf_op jit(solution)/shard_map/all_to_all | solution.py:49
  92.3 10.2 %all_to_all.60 = f32[16,1,1024]{2,1,0:T(1,128)S(1)} all-to-all(f32[16,1,1024]{2,1,0:T(1,128)S(1)} %broadcast_in_dim.25), channel_id=1, replica_groups={{0,4,8,12,32,36,40,44,64,68,72,76,96,100,104,108},{1,5,9,13,33,37,41,45..., dimensions={0} | all-to-all | bytes 131072 | tf_op jit(solution)/shard_map/all_to_all | solution.py:49
  104.0 3.3 %all-to-all-start.4 = ((f32[8,1,512]{2,1,0:T(1,128)}), f32[8,1,512]{2,1,0:T(1,128)S(1)}, u32[]{:S(2)}, u32[]{:S(2)}) async-start(f32[8,1,512]{2,1,0:T(1,128)} %broadcast_in_dim.26), calls=%async_computation.4 | async-start | bytes 32768 | tf_op jit(solution)/shard_map/all_to_all | solution.py:49
  108.4 4.1 %all-to-all-done.4 = f32[8,1,512]{2,1,0:T(1,128)S(1)} async-done(((f32[8,1,512]{2,1,0:T(1,128)}), f32[8,1,512]{2,1,0:T(1,128)S(1)}, u32[]{:S(2)}, u32[]{:S(2)}) %all-to-all-start.4) | async-done | bytes 16416 | tf_op jit(solution)/shard_map/all_to_all | solution.py:49
  113.4 10.8 %all_to_all.61 = f32[16,1,1024]{2,1,0:T(1,128)S(1)} all-to-all(f32[16,1,1024]{2,1,0:T(1,128)S(1)} %broadcast_in_dim.27), channel_id=1, replica_groups={{0,4,8,12,32,36,40,44,64,68,72,76,96,100,104,108},{1,5,9,13,33,37,41,45..., dimensions={0} | all-to-all | bytes 131072 | tf_op jit(solution)/shard_map/all_to_all | solution.py:49
  125.1 7.6 %all_to_all.62 = f32[8,1,512]{2,1,0:T(1,128)S(1)} all-to-all(f32[8,1,512]{2,1,0:T(1,128)S(1)} %broadcast_in_dim.28), channel_id=1, replica_groups={{0,1,2,3,16,17,18,19},{4,5,6,7,20,21,22,23},{8,9,10,11,24,25,26,27},{12..., dimensions={0} | all-to-all | bytes 32768 | tf_op jit(solution)/shard_map/all_to_all | solution.py:49
  133.7 10.8 %all_to_all.63 = f32[16,1,1024]{2,1,0:T(1,128)S(1)} all-to-all(f32[16,1,1024]{2,1,0:T(1,128)S(1)} %broadcast_in_dim.29), channel_id=1, replica_groups={{0,4,8,12,32,36,40,44,64,68,72,76,96,100,104,108},{1,5,9,13,33,37,41,45..., dimensions={0} | all-to-all | bytes 131072 | tf_op jit(solution)/shard_map/all_to_all | solution.py:49
  145.3 7.6 %all_to_all.64 = f32[8,1,512]{2,1,0:T(1,128)S(1)} all-to-all(f32[8,1,512]{2,1,0:T(1,128)S(1)} %broadcast_in_dim.30), channel_id=1, replica_groups={{0,1,2,3,16,17,18,19},{4,5,6,7,20,21,22,23},{8,9,10,11,24,25,26,27},{12..., dimensions={0} | all-to-all | bytes 32768 | tf_op jit(solution)/shard_map/all_to_all | solution.py:49
  154.5 3.7 %all-to-all-start.9 = ((f32[16,1,1536]{2,1,0:T(1,128)}), f32[16,1,1536]{2,1,0:T(1,128)S(1)}, u32[]{:S(2)}, u32[]{:S(2)}) async-start(f32[16,1,1536]{2,1,0:T(1,128)} %broadcast_in_dim.31), calls=%async_computation.9 | async-start | bytes 196608 | tf_op jit(solution)/shard_map/all_to_all | solution.py:49
  158.3 7.5 %all-to-all-done.9 = f32[16,1,1536]{2,1,0:T(1,128)S(1)} async-done(((f32[16,1,1536]{2,1,0:T(1,128)}), f32[16,1,1536]{2,1,0:T(1,128)S(1)}, u32[]{:S(2)}, u32[]{:S(2)}) %all-to-all-start.9) | async-done | bytes 98336 | tf_op jit(solution)/shard_map/all_to_all | solution.py:49
  167.2 3.3 %all-to-all-start.10 = ((f32[8,1,1536]{2,1,0:T(1,128)}), f32[8,1,1536]{2,1,0:T(1,128)S(1)}, u32[]{:S(2)}, u32[]{:S(2)}) async-start(f32[8,1,1536]{2,1,0:T(1,128)} %broadcast_in_dim.32), calls=%async_computation.10 | async-start | bytes 98304 | tf_op jit(solution)/shard_map/all_to_all | solution.py:49
  171.3 4.6 %all-to-all-done.10 = f32[8,1,1536]{2,1,0:T(1,128)S(1)} async-done(((f32[8,1,1536]{2,1,0:T(1,128)}), f32[8,1,1536]{2,1,0:T(1,128)S(1)}, u32[]{:S(2)}, u32[]{:S(2)}) %all-to-all-start.10) | async-done | bytes 49184 | tf_op jit(solution)/shard_map/all_to_all | solution.py:49
  176.7 1.9 exponential_convert_fusion
  178.6 9.4 %shard_map.52 = bf16[16,256,256]{2,1,0:T(8,128)(2,1)} custom-call(s32[4]{0:T(128)S(1)} %pad_add_fusion.place, bf16[1024,256]{1,0:T(8,128)(2,1)S(1)} %get-tuple-element.68.my_weights, bf16[1024,256]{1,0:T(8,128)(2,1)S(1)} %get-tuple-element.67.other_weights, bf16[512,1024]{1,0:T(8,128)(2,1)S(1)} %pad_maximum_fusion.refs_1_.refs_0_, ...), custom_call_target="tpu_custom_call" | custom-call | flops 4294967296 | bytes 20971520 | tf_op jit(solution)/shard_map/pallas_call | solution.py:190
  188.0 32.3 %all_to_all.65 = bf16[16,256,256]{2,1,0:T(8,128)(2,1)S(1)} all-to-all(bf16[16,256,256]{2,1,0:T(8,128)(2,1)} %shard_map.52), channel_id=1, replica_groups=mesh['row'=8,'col'=16] {'col'}, dimensions={0} | all-to-all | bytes 4194304 | tf_op jit(solution)/shard_map/all_to_all | solution.py:294
  (127 shorter events, 25.6 us)
Async XLA Ops:
  0.6 5.6 %collective-permute-start = (bf16[2,256,512]{2,1,0:T(8,128)(2,1)}, bf16[2,256,512]{2,1,0:T(8,128)(2,1)S(1)}, u32[]{:S(2)}, u32[]{:S(2)}) collective-permute-start(bf16[2,256,512]{2,1,0:T(8,128)(2,1)} %bitcast.79), channel_id=1, source_target_pairs={{0,16},{1,17},{2,18},{3,19},{4,20},{5,21},{6,22},{7,23},{8,24},{9,... | collective-permute-start | bytes 1572872 | tf_op jit(solution)/shard_map/ppermute | solution.py:44
  0.7 15.5 %all-to-all-start = ((bf16[4,256,256]{1,2,0:T(8,128)(2,1)}), bf16[4,256,256]{1,2,0:T(8,128)(2,1)S(1)}, u32[]{:S(2)}, u32[]{:S(2)}) async-start(bf16[4,256,256]{1,2,0:T(8,128)(2,1)} %bitcast.75), calls=%async_computation | async-start | bytes 1048576 | tf_op jit(solution)/shard_map/all_to_all | solution.py:223
  6.4 15.8 %collective-permute-start.1 = (bf16[256,1024]{1,0:T(8,128)(2,1)S(1)}, bf16[256,1024]{1,0:T(8,128)(2,1)S(1)}, u32[]{:S(2)}, u32[]{:S(2)}) collective-permute-start(bf16[256,1024]{1,0:T(8,128)(2,1)S(1)} %maximum_select_fusion), channel_id=1, source_target_pairs={{0,32},{1,33},{2,34},{3,35},{4,36},{5,37},{6,38},{7,39},{8,40},{9,... | collective-permute-start | bytes 1572872 | tf_op jit(solution)/shard_map/ppermute | solution.py:44
  8.4 14.6 %collective-permute-start.2 = (bf16[256,1024]{1,0:T(8,128)(2,1)S(1)}, bf16[256,1024]{1,0:T(8,128)(2,1)S(1)}, u32[]{:S(2)}, u32[]{:S(2)}) collective-permute-start(bf16[256,1024]{1,0:T(8,128)(2,1)S(1)} %maximum_select_fusion), channel_id=1, source_target_pairs={{0,96},{1,97},{2,98},{3,99},{4,100},{5,101},{6,102},{7,103},{8,104... | collective-permute-start | bytes 1572872 | tf_op jit(solution)/shard_map/ppermute | solution.py:44
  10.6 14.3 %collective-permute-start.3 = (bf16[256,1024]{1,0:T(8,128)(2,1)S(1)}, bf16[256,1024]{1,0:T(8,128)(2,1)}, u32[]{:S(2)}, u32[]{:S(2)}) collective-permute-start(bf16[256,1024]{1,0:T(8,128)(2,1)S(1)} %maximum_select_fusion), channel_id=1, source_target_pairs={{0,64},{1,65},{2,66},{3,67},{4,68},{5,69},{6,70},{7,71},{8,72},{9,... | collective-permute-start | bytes 1572872 | tf_op jit(solution)/shard_map/ppermute | solution.py:44
  17.8 29.9 %all-to-all-start.1 = ((bf16[4,1024,256]{2,1,0:T(8,128)(2,1)}), bf16[4,1024,256]{2,1,0:T(8,128)(2,1)}, u32[]{:S(2)}, u32[]{:S(2)}) async-start(bf16[4,1024,256]{2,1,0:T(8,128)(2,1)} %broadcast_in_dim.23), calls=%async_computation.1 | async-start | bytes 4194304 | tf_op jit(solution)/shard_map/all_to_all | solution.py:226
  22.3 0.8 copy-start.3
  24.9 4.5 %copy-start.4 = (bf16[256,1024]{1,0:T(8,128)(2,1)S(1)}, bf16[256,1024]{1,0:T(8,128)(2,1)}, u32[]{:S(2)}) copy-start(bf16[256,1024]{1,0:T(8,128)(2,1)} %copy-done.3) | copy-start | bytes 1572868
  26.1 33.9 %copy-start = (bf16[512,1024]{1,0:T(8,128)(2,1)}, bf16[512,1024]{1,0:T(8,128)(2,1)S(1)}, u32[]{:S(2)}) copy-start(bf16[512,1024]{1,0:T(8,128)(2,1)S(1)} %constant_dynamic-update-slice_fusion.refs_2_.refs_1_) | copy-start | bytes 3145732
  26.1 21.7 %collective-permute-start.5 = (bf16[512,1024]{1,0:T(8,128)(2,1)S(1)}, bf16[512,1024]{1,0:T(8,128)(2,1)}, u32[]{:S(2)}, u32[]{:S(2)}) collective-permute-start(bf16[512,1024]{1,0:T(8,128)(2,1)S(1)} %constant_dynamic-update-slice_fusion.refs_2_.refs_1_), channel_id=1, source_target_pairs={{0,12},{1,13},{2,14},{3,15},{4,0},{5,1},{6,2},{7,3},{8,4},{9,5},{1... | collective-permute-start | bytes 3145736 | tf_op jit(solution)/shard_map/ppermute | solution.py:44
  29.4 18.4 %collective-permute-start.7 = (bf16[512,1024]{1,0:T(8,128)(2,1)S(1)}, bf16[512,1024]{1,0:T(8,128)(2,1)}, u32[]{:S(2)}, u32[]{:S(2)}) collective-permute-start(bf16[512,1024]{1,0:T(8,128)(2,1)S(1)} %constant_dynamic-update-slice_fusion.refs_2_.refs_1_), channel_id=1, source_target_pairs={{0,4},{1,5},{2,6},{3,7},{4,8},{5,9},{6,10},{7,11},{8,12},{9,13},{1... | collective-permute-start | bytes 3145736 | tf_op jit(solution)/shard_map/ppermute | solution.py:44
  29.4 27.3 %collective-permute-start.4 = (bf16[512,1024]{1,0:T(8,128)(2,1)S(1)}, bf16[512,1024]{1,0:T(8,128)(2,1)}, u32[]{:S(2)}, u32[]{:S(2)}) collective-permute-start(bf16[512,1024]{1,0:T(8,128)(2,1)S(1)} %pad_maximum_fusion.refs_1_.refs_0_), channel_id=1, source_target_pairs={{0,4},{1,5},{2,6},{3,7},{4,8},{5,9},{6,10},{7,11},{8,12},{9,13},{1... | collective-permute-start | bytes 3145736 | tf_op jit(solution)/shard_map/ppermute | solution.py:44
  30.3 26.4 %collective-permute-start.6 = (bf16[512,1024]{1,0:T(8,128)(2,1)S(1)}, bf16[512,1024]{1,0:T(8,128)(2,1)}, u32[]{:S(2)}, u32[]{:S(2)}) collective-permute-start(bf16[512,1024]{1,0:T(8,128)(2,1)S(1)} %pad_maximum_fusion.refs_1_.refs_0_), channel_id=1, source_target_pairs={{0,12},{1,13},{2,14},{3,15},{4,0},{5,1},{6,2},{7,3},{8,4},{9,5},{1... | collective-permute-start | bytes 3145736 | tf_op jit(solution)/shard_map/ppermute | solution.py:44
  56.7 10.6 %collective-permute-start.8 = (bf16[16,256,256]{2,1,0:T(8,128)(2,1)}, bf16[16,256,256]{2,1,0:T(8,128)(2,1)}, u32[]{:S(2)}, u32[]{:S(2)}) collective-permute-start(bf16[16,256,256]{2,1,0:T(8,128)(2,1)} %bitcast.10.refs_0_), channel_id=1, source_target_pairs={{0,16},{1,17},{2,18},{3,19},{4,20},{5,21},{6,22},{7,23},{8,24},{9,... | collective-permute-start | bytes 6291464 | tf_op jit(solution)/shard_map/ppermute | solution.py:44
  57.8 15.1 %collective-permute-start.10 = (bf16[512,1024]{1,0:T(8,128)(2,1)}, bf16[512,1024]{1,0:T(8,128)(2,1)}, u32[]{:S(2)}, u32[]{:S(2)}) collective-permute-start(bf16[512,1024]{1,0:T(8,128)(2,1)} %collective-permute-done.5.refs_6_.refs_5_), channel_id=1, source_target_pairs={{0,12},{1,13},{2,14},{3,15},{4,0},{5,1},{6,2},{7,3},{8,4},{9,5},{1... | collective-permute-start | bytes 3145736 | tf_op jit(solution)/shard_map/ppermute | solution.py:44
  59.0 16.3 %collective-permute-start.9 = (bf16[512,1024]{1,0:T(8,128)(2,1)}, bf16[512,1024]{1,0:T(8,128)(2,1)}, u32[]{:S(2)}, u32[]{:S(2)}) collective-permute-start(bf16[512,1024]{1,0:T(8,128)(2,1)} %collective-permute-done.4.refs_5_.refs_4_), channel_id=1, source_target_pairs={{0,4},{1,5},{2,6},{3,7},{4,8},{5,9},{6,10},{7,11},{8,12},{9,13},{1... | collective-permute-start | bytes 3145736 | tf_op jit(solution)/shard_map/ppermute | solution.py:44
  59.9 42.7 %collective-permute-start.12 = (bf16[512,1024]{1,0:T(8,128)(2,1)}, bf16[512,1024]{1,0:T(8,128)(2,1)}, u32[]{:S(2)}, u32[]{:S(2)}) collective-permute-start(bf16[512,1024]{1,0:T(8,128)(2,1)} %collective-permute-done.6.refs_3_.refs_2_), channel_id=1, source_target_pairs={{0,16},{1,17},{2,18},{3,19},{4,20},{5,21},{6,22},{7,23},{8,24},{9,... | collective-permute-start | bytes 3145736 | tf_op jit(solution)/shard_map/ppermute | solution.py:44
  60.0 42.7 %collective-permute-start.13 = (bf16[512,1024]{1,0:T(8,128)(2,1)}, bf16[512,1024]{1,0:T(8,128)(2,1)}, u32[]{:S(2)}, u32[]{:S(2)}) collective-permute-start(bf16[512,1024]{1,0:T(8,128)(2,1)} %collective-permute-done.7.refs_4_.refs_3_), channel_id=1, source_target_pairs={{0,16},{1,17},{2,18},{3,19},{4,20},{5,21},{6,22},{7,23},{8,24},{9,... | collective-permute-start | bytes 3145736 | tf_op jit(solution)/shard_map/ppermute | solution.py:44
  60.5 1.2 copy-start.1
  67.3 35.3 %collective-permute-start.14 = (bf16[512,1024]{1,0:T(8,128)(2,1)}, bf16[512,1024]{1,0:T(8,128)(2,1)}, u32[]{:S(2)}, u32[]{:S(2)}) collective-permute-start(bf16[512,1024]{1,0:T(8,128)(2,1)} %collective-permute-done.4.refs_5_.refs_4_), channel_id=1, source_target_pairs={{0,16},{1,17},{2,18},{3,19},{4,20},{5,21},{6,22},{7,23},{8,24},{9,... | collective-permute-start | bytes 3145736 | tf_op jit(solution)/shard_map/ppermute | solution.py:44
  72.9 29.7 %collective-permute-start.15 = (bf16[512,1024]{1,0:T(8,128)(2,1)}, bf16[512,1024]{1,0:T(8,128)(2,1)}, u32[]{:S(2)}, u32[]{:S(2)}) collective-permute-start(bf16[512,1024]{1,0:T(8,128)(2,1)} %collective-permute-done.5.refs_6_.refs_5_), channel_id=1, source_target_pairs={{0,16},{1,17},{2,18},{3,19},{4,20},{5,21},{6,22},{7,23},{8,24},{9,... | collective-permute-start | bytes 3145736 | tf_op jit(solution)/shard_map/ppermute | solution.py:44
  81.8 9.6 %all-to-all-start.2 = ((f32[8,1,512]{2,1,0:T(1,128)}), f32[8,1,512]{2,1,0:T(1,128)S(1)}, u32[]{:S(2)}, u32[]{:S(2)}) async-start(f32[8,1,512]{2,1,0:T(1,128)} %broadcast_in_dim.24), calls=%async_computation.2 | async-start | bytes 32768 | tf_op jit(solution)/shard_map/all_to_all | solution.py:49
  87.6 15.1 %collective-permute-start.11 = (f32[1024,256]{1,0:T(8,128)}, f32[1024,256]{1,0:T(8,128)}, u32[]{:S(2)}, u32[]{:S(2)}) collective-permute-start(f32[1024,256]{1,0:T(8,128)} %get-tuple-element.66), channel_id=1, source_target_pairs={{0,16},{1,17},{2,18},{3,19},{4,20},{5,21},{6,22},{7,23},{8,24},{9,... | collective-permute-start | bytes 3145736 | tf_op jit(solution)/shard_map/ppermute | solution.py:44
  104.0 8.5 %all-to-all-start.4 = ((f32[8,1,512]{2,1,0:T(1,128)}), f32[8,1,512]{2,1,0:T(1,128)S(1)}, u32[]{:S(2)}, u32[]{:S(2)}) async-start(f32[8,1,512]{2,1,0:T(1,128)} %broadcast_in_dim.26), calls=%async_computation.4 | async-start | bytes 32768 | tf_op jit(solution)/shard_map/all_to_all | solution.py:49
  107.3 17.1 %collective-permute-start.19 = (bf16[512,1024]{1,0:T(8,128)(2,1)}, bf16[512,1024]{1,0:T(8,128)(2,1)}, u32[]{:S(2)}, u32[]{:S(2)}) collective-permute-start(bf16[512,1024]{1,0:T(8,128)(2,1)} %copy-done), channel_id=1, source_target_pairs={{0,16},{1,17},{2,18},{3,19},{4,20},{5,21},{6,22},{7,23},{8,24},{9,... | collective-permute-start | bytes 3145736 | tf_op jit(solution)/shard_map/ppermute | solution.py:44
  107.7 16.7 %collective-permute-start.18 = (bf16[512,1024]{1,0:T(8,128)(2,1)S(1)}, bf16[512,1024]{1,0:T(8,128)(2,1)}, u32[]{:S(2)}, u32[]{:S(2)}) collective-permute-start(bf16[512,1024]{1,0:T(8,128)(2,1)S(1)} %pad_maximum_fusion.refs_1_.refs_0_), channel_id=1, source_target_pairs={{0,16},{1,17},{2,18},{3,19},{4,20},{5,21},{6,22},{7,23},{8,24},{9,... | collective-permute-start | bytes 3145736 | tf_op jit(solution)/shard_map/ppermute | solution.py:44
  107.9 16.5 %collective-permute-start.16 = (bf16[512,1024]{1,0:T(8,128)(2,1)}, bf16[512,1024]{1,0:T(8,128)(2,1)}, u32[]{:S(2)}, u32[]{:S(2)}) collective-permute-start(bf16[512,1024]{1,0:T(8,128)(2,1)} %collective-permute-done.9.refs_2_.refs_6_), channel_id=1, source_target_pairs={{0,16},{1,17},{2,18},{3,19},{4,20},{5,21},{6,22},{7,23},{8,24},{9,... | collective-permute-start | bytes 3145736 | tf_op jit(solution)/shard_map/ppermute | solution.py:44
  108.2 16.2 %collective-permute-start.17 = (bf16[512,1024]{1,0:T(8,128)(2,1)}, bf16[512,1024]{1,0:T(8,128)(2,1)}, u32[]{:S(2)}, u32[]{:S(2)}) collective-permute-start(bf16[512,1024]{1,0:T(8,128)(2,1)} %collective-permute-done.10.refs_3_.refs_7_), channel_id=1, source_target_pairs={{0,16},{1,17},{2,18},{3,19},{4,20},{5,21},{6,22},{7,23},{8,24},{9,... | collective-permute-start | bytes 3145736 | tf_op jit(solution)/shard_map/ppermute | solution.py:44
  154.5 11.3 %all-to-all-start.9 = ((f32[16,1,1536]{2,1,0:T(1,128)}), f32[16,1,1536]{2,1,0:T(1,128)S(1)}, u32[]{:S(2)}, u32[]{:S(2)}) async-start(f32[16,1,1536]{2,1,0:T(1,128)} %broadcast_in_dim.31), calls=%async_computation.9 | async-start | bytes 196608 | tf_op jit(solution)/shard_map/all_to_all | solution.py:49
  166.6 12.1 %copy-start.2 = (bf16[512,1024]{1,0:T(8,128)(2,1)S(1)}, bf16[512,1024]{1,0:T(8,128)(2,1)}, u32[]{:S(2)}) copy-start(bf16[512,1024]{1,0:T(8,128)(2,1)} %copy-done) | copy-start | bytes 3145732
  167.2 8.6 %all-to-all-start.10 = ((f32[8,1,1536]{2,1,0:T(1,128)}), f32[8,1,1536]{2,1,0:T(1,128)S(1)}, u32[]{:S(2)}, u32[]{:S(2)}) async-start(f32[8,1,1536]{2,1,0:T(1,128)} %broadcast_in_dim.32), calls=%async_computation.10 | async-start | bytes 98304 | tf_op jit(solution)/shard_map/all_to_all | solution.py:49
